TPU v7x, 32 devices: a whole 2x2x4 slice. The times are simulated.
32 devices in a mesh: row: 4 (over y, x), col: 8 (over z, core).
Axes of the slice: x: 2, y: 2, z: 4, core: 2. Of those that a mesh axis runs over, the one named last changes fastest.
Arguments:
- features: bfloat16 [8192, 128], P(('row', 'col')), may hold values from -3 to 3
- weight: bfloat16 [128, 128], replicated, may hold values from -0.5 to 0.5
- cuts: int32 [32, 8], P(('row', 'col')), may hold values from 0 to 255
- pos_rows: int32 [4, 8, 384], P('row', 'col'), may hold values from 0 to 15
- pos_cols: int32 [4, 8, 384], P('row', 'col'), may hold values from 0 to 7
- pos_keys: int32 [4, 8, 384], P('row', 'col'), may hold values from 0 to 1073741823
- pos_count: int32 [4, 8], P('row', 'col'), may hold values from 96 to 384, as said below
- neg_rows: int32 [4, 8, 128], P('row', 'col'), may hold values from 0 to 15
- neg_cols: int32 [4, 8, 128], P('row', 'col'), may hold values from 0 to 7
Outputs:
- grad_features: bfloat16 [8192, 128], P(('row', 'col'))
- grad_weight: float32 [128, 128], replicated
Inputs may be any that keep to these rules, and one draw needn't show every extreme that they name: `pos_count`: one tile in every draw has all 384 slots live.
All inputs are finite; a program needn't handle non-finite values.
Results may differ from a plain program's by a relative error of at most 0.0053.
Values may be sent and summed in bfloat16 or wider, within the bound.
No kernel may reach another device: no remote copies, remote signals or barrier semaphores. Data moves between devices by JAX's collectives and lax.ppermute only.
A program may use at most 64 MiB of HBM per device.

v0:
```python
import jax
import jax.numpy as jnp
from jax import lax
from jax.sharding import PartitionSpec as P

BLOCK = 128
GROUP = 32


def padded_2(cells, sides, width):
    for axis, dim in sides:
        count = lax.axis_size(axis)
        ends = count - 1
        head = lax.slice_in_dim(cells, 0, width, axis=dim)
        tail = lax.slice_in_dim(cells, cells.shape[dim] - width, cells.shape[dim], axis=dim)
        cells = jnp.concatenate(
            [
                lax.ppermute(tail, axis, [(i, (i + 1) % count) for i in range(ends)]),
                cells,
                lax.ppermute(head, axis, [((i + 1) % count, i) for i in range(ends)]),
            ],
            axis=dim,
        )
    return cells


def edge_targets(keys, size):
    first = lax.broadcasted_iota(jnp.int32, (size, size), 0)
    second = lax.broadcasted_iota(jnp.int32, (size, size), 1)
    hashed = (keys[:, None, None] + 40503 * (size * first + second)[None]) % 1073741824
    mixed = jnp.right_shift(jnp.bitwise_xor(hashed, jnp.right_shift(hashed, 11)), 7)
    return (mixed % 5 == 0).astype(jnp.float32)


def operator_local(values, link_f, padded):
    own = values.astype(jnp.float32)
    before = padded[0, :-2].astype(jnp.float32)
    after = padded[1, 2:].astype(jnp.float32)
    return 0.5 * own + 0.25 * (link_f.astype(jnp.float32) * before + after)


def reduce_rows(partial_value):
    width = partial_value.shape[-1]
    return lax.psum_scatter(
        partial_value.reshape(-1, width), "col", scatter_dimension=0, tiled=True
    )


def reduce_cols(partial_value):
    return lax.psum_scatter(
        partial_value.reshape(-1, partial_value.shape[-1]), "row", scatter_dimension=0, tiled=True
    )


def decode_pairs(carry, row_z, col_z, rows, cols, keys, count, positive):
    trips = (count + GROUP - 1) // GROUP

    def step(turn, state):
        acc_rows, acc_cols = state
        start = turn * GROUP
        group_rows = lax.dynamic_slice_in_dim(rows, start, GROUP)
        group_cols = lax.dynamic_slice_in_dim(cols, start, GROUP)
        near = jnp.take(row_z, group_rows, axis=0)
        far = jnp.take(col_z, group_cols, axis=0)
        logits = jnp.einsum("gal,gbl->gab", near, far, preferred_element_type=jnp.float32)
        if positive:
            targets = edge_targets(lax.dynamic_slice_in_dim(keys, start, GROUP), BLOCK)
        else:
            targets = jnp.zeros_like(logits)
        slots = start + lax.broadcasted_iota(jnp.int32, (GROUP,), 0)
        live = (slots < count).astype(jnp.float32)
        pair_grad = ((jax.nn.sigmoid(logits) - targets) * (live[:, None, None] / 32.0)).astype(
            jnp.bfloat16
        )
        acc_rows = acc_rows.at[group_rows].add(
            jnp.einsum("gab,gbl->gal", pair_grad, far, preferred_element_type=jnp.float32)
        )
        acc_cols = acc_cols.at[group_cols].add(
            jnp.einsum("gab,gal->gbl", pair_grad, near, preferred_element_type=jnp.float32)
        )
        return (acc_rows, acc_cols)

    return lax.fori_loop(0, trips, step, carry)


def local(features, weight, cuts, pos_rows, pos_cols, pos_keys, pos_count, neg_rows, neg_cols):
    nodes_here = features.shape[0]
    width = weight.shape[1]
    offsets = lax.broadcasted_iota(jnp.int32, (cuts.shape[1], nodes_here), 1)
    hit = jnp.any(cuts[0][:, None] == offsets, axis=0)
    link_f = (1 - hit.astype(jnp.int32)).astype(jnp.bfloat16)[:, None]
    stacked = jnp.stack([features, features * link_f])
    padded = padded_2(stacked, ((("row", "col"), 1),), 1)
    agg = operator_local(features, link_f, padded).astype(jnp.bfloat16)
    latent = jnp.dot(agg, weight, preferred_element_type=jnp.float32).astype(jnp.bfloat16)
    row_z = lax.all_gather(latent, "col", axis=0, tiled=True).reshape(-1, BLOCK, width)
    col_z = lax.all_gather(latent, "row", axis=0, tiled=True).reshape(-1, BLOCK, width)
    local_rows = pos_rows[0, 0]
    local_cols = pos_cols[0, 0]
    local_keys = pos_keys[0, 0]
    live_count = pos_count[0, 0]
    negative_rows = neg_rows[0, 0]
    negative_cols = neg_cols[0, 0]
    negative_count = negative_rows.shape[0]
    empty = (jnp.zeros(row_z.shape, jnp.float32), jnp.zeros(col_z.shape, jnp.float32))
    carry = decode_pairs(empty, row_z, col_z, local_rows, local_cols, local_keys, live_count, True)
    carry = decode_pairs(
        carry, row_z, col_z, negative_rows, negative_cols, negative_rows, negative_count, False
    )
    mine_rows = reduce_rows(carry[0])
    mine_cols = reduce_cols(carry[1])
    dlatent = (mine_rows + mine_cols).astype(jnp.bfloat16)
    total_nodes = nodes_here * lax.axis_size("row") * lax.axis_size("col")
    share = lax.dot_general(
        agg, dlatent, (((0,), (0,)), ((), ())), preferred_element_type=jnp.float32
    )
    grad_weight = lax.psum(share, ("row", "col")) * total_nodes ** (-0.5)
    dagg = lax.dot_general(
        dlatent, weight, (((1,), (1,)), ((), ())), preferred_element_type=jnp.float32
    ).astype(jnp.bfloat16)
    stacked_grad = jnp.stack([dagg, dagg * link_f])
    padded_grad = padded_2(stacked_grad, ((("row", "col"), 1),), 1)
    grad_features = operator_local(dagg, link_f, padded_grad).astype(jnp.bfloat16)
    return (grad_features, grad_weight)


def solution(mesh):
    placed = (
        P(("row", "col"), None),
        P(),
        P(("row", "col"), None),
        P("row", "col", None),
        P("row", "col", None),
        P("row", "col", None),
        P("row", "col"),
        P("row", "col", None),
        P("row", "col", None),
    )
    return jax.shard_map(
        local, mesh=mesh, in_specs=placed, out_specs=(P(("row", "col"), None), P()), check_vma=False
    )
```

profile of v0, /device:TPU:0, one launch (start us, length us, event | category | flops | bytes accessed | tf_op | source)
XLA Modules:
  0.0 582.4 jit_solution(6960707165303085103)
XLA Ops:
  18.4 19.1 %all_gather.6 = bf16[2048,128]{1,0:T(8,128)(2,1)S(1)} all-gather(bf16[256,128]{1,0:T(8,128)(2,1)S(1)} %convolution_convert_fusion.1), channel_id=1, replica_groups=mesh['row'=4,'col'=8] {'col'}, dimensions={0}, use_global_device_ids=true | all-gather | bytes 589824 | tf_op jit(solution)/shard_map/all_gather | solution.py:96
  37.5 10.4 %all_gather.7 = bf16[1024,128]{1,0:T(8,128)(2,1)S(1)} all-gather(bf16[256,128]{1,0:T(8,128)(2,1)S(1)} %convolution_convert_fusion.1), channel_id=1, replica_groups=mesh['row'=4,'col'=8] {'row'}, dimensions={0}, use_global_device_ids=true | all-gather | bytes 327680 | tf_op jit(solution)/shard_map/all_gather | solution.py:97
  48.1 221.8 %while.30 = (s32[]{:T(128)}, f32[16,128,128]{2,1,0:T(8,128)S(1)}, f32[8,128,128]{2,1,0:T(8,128)S(1)}, s32[]{:T(128)}, s32[384]{0:T(512)S(1)}, /*index=5*/bf16[16...) while((s32[]{:T(128)}, f32[16,128,128]{2,1,0:T(8,128)S(1)}, ...), condition=%wide.region_4.5_spmd, body=%wide.region_1.4_spmd.sunk | while | flops 421038688 | bytes 36842808 | solution.py:83
  57.8 4.7 scatter_fusion.1
  65.6 4.7 scatter_fusion
  87.7 4.7 scatter_fusion
  109.9 4.7 scatter_fusion
  124.3 4.7 scatter_fusion.1
  132.1 4.7 scatter_fusion
  154.3 4.7 scatter_fusion
  176.4 4.7 scatter_fusion
  198.6 4.7 scatter_fusion
  220.8 4.7 scatter_fusion
  243.0 4.7 scatter_fusion
  265.1 4.7 scatter_fusion
  269.8 76.9 %while.31 = (s32[]{:T(128)}, f32[16,128,128]{2,1,0:T(8,128)S(1)}, f32[8,128,128]{2,1,0:T(8,128)S(1)}, s32[128]{0:T(128)S(1)}, bf16[16,128,128]{2,1,0:T(8,128)(2,...) while((s32[]{:T(128)}, f32[16,128,128]{2,1,0:T(8,128)S(1)}, ...), condition=%wide.region_8.9_spmd, body=%wide.region_5.8_spmd.sunk | while | flops 408422880 | bytes 36710296 | solution.py:83
  276.6 4.7 scatter_fusion.3
  284.4 4.7 scatter_fusion.2
  303.6 4.7 scatter_fusion.2
  322.8 4.7 scatter_fusion.2
  342.0 4.7 scatter_fusion.2
  348.3 65.0 %reduce-scatter.5.cloned.1.call-done = f32[256,128]{1,0:T(8,128)} async-done(((f32[1024,128]{1,0:T(8,128)}), f32[256,128]{1,0:T(8,128)}) %reduce-scatter.5.cloned.1.call-update) | async-done | bytes 131088 | tf_op jit(solution)/shard_map/reduce_scatter | solution.py:50
  413.4 34.8 %reduce-scatter.3.cloned.1.call-done = f32[256,128]{1,0:T(8,128)} async-done(((f32[2048,128]{1,0:T(8,128)}), f32[256,128]{1,0:T(8,128)}) %reduce-scatter.3.cloned.1.call-update) | async-done | bytes 131088 | tf_op jit(solution)/shard_map/reduce_scatter | solution.py:44
  454.6 119.8 %all-reduce.2.cloned.1.call-done = f32[128,128]{1,0:T(8,128)} async-done(((f32[128,128]{1,0:T(8,128)}), f32[128,128]{1,0:T(8,128)}) %all-reduce.2.cloned.1.call-update) | async-done | bytes 65552 | tf_op jit(solution)/shard_map/psum | solution.py:117
  (265 shorter events, 237.9 us)
Async XLA Ops:
  7.2 11.1 %copy-start = (bf16[128,128]{1,0:T(8,128)(2,1)S(1)}, bf16[128,128]{1,0:T(8,128)(2,1)}, u32[]{:S(2)}) copy-start(bf16[128,128]{1,0:T(8,128)(2,1)} %param.14) | copy-start | bytes 98308
  7.2 406.2 %reduce-scatter.5.cloned.1.call-start = ((), (), s32[]{:S(2)}) async-start(), calls=%async_computation.3 | async-start | bytes 655360 | tf_op jit(solution)/shard_map/reduce_scatter | solution.py:50
  9.6 6.4 %collective-permute-start = (bf16[2,1,128]{2,1,0:T(2,128)(2,1)S(1)}, bf16[2,1,128]{2,1,0:T(2,128)(2,1)S(1)}, u32[]{:S(2)}, u32[]{:S(2)}) collective-permute-start(bf16[2,1,128]{2,1,0:T(2,128)(2,1)S(1)} %get-tuple-element.341), channel_id=1, source_target_pairs={{0,1},{1,2},{2,3},{3,4},{4,5},{5,6},{6,7},{7,8},{8,9},{9,10},{10,1... | collective-permute-start | bytes 1544 | tf_op jit(solution)/shard_map/ppermute | solution.py:18
  12.0 5.2 collective-permute-start.1
  48.0 221.8 %copy-start.7 = (s32[1,1,128]{2,1,0:T(1,128)S(1)}, s32[1,1,128]{2,1,0:T(1,128)}, u32[]{:S(2)}) copy-start(s32[1,1,128]{2,1,0:T(1,128)} %param.20) | copy-start | bytes 1540
  48.0 221.8 %copy-start.8 = (s32[1,1,128]{2,1,0:T(1,128)S(1)}, s32[1,1,128]{2,1,0:T(1,128)}, u32[]{:S(2)}) copy-start(s32[1,1,128]{2,1,0:T(1,128)} %param.21) | copy-start | bytes 1540
  51.4 4.4 copy-start.3
  73.6 4.4 copy-start.3
  95.8 4.4 copy-start.3
  118.0 4.4 copy-start.3
  140.1 4.4 copy-start.3
  162.3 4.4 copy-start.3
  184.5 4.4 copy-start.3
  206.7 4.4 copy-start.3
  228.8 4.4 copy-start.3
  251.0 4.4 copy-start.3
  272.4 2.3 copy-start.5
  291.6 2.3 copy-start.5
  310.8 2.3 copy-start.5
  330.0 2.3 copy-start.5
  347.6 100.7 %reduce-scatter.3.cloned.1.call-start = ((), (), s32[]{:S(2)}) async-start(), calls=%async_computation.2 | async-start | bytes 1179648 | tf_op jit(solution)/shard_map/reduce_scatter | solution.py:44
  348.3 226.1 %all-reduce.2.cloned.1.call-start = ((), (), s32[]{:S(2)}) async-start(), calls=%async_computation.4 | async-start | bytes 131072 | tf_op jit(solution)/shard_map/psum | solution.py:117
  449.5 3.5 collective-permute-start.2
  450.8 3.0 collective-permute-start.3
  (16 other events, 29.1 us)
Sparse Core Ops, SparseCore 0:
  347.7 65.6 reduce-scatter.4
  415.8 32.4 reduce-scatter.2
  455.3 119.0 all-reduce.1
where the time goes:
time: 587 us; the launch traced here: 582 us
  waiting for transfers between devices  222 us (38%)
  other arithmetic  148 us (25%)
  matrix products  124 us (21%)
  local copies, waits for them, and re-layouts  36 us (6%)
  blocking collectives  29.5 us (5%)
  between operations  14.6 us (2%)
  starting transfers between devices  6.34 us (1%)
    psum x1, waiting for transfers between devices, local(): grad_weight = lax.psum(share, ('row', 'col')) * total_nodes ** (-0.5)  120 us
    scatter-add x14, other arithmetic, step(): acc_rows.at[group_rows]  65.3 us
    scatter-add x14, other arithmetic, step(): acc_cols.at[group_cols]  65.2 us
    reduce_scatter x1, waiting for transfers between devices, reduce_cols(): lax.psum_scatter(partial_value.reshape(-1, partial_value.shape[-1]), 'row...  65 us
    dot_general x14, matrix products, step(): jnp.einsum('gal,gbl->gab', near, far, preferred_element_type=jnp.float32)  53.1 us
    dot_general x14, matrix products, step(): jnp.einsum('gab,gbl->gal', pair_grad, far, preferred_element_type=jnp.flo...  43.2 us
    reduce_scatter x1, waiting for transfers between devices, reduce_rows(): lax.psum_scatter(partial_value.reshape(-1, width), 'col', scatter_dimensi...  34.8 us
    dot_general x14, matrix products, step(): jnp.einsum('gab,gal->gbl', pair_grad, near, preferred_element_type=jnp.fl...  26.9 us
  transfers between devices with their start and end apart: 7, of which 5 were waited for; matrix products, arithmetic and copies ran while one was open for 1% of the time, Pallas kernels for 0%

commit v1 on v0

v1 whole, which is shorter than its diff:
```python
import functools

import jax
import jax.numpy as jnp
from jax import lax
from jax.experimental import pallas as pl
from jax.experimental.pallas import tpu as pltpu
from jax.sharding import PartitionSpec as P

BLOCK = 128
AXES = ("row", "col")
INV5 = -858993459
ANY = pl.BlockSpec(memory_space=pl.ANY)
VMEM = pl.BlockSpec(memory_space=pltpu.VMEM)
SMEM = pl.BlockSpec(memory_space=pltpu.SMEM)
CHUNK_CELLS = 128


def params(mib):
    return pltpu.CompilerParams(vmem_limit_bytes=mib * 2**20)


def swap(x, axis, step):
    count = lax.axis_size(axis)
    return lax.ppermute(x, axis, [(i, i ^ step) for i in range(count)])


def swap_next(x):
    count = lax.axis_size("row") * lax.axis_size("col")
    pairs = []
    for s in range(1, count - 1, 2):
        pairs += [(s, s + 1), (s + 1, s)]
    return lax.ppermute(x, AXES, pairs)


def links(cuts_ref, rows, width):
    node = lax.broadcasted_iota(jnp.int32, (rows, width), 0)
    cut = node == cuts_ref[0, 0]
    for t in range(1, cuts_ref.shape[1]):
        cut = jnp.logical_or(cut, node == cuts_ref[0, t])
    return jnp.where(cut, 0.0, 1.0).astype(jnp.float32)


def edges(values, link, out_ref):
    rows, width = values.shape
    head = link[0:8] * values[0:8]
    tail = values[rows - 8 : rows]
    out_ref[...] = jnp.concatenate([head, tail], axis=0).astype(out_ref.dtype)


def stencil(values, link, near_ref, far_ref):
    rows, width = values.shape
    odd = lax.rem(lax.axis_index("col"), 2) == 1
    near = near_ref[...].astype(jnp.float32)
    far = far_ref[...].astype(jnp.float32)
    prev = jnp.where(odd, near[15:16], far[15:16])
    nxt = jnp.where(odd, far[0:1], near[0:1])
    node = lax.broadcasted_iota(jnp.int32, (rows, width), 0)
    before = jnp.where(node == 0, prev, pltpu.roll(values, 1, 0))
    after = jnp.where(node == rows - 1, nxt, pltpu.roll(link * values, rows - 1, 0))
    return 0.5 * values + 0.25 * (link * before + after)


def edge_kernel(cuts_ref, features_ref, out_ref):
    values = features_ref[...].astype(jnp.float32)
    edges(values, links(cuts_ref, *values.shape), out_ref)


def agg_kernel(cuts_ref, features_ref, near_ref, far_ref, out_ref):
    values = features_ref[...].astype(jnp.float32)
    link = links(cuts_ref, *values.shape)
    out_ref[...] = stencil(values, link, near_ref, far_ref).astype(out_ref.dtype)


def target_kernel(
    base, blocks, cols, per, filtered,
    rows_hbm, cols_hbm, keys_hbm, count_hbm, nrows_hbm, ncols_hbm,
    t_hbm, n_hbm,
    rows_s, cols_s, keys_s, count_s, nrows_s, ncols_s, npos_s, n_s,
    acc, step_ref, out, sems, osems,
):
    pairs = [
        (rows_hbm, rows_s), (cols_hbm, cols_s), (keys_hbm, keys_s),
        (count_hbm, count_s), (nrows_hbm, nrows_s), (ncols_hbm, ncols_s),
    ]
    copies = [pltpu.make_async_copy(a, b, sems.at[t]) for t, (a, b) in enumerate(pairs)]
    for copy in copies:
        copy.start()
    a = lax.broadcasted_iota(jnp.int32, (BLOCK, BLOCK), 0)
    b = lax.broadcasted_iota(jnp.int32, (BLOCK, BLOCK), 1)
    step_ref[...] = (a * BLOCK + b) * jnp.int32(4 * 40503)

    def clear(i, _):
        at = pl.multiple_of(i * BLOCK, BLOCK)
        acc[pl.ds(at, BLOCK), :] = jnp.zeros((BLOCK, cols * BLOCK), jnp.float32)
        return 0

    lax.fori_loop(0, blocks, clear, 0)
    for t in range(blocks * cols):
        npos_s[t] = 0
        n_s[0, t] = 0
    for copy in copies:
        copy.wait()
    here_rows = per * lax.axis_index("col")
    here_cols = per * lax.axis_index("row")
    count = count_s[0, 0]
    slots = rows_s.shape[2]
    unroll = 4 if slots % 4 == 0 else 1

    def place(i, j):
        return jnp.bitwise_xor(i, here_rows) - base, jnp.bitwise_xor(j, here_cols)

    def positive(s):
        i, j = place(rows_s[0, 0, s], cols_s[0, 0, s])
        key = keys_s[0, 0, s] * 4
        live = s < count

        def add():
            row = pl.multiple_of(i * BLOCK, BLOCK)
            col = pl.multiple_of(j * BLOCK, BLOCK)
            mixed = step_ref[...] + key
            mixed = jnp.bitwise_xor(
                lax.shift_right_logical(mixed, 9), lax.shift_right_logical(mixed, 20)
            )
            fifth = mixed * jnp.int32(INV5) + jnp.int32(-(2**31))
            hit = fifth < jnp.int32(-(2**31) + 2**21)
            one = jnp.where(live, 1.0, 0.0).astype(jnp.float32)
            acc[pl.ds(row, BLOCK), pl.ds(col, BLOCK)] += jnp.where(hit, one, 0.0)
            npos_s[i * cols + j] += jnp.where(live, 1, 0)

        if filtered:
            pl.when(jnp.logical_and(i >= 0, i < blocks))(add)
        else:
            add()

    def positives(g, _):
        for u in range(unroll):
            positive(g * unroll + u)
        return 0

    lax.fori_loop(0, (count + unroll - 1) // unroll, positives, 0)

    def negative(s, _):
        i, j = place(nrows_s[0, 0, s], ncols_s[0, 0, s])

        def add():
            n_s[0, i * cols + j] += 1

        if filtered:
            pl.when(jnp.logical_and(i >= 0, i < blocks))(add)
        else:
            add()
        return 0

    lax.fori_loop(0, nrows_s.shape[2], negative, 0)

    def finish(i, _):
        at = pl.multiple_of(i * BLOCK, BLOCK)
        for j in range(cols):
            half = lax.shift_right_logical(npos_s[i * cols + j], 1).astype(jnp.float32)
            tile = acc[pl.ds(at, BLOCK), pl.ds(j * BLOCK, BLOCK)]
            out[pl.ds(at, BLOCK), pl.ds(j * BLOCK, BLOCK)] = (half - tile).astype(out.dtype)
        pltpu.make_async_copy(
            out.at[pl.ds(at, BLOCK), :], t_hbm.at[pl.ds(at, BLOCK), :], osems.at[i]
        ).start()
        return 0

    lax.fori_loop(0, blocks, finish, 0)

    def total(t, _):
        n_s[0, blocks * cols + t] = n_s[0, t] + lax.bitwise_and(npos_s[t], 1)
        n_s[0, t] += npos_s[t]
        return 0

    lax.fori_loop(0, blocks * cols, total, 0)
    ncopy = pltpu.make_async_copy(n_s, n_hbm, sems.at[0])
    ncopy.start()

    def drain(i, _):
        at = pl.multiple_of(i * BLOCK, BLOCK)
        pltpu.make_async_copy(
            out.at[pl.ds(at, BLOCK), :], t_hbm.at[pl.ds(at, BLOCK), :], osems.at[i]
        ).wait()
        return 0

    lax.fori_loop(0, blocks, drain, 0)
    ncopy.wait()


def targets(base, blocks, cols, per, filtered, slots):
    smem = [pltpu.SMEM(x.shape, x.dtype) for x in slots]
    cells = blocks * cols
    return pl.pallas_call(
        functools.partial(target_kernel, base, blocks, cols, per, filtered),
        out_shape=(
            jax.ShapeDtypeStruct((blocks * BLOCK, cols * BLOCK), jnp.bfloat16),
            jax.ShapeDtypeStruct((1, 2 * cells), jnp.int32),
        ),
        in_specs=[ANY] * 6,
        out_specs=(ANY, ANY),
        scratch_shapes=smem
        + [
            pltpu.SMEM((cells,), jnp.int32),
            pltpu.SMEM((1, 2 * cells), jnp.int32),
            pltpu.VMEM((blocks * BLOCK, cols * BLOCK), jnp.float32),
            pltpu.VMEM((BLOCK, BLOCK), jnp.int32),
            pltpu.VMEM((blocks * BLOCK, cols * BLOCK), jnp.bfloat16),
            pltpu.SemaphoreType.DMA((6,)),
            pltpu.SemaphoreType.DMA((blocks,)),
        ],
        compiler_params=params(40),
        cost_estimate=pl.CostEstimate(
            flops=slots[0].shape[2] * BLOCK * BLOCK * 10,
            bytes_accessed=cells * BLOCK * BLOCK * 8,
            transcendentals=0,
        ),
    )(*slots)


def decode_kernel(row_parts, col_parts, refs):
    refs = list(refs)
    t_hbm, n_hbm, weight_ref = refs[:3]
    row_refs = refs[3 : 3 + len(row_parts)]
    col_refs = refs[3 + len(row_parts) : 3 + len(row_parts) + len(col_parts)]
    rest = refs[3 + len(row_parts) + len(col_parts) :]
    drow_refs = rest[: len(row_parts)]
    dcol_refs = rest[len(row_parts) : len(row_parts) + len(col_parts)]
    share_ref, t_ref, n_s, row_z, col_z, col_acc, tsems, nsem = rest[
        len(row_parts) + len(col_parts) :
    ]
    shard = col_refs[0].shape[0]
    nrow = row_z.shape[0] // shard
    ncol = col_z.shape[0] // shard
    per = shard // BLOCK
    cols = ncol * per
    cells = nrow * per * cols

    def t_copy(p):
        at = pl.ds(p * shard, shard)
        return pltpu.make_async_copy(t_hbm.at[at, :], t_ref.at[at, :], tsems.at[p])

    ncopy = pltpu.make_async_copy(n_hbm, n_s, nsem)
    ncopy.start()
    for p in range(nrow):
        t_copy(p).start()
    weight = weight_ref[...]
    dots = functools.partial(lax.dot_general, preferred_element_type=jnp.float32)
    nn = (((1,), (0,)), ((), ()))
    nt = (((1,), (1,)), ((), ()))
    tn = (((0,), (0,)), ((), ()))
    at = 0
    for ref in col_refs:
        rows = ref.shape[0]
        col_z[at : at + rows, :] = dots(ref[...], weight, nn).astype(jnp.bfloat16)
        at += rows
    at = 0
    for ref in row_refs:
        rows = ref.shape[0]
        row_z[at : at + rows, :] = dots(ref[...], weight, nn).astype(jnp.bfloat16)
        at += rows
    ncopy.wait()
    share = jnp.zeros(share_ref.shape, jnp.float32)
    spots = [(ref, out, t) for ref, out in zip(row_refs, drow_refs) for t in range(ref.shape[0] // shard)]
    for p, (row_ref, drow_ref, t) in enumerate(spots):
        t_copy(p).wait()
        near = row_z[p * shard : (p + 1) * shard, :]
        half = near * jnp.bfloat16(0.5)
        drow = None
        for q in range(ncol):
            far = col_z[q * shard : (q + 1) * shard, :]
            curve = jnp.tanh(dots(half, far, nt))
            bands = []
            for i in range(per):
                line = []
                for j in range(per):
                    cell = (p * per + i) * cols + q * per + j
                    n = 0.5 * n_s[0, cell].astype(jnp.float32)
                    lift = 0.5 * n_s[0, cells + cell].astype(jnp.float32)
                    part = curve[i * BLOCK : (i + 1) * BLOCK, j * BLOCK : (j + 1) * BLOCK]
                    row = p * shard + i * BLOCK
                    col = q * shard + j * BLOCK
                    tile = t_ref[row : row + BLOCK, col : col + BLOCK].astype(jnp.float32)
                    line.append((n * part + (tile + lift)).astype(jnp.bfloat16))
                bands.append(jnp.concatenate(line, axis=1))
            grad = jnp.concatenate(bands, axis=0)
            term = dots(grad, far, nn)
            drow = term if drow is None else drow + term
            back = dots(grad, near, tn)
            if p == 0:
                col_acc[q * shard : (q + 1) * shard, :] = back
            else:
                col_acc[q * shard : (q + 1) * shard, :] += back
        rounded = (drow * (1.0 / 32.0)).astype(jnp.bfloat16)
        drow_ref[t * shard : (t + 1) * shard, :] = rounded
        share += dots(row_ref[t * shard : (t + 1) * shard, :], rounded, tn)
    for q in range(ncol):
        rounded = (col_acc[q * shard : (q + 1) * shard, :] * (1.0 / 32.0)).astype(jnp.bfloat16)
        dcol_refs[q][...] = rounded
        share += dots(col_refs[q][...], rounded, tn)
    share_ref[...] = share.astype(share_ref.dtype)


def decode(t, n, weight, row_parts, col_parts):
    shard = col_parts[0].shape[0]
    nrow = sum(x.shape[0] for x in row_parts) // shard
    ncol = len(col_parts)
    width = weight.shape[1]
    outs = [jax.ShapeDtypeStruct(x.shape, jnp.bfloat16) for x in row_parts + col_parts]
    outs.append(jax.ShapeDtypeStruct((weight.shape[0], width), jnp.bfloat16))
    result = pl.pallas_call(
        lambda *refs: decode_kernel(row_parts, col_parts, refs),
        out_shape=outs,
        in_specs=[ANY, ANY] + [VMEM] * (1 + len(row_parts) + len(col_parts)),
        out_specs=[VMEM] * len(outs),
        scratch_shapes=[
            pltpu.VMEM(t.shape, t.dtype),
            pltpu.SMEM(n.shape, n.dtype),
            pltpu.VMEM((nrow * shard, width), jnp.bfloat16),
            pltpu.VMEM((ncol * shard, width), jnp.bfloat16),
            pltpu.VMEM((ncol * shard, width), jnp.float32),
            pltpu.SemaphoreType.DMA((nrow,)),
            pltpu.SemaphoreType.DMA,
        ],
        compiler_params=params(40),
        cost_estimate=pl.CostEstimate(
            flops=6 * t.shape[0] * t.shape[1] * width,
            bytes_accessed=t.shape[0] * t.shape[1] * 2,
            transcendentals=t.shape[0] * t.shape[1],
        ),
    )(t, n, weight, *row_parts, *col_parts)
    return result[: len(row_parts)], result[len(row_parts) : -1], result[-1]


def latent_kernel(count, cuts_ref, weight_ref, *refs):
    parts = refs[:count]
    dagg_ref, edge_ref = refs[count:]
    total = parts[0][...].astype(jnp.float32)
    for part in parts[1:]:
        total += part[...].astype(jnp.float32)
    dlatent = total.astype(jnp.bfloat16)
    dagg = lax.dot_general(
        dlatent, weight_ref[...], (((1,), (1,)), ((), ())), preferred_element_type=jnp.float32
    ).astype(jnp.bfloat16)
    dagg_ref[...] = dagg
    values = dagg.astype(jnp.float32)
    edges(values, links(cuts_ref, *values.shape), edge_ref)


def f32(x):
    return x.astype(jnp.float32)


def tree_sum(parts):
    parts = [f32(x) for x in parts]
    while len(parts) > 1:
        parts = [a + b for a, b in zip(parts[::2], parts[1::2])]
    return parts[0]


def local(features, weight, cuts, pos_rows, pos_cols, pos_keys, pos_count, neg_rows, neg_cols):
    shard, width = features.shape
    ncol = lax.axis_size("col")
    nrow = lax.axis_size("row")
    half = ncol // 2
    per = shard // BLOCK
    message = jax.ShapeDtypeStruct((16, width), jnp.bfloat16)
    ends = pl.pallas_call(
        edge_kernel, out_shape=message, in_specs=[SMEM, VMEM], out_specs=VMEM
    )(cuts, features)
    near, far = swap(ends, "col", 1), swap_next(ends)
    slots = (pos_rows, pos_cols, pos_keys, pos_count, neg_rows, neg_cols)
    cols = nrow * per
    pieces = max(1, ncol * per * cols // CHUNK_CELLS)
    blocks = ncol * per // pieces
    found = [targets(k * blocks, blocks, cols, per, pieces > 1, slots) for k in range(pieces)]
    agg = pl.pallas_call(
        agg_kernel,
        out_shape=jax.ShapeDtypeStruct(features.shape, jnp.bfloat16),
        in_specs=[SMEM, VMEM, VMEM, VMEM],
        out_specs=VMEM,
    )(cuts, features, near, far)
    mine = [agg] + [swap(agg, "col", 2 * k) for k in range(1, half)]
    col_parts = [agg] + [swap(agg, "row", k) for k in range(1, nrow)]
    stacked = jnp.concatenate(mine, axis=0)
    theirs = swap(stacked, "col", 1)
    ordered = [x for k in range(half) for x in (mine[k], theirs[k * shard : (k + 1) * shard])]
    per_piece = blocks // per
    drow, dcols, shares = [], [], []
    for k, (t, n) in enumerate(found):
        out_rows, out_cols, share = decode(
            t, n, weight, ordered[k * per_piece : (k + 1) * per_piece], col_parts
        )
        drow += out_rows
        dcols.append(out_cols)
        shares.append(share)
    dcol = dcols[0] if pieces == 1 else [tree_sum(x).astype(jnp.bfloat16) for x in zip(*dcols)]
    share = shares[0] if pieces == 1 else tree_sum(shares).astype(jnp.bfloat16)
    send = jnp.concatenate(drow[1::2] + [share], axis=0)
    got = swap(send, "col", 1)
    kept = [
        (f32(drow[2 * k]) + f32(got[k * shard : (k + 1) * shard])).astype(jnp.bfloat16)
        for k in range(half)
    ]
    share = (f32(share) + f32(got[half * shard :])).astype(jnp.bfloat16)
    arrived = [kept[0]] + [swap(kept[k], "col", 2 * k) for k in range(1, half)]
    arrived += [dcol[0]] + [swap(dcol[k], "row", k) for k in range(1, nrow)]
    share = tree_sum([share] + [swap(share, "row", k) for k in range(1, nrow)]).astype(jnp.bfloat16)
    dagg, dends = pl.pallas_call(
        functools.partial(latent_kernel, len(arrived)),
        out_shape=(jax.ShapeDtypeStruct(features.shape, jnp.bfloat16), message),
        in_specs=[SMEM, VMEM] + [VMEM] * len(arrived),
        out_specs=(VMEM, VMEM),
    )(cuts, weight, *arrived)
    near, far = swap(dends, "col", 1), swap_next(dends)
    share = tree_sum([share] + [swap(share, "col", 2 * k) for k in range(1, half)])
    grad_features = pl.pallas_call(
        agg_kernel,
        out_shape=jax.ShapeDtypeStruct(features.shape, jnp.bfloat16),
        in_specs=[SMEM, VMEM, VMEM, VMEM],
        out_specs=VMEM,
    )(cuts, dagg, near, far)
    grad_weight = share * (shard * ncol * nrow) ** (-0.5)
    return (grad_features, grad_weight)


def solution(mesh):
    placed = (
        P(AXES, None),
        P(),
        P(AXES, None),
        P("row", "col", None),
        P("row", "col", None),
        P("row", "col", None),
        P("row", "col"),
        P("row", "col", None),
        P("row", "col", None),
    )
    return jax.shard_map(
        local, mesh=mesh, in_specs=placed, out_specs=(P(AXES, None), P()), check_vma=False
    )
```

time: 587 us -> 89.6 us (0.15)
  the two profiles are of different devices: /device:TPU:0 before, /device:TPU:4 now
where the time goes in v1:
time: 89.6 us; the launch traced here: 88.9 us
  starting transfers between devices  33.5 us (37%)
  Pallas kernels  25.9 us (29%)
  waiting for transfers between devices  18.4 us (21%)
  local copies, waits for them, and re-layouts  7.4 us (8%)
  other arithmetic  2.24 us (3%)
  between operations  1.49 us (2%)
    ppermute x22, starting transfers between devices, swap(): return lax.ppermute(x, axis, [(i, i ^ step) for i in range(count)])  25.8 us
    pallas_call x1, Pallas kernels, targets(): pl.pallas_call(functools.partial(target_kernel, base, blocks, cols, per,...  10.4 us
    ppermute x22, waiting for transfers between devices, swap(): return lax.ppermute(x, axis, [(i, i ^ step) for i in range(count)])  9.62 us
    pallas_call x1, Pallas kernels, decode(): pl.pallas_call(lambda *refs: decode_kernel(row_parts, col_parts, refs), o...  8.88 us
    ppermute x2, waiting for transfers between devices, swap_next(): return lax.ppermute(x, AXES, pairs)  8.78 us
    ppermute x2, starting transfers between devices, swap_next(): return lax.ppermute(x, AXES, pairs)  7.72 us
    unnamed x40, local copies, waits for them, and re-layouts  7.37 us
    pallas_call x2, Pallas kernels, local(): pl.pallas_call(agg_kernel, out_shape=jax.ShapeDtypeStruct(features.shape,...  3.24 us
  transfers between devices with their start and end apart: 24, of which 9 were waited for; matrix products, arithmetic and copies ran while one was open for 2% of the time, Pallas kernels for 14%

profile of v1, /device:TPU:4, one launch (start us, length us, event | category | flops | bytes accessed | tf_op | source)
XLA Modules:
  0.0 88.9 jit_solution(6469107495962225167)
XLA Ops:
  0.6 1.5 %shard_map.105 = bf16[16,128]{1,0:T(8,128)(2,1)} custom-call(s32[1,8]{1,0:T(1,128)} %cuts_ref.7, bf16[256,128]{1,0:T(8,128)(2,1)} %features_ref.3), custom_call_target="tpu_custom_call" | custom-call | tf_op jit(solution)/shard_map/pallas_call | solution.py:367
  2.1 5.8 %collective-permute-start.1 = (bf16[16,128]{1,0:T(8,128)(2,1)}, bf16[16,128]{1,0:T(8,128)(2,1)S(1)}, u32[]{:S(2)}, u32[]{:S(2)}) collective-permute-start(bf16[16,128]{1,0:T(8,128)(2,1)} %shard_map.105), channel_id=1, source_target_pairs={{1,2},{2,1},{3,4},{4,3},{5,6},{6,5},{7,8},{8,7},{9,10},{10,9},{11,... | collective-permute-start | bytes 12296 | tf_op jit(solution)/shard_map/ppermute | solution.py:33
  8.0 2.8 %collective-permute-done.1.far_ref = bf16[16,128]{1,0:T(8,128)(2,1)S(1)} collective-permute-done((bf16[16,128]{1,0:T(8,128)(2,1)}, bf16[16,128]{1,0:T(8,128)(2,1)S(1)}, u32[]{:S(2)}, u32[]{:S(2)}) %collective-permute-start.1) | collective-permute-done | bytes 4128 | tf_op jit(solution)/shard_map/ppermute | solution.py:33
  12.0 1.6 %shard_map.106.refs_3_.refs_11_ = bf16[256,128]{1,0:T(8,128)(2,1)} custom-call(s32[1,8]{1,0:T(1,128)} %cuts_ref.7, bf16[256,128]{1,0:T(8,128)(2,1)} %features_ref.3, bf16[16,128]{1,0:T(8,128)(2,1)} %copy-done.17, bf16[16,128]{1,0:T(8,128)(2,1)} %copy-done.16), custom_call_target="tpu_custom_call" | custom-call | tf_op jit(solution)/shard_map/pallas_call | solution.py:376
  13.6 4.4 %collective-permute-start.2 = (bf16[256,128]{1,0:T(8,128)(2,1)}, bf16[256,128]{1,0:T(8,128)(2,1)S(1)}, u32[]{:S(2)}, u32[]{:S(2)}) collective-permute-start(bf16[256,128]{1,0:T(8,128)(2,1)} %shard_map.106.refs_3_.refs_11_), channel_id=1, source_target_pairs={{0,2},{1,3},{2,0},{3,1},{4,6},{5,7},{6,4},{7,5},{8,10},{9,11},{10,... | collective-permute-start | bytes 196616 | tf_op jit(solution)/shard_map/ppermute | solution.py:25
  18.0 2.1 %collective-permute-done.4.refs_9_ = bf16[256,128]{1,0:T(8,128)(2,1)S(1)} collective-permute-done((bf16[256,128]{1,0:T(8,128)(2,1)}, bf16[256,128]{1,0:T(8,128)(2,1)S(1)}, u32[]{:S(2)}, u32[]{:S(2)}) %collective-permute-start.4) | collective-permute-done | bytes 65568 | tf_op jit(solution)/shard_map/ppermute | solution.py:25
  20.8 1.3 %collective-permute-done.2.refs_5_ = bf16[256,128]{1,0:T(8,128)(2,1)S(1)} collective-permute-done((bf16[256,128]{1,0:T(8,128)(2,1)}, bf16[256,128]{1,0:T(8,128)(2,1)S(1)}, u32[]{:S(2)}, u32[]{:S(2)}) %collective-permute-start.2) | collective-permute-done | bytes 65568 | tf_op jit(solution)/shard_map/ppermute | solution.py:25
  27.1 10.4 %shard_map.104 = (bf16[2048,1024]{1,0:T(8,128)(2,1)S(1)}, s32[1,256]{1,0:T(1,128)S(1)}) custom-call(s32[1,1,384]{2,1,0:T(1,128)S(1)} %copy-done.3, s32[1,1,384]{2,1,0:T(1,128)S(1)} %copy-done.4, s32[1,1,384]{2,1,0:T(1,128)S(1)} %copy-done.5, s32[1,1]{1,0:T(1,128)S(6)} %copy.15.count_hbm, s32[1,1,128]{2,1,0:T(1,128)S(1)} %copy-done.6, s32[1,1,128]{2,1,0:T(1,128)S(1)} %copy-done.7), custom_call_target="tpu_custom_call" | custom-call | flops 62914560 | bytes 16777216 | tf_op jit(solution)/shard_map/pallas_call | solution.py:193
  37.5 6.0 %collective-permute-start.8 = (bf16[256,128]{1,0:T(8,128)(2,1)}, bf16[256,128]{1,0:T(8,128)(2,1)S(1)}, u32[]{:S(2)}, u32[]{:S(2)}) collective-permute-start(bf16[256,128]{1,0:T(8,128)(2,1)} %shard_map.106.refs_3_.refs_11_), channel_id=1, source_target_pairs={{0,24},{8,16},{16,8},{24,0},{1,25},{9,17},{17,9},{25,1},{2,26},{10... | collective-permute-start | bytes 196616 | tf_op jit(solution)/shard_map/ppermute | solution.py:25
  44.2 1.8 %collective-permute-done.8.refs_14_ = bf16[256,128]{1,0:T(8,128)(2,1)S(1)} collective-permute-done((bf16[256,128]{1,0:T(8,128)(2,1)}, bf16[256,128]{1,0:T(8,128)(2,1)S(1)}, u32[]{:S(2)}, u32[]{:S(2)}) %collective-permute-start.8) | collective-permute-done | bytes 65568 | tf_op jit(solution)/shard_map/ppermute | solution.py:25
  46.0 2.0 %collective-permute-done.7.refs_13_ = bf16[256,128]{1,0:T(8,128)(2,1)S(1)} collective-permute-done((bf16[256,128]{1,0:T(8,128)(2,1)}, bf16[256,128]{1,0:T(8,128)(2,1)S(1)}, u32[]{:S(2)}, u32[]{:S(2)}) %collective-permute-start.7) | collective-permute-done | bytes 65568 | tf_op jit(solution)/shard_map/ppermute | solution.py:25
  49.6 8.9 %shard_map.107 = (bf16[256,128]{1,0:T(8,128)(2,1)S(1)}, bf16[256,128]{1,0:T(8,128)(2,1)S(1)}, bf16[256,128]{1,0:T(8,128)(2,1)S(1)}, bf16[256,128]{1,0:T(8,128)(2...) custom-call(bf16[2048,1024]{1,0:T(8,128)(2,1)S(1)} %get-tuple-elemen, ...), custom_call_target="tpu_custom_call" | custom-call | flops 1610612736 | bytes 4194304 | tf_op jit(solution)/shard_map/pallas_call | solution.py:310
  59.5 1.3 %collective-permute-start.14 = (bf16[256,128]{1,0:T(8,128)(2,1)S(1)}, bf16[256,128]{1,0:T(8,128)(2,1)S(1)}, u32[]{:S(2)}, u32[]{:S(2)}) collective-permute-start(bf16[256,128]{1,0:T(8,128)(2,1)S(1)} %get-tuple-element.32), channel_id=1, source_target_pairs={{0,16},{8,24},{16,0},{24,8},{1,17},{9,25},{17,1},{25,9},{2,18},{10... | collective-permute-start | bytes 196616 | tf_op jit(solution)/shard_map/ppermute | solution.py:25
  60.9 1.5 %collective-permute-start.20 = (bf16[128,128]{1,0:T(8,128)(2,1)S(1)}, bf16[128,128]{1,0:T(8,128)(2,1)S(1)}, u32[]{:S(2)}, u32[]{:S(2)}) collective-permute-start(bf16[128,128]{1,0:T(8,128)(2,1)S(1)} %add_convert_fusion.5), channel_id=1, source_target_pairs={{0,24},{8,16},{16,8},{24,0},{1,25},{9,17},{17,9},{25,1},{2,26},{10... | collective-permute-start | bytes 98312 | tf_op jit(solution)/shard_map/ppermute | solution.py:25
  62.3 2.0 %collective-permute-start.19 = (bf16[128,128]{1,0:T(8,128)(2,1)S(1)}, bf16[128,128]{1,0:T(8,128)(2,1)S(1)}, u32[]{:S(2)}, u32[]{:S(2)}) collective-permute-start(bf16[128,128]{1,0:T(8,128)(2,1)S(1)} %add_convert_fusion.5), channel_id=1, source_target_pairs={{0,16},{8,24},{16,0},{24,8},{1,17},{9,25},{17,1},{25,9},{2,18},{10... | collective-permute-start | bytes 98312 | tf_op jit(solution)/shard_map/ppermute | solution.py:25
  65.1 1.4 %collective-permute-start.15 = (bf16[256,128]{1,0:T(8,128)(2,1)S(1)}, bf16[256,128]{1,0:T(8,128)(2,1)S(1)}, u32[]{:S(2)}, u32[]{:S(2)}) collective-permute-start(bf16[256,128]{1,0:T(8,128)(2,1)S(1)} %get-tuple-element.33), channel_id=1, source_target_pairs={{0,24},{8,16},{16,8},{24,0},{1,25},{9,17},{17,9},{25,1},{2,26},{10... | collective-permute-start | bytes 196616 | tf_op jit(solution)/shard_map/ppermute | solution.py:25
  67.4 1.2 %collective-permute-done.18 = bf16[128,128]{1,0:T(8,128)(2,1)S(1)} collective-permute-done((bf16[128,128]{1,0:T(8,128)(2,1)S(1)}, bf16[128,128]{1,0:T(8,128)(2,1)S(1)}, u32[]{:S(2)}, u32[]{:S(2)}) %collective-permute-start.18) | collective-permute-done | bytes 32800 | tf_op jit(solution)/shard_map/ppermute | solution.py:25
  68.6 2.3 %collective-permute-start.10 = (bf16[256,128]{1,0:T(8,128)(2,1)S(1)}, bf16[256,128]{1,0:T(8,128)(2,1)S(1)}, u32[]{:S(2)}, u32[]{:S(2)}) collective-permute-start(bf16[256,128]{1,0:T(8,128)(2,1)S(1)} %get-tuple-element.38), channel_id=1, source_target_pairs={{0,2},{1,3},{2,0},{3,1},{4,6},{5,7},{6,4},{7,5},{8,10},{9,11},{10,... | collective-permute-start | bytes 196616 | tf_op jit(solution)/shard_map/ppermute | solution.py:25
  71.0 0.9 %collective-permute-start.23 = (bf16[128,128]{1,0:T(8,128)(2,1)S(1)}, bf16[128,128]{1,0:T(8,128)(2,1)S(1)}, u32[]{:S(2)}, u32[]{:S(2)}) collective-permute-start(bf16[128,128]{1,0:T(8,128)(2,1)S(1)} %add_convert_fusion.4), channel_id=1, source_target_pairs={{0,6},{1,7},{2,4},{3,5},{4,2},{5,3},{6,0},{7,1},{8,14},{9,15},{10,... | collective-permute-start | bytes 98312 | tf_op jit(solution)/shard_map/ppermute | solution.py:25
  73.0 2.5 %collective-permute-start.21 = (bf16[128,128]{1,0:T(8,128)(2,1)S(1)}, bf16[128,128]{1,0:T(8,128)(2,1)S(1)}, u32[]{:S(2)}, u32[]{:S(2)}) collective-permute-start(bf16[128,128]{1,0:T(8,128)(2,1)S(1)} %add_convert_fusion.4), channel_id=1, source_target_pairs={{0,2},{1,3},{2,0},{3,1},{4,6},{5,7},{6,4},{7,5},{8,10},{9,11},{10,... | collective-permute-start | bytes 98312 | tf_op jit(solution)/shard_map/ppermute | solution.py:25
  76.1 1.9 %shard_map.108 = (bf16[256,128]{1,0:T(8,128)(2,1)}, bf16[16,128]{1,0:T(8,128)(2,1)}) custom-call(s32[1,8]{1,0:T(1,128)} %cuts_ref.7, bf16[128,128]{1,0:T(8,128)(2,1)} %weight_ref.1, bf16[256,128]{1,0:T(8,128)(2,1)} %get-tuple-element.39.refs_0_, bf16[256,128]{1,0:T(8,128)(2,1)} %copy-done.13, bf16[256,128]{1,0:T(8,128)(2,1)} %copy-done.12, ...), custom_call_target="tpu_custom_call" | custom-call | tf_op jit(solution)/shard_map/pallas_call | solution.py:408
  78.0 1.9 %collective-permute-start.17 = (bf16[16,128]{1,0:T(8,128)(2,1)}, bf16[16,128]{1,0:T(8,128)(2,1)S(1)}, u32[]{:S(2)}, u32[]{:S(2)}) collective-permute-start(bf16[16,128]{1,0:T(8,128)(2,1)} %get-tuple-element.35), channel_id=1, source_target_pairs={{1,2},{2,1},{3,4},{4,3},{5,6},{6,5},{7,8},{8,7},{9,10},{10,9},{11,... | collective-permute-start | bytes 12296 | tf_op jit(solution)/shard_map/ppermute | solution.py:33
  80.8 6.0 %collective-permute-done.17.far_ref = bf16[16,128]{1,0:T(8,128)(2,1)S(1)} collective-permute-done((bf16[16,128]{1,0:T(8,128)(2,1)}, bf16[16,128]{1,0:T(8,128)(2,1)S(1)}, u32[]{:S(2)}, u32[]{:S(2)}) %collective-permute-start.17) | collective-permute-done | bytes 4128 | tf_op jit(solution)/shard_map/ppermute | solution.py:33
  87.3 1.6 %shard_map.109 = bf16[256,128]{1,0:T(8,128)(2,1)} custom-call(s32[1,8]{1,0:T(1,128)} %cuts_ref.7, bf16[256,128]{1,0:T(8,128)(2,1)} %get-tuple-element.34.features_ref, bf16[16,128]{1,0:T(8,128)(2,1)} %copy-done.15, bf16[16,128]{1,0:T(8,128)(2,1)} %copy-done.14), custom_call_target="tpu_custom_call" | custom-call | tf_op jit(solution)/shard_map/pallas_call | solution.py:416
  (77 shorter events, 14.3 us)
Async XLA Ops:
  2.1 8.7 %collective-permute-start.1 = (bf16[16,128]{1,0:T(8,128)(2,1)}, bf16[16,128]{1,0:T(8,128)(2,1)S(1)}, u32[]{:S(2)}, u32[]{:S(2)}) collective-permute-start(bf16[16,128]{1,0:T(8,128)(2,1)} %shard_map.105), channel_id=1, source_target_pairs={{1,2},{2,1},{3,4},{4,3},{5,6},{6,5},{7,8},{8,7},{9,10},{10,9},{11,... | collective-permute-start | bytes 12296 | tf_op jit(solution)/shard_map/ppermute | solution.py:33
  7.9 2.9 %collective-permute-start = (bf16[16,128]{1,0:T(8,128)(2,1)}, bf16[16,128]{1,0:T(8,128)(2,1)S(1)}, u32[]{:S(2)}, u32[]{:S(2)}) collective-permute-start(bf16[16,128]{1,0:T(8,128)(2,1)} %shard_map.105), channel_id=1, source_target_pairs={{0,1},{1,0},{2,3},{3,2},{4,5},{5,4},{6,7},{7,6},{8,9},{9,8},{10,11... | collective-permute-start | bytes 12296 | tf_op jit(solution)/shard_map/ppermute | solution.py:25
  13.6 6.5 %collective-permute-start.4 = (bf16[256,128]{1,0:T(8,128)(2,1)}, bf16[256,128]{1,0:T(8,128)(2,1)S(1)}, u32[]{:S(2)}, u32[]{:S(2)}) collective-permute-start(bf16[256,128]{1,0:T(8,128)(2,1)} %shard_map.106.refs_3_.refs_11_), channel_id=1, source_target_pairs={{0,6},{1,7},{2,4},{3,5},{4,2},{5,3},{6,0},{7,1},{8,14},{9,15},{10,... | collective-permute-start | bytes 196616 | tf_op jit(solution)/shard_map/ppermute | solution.py:25
  13.6 7.2 %collective-permute-start.3 = (bf16[256,128]{1,0:T(8,128)(2,1)}, bf16[256,128]{1,0:T(8,128)(2,1)S(1)}, u32[]{:S(2)}, u32[]{:S(2)}) collective-permute-start(bf16[256,128]{1,0:T(8,128)(2,1)} %shard_map.106.refs_3_.refs_11_), channel_id=1, source_target_pairs={{0,4},{1,5},{2,6},{3,7},{4,0},{5,1},{6,2},{7,3},{8,12},{9,13},{10,... | collective-permute-start | bytes 196616 | tf_op jit(solution)/shard_map/ppermute | solution.py:25
  13.6 8.5 %collective-permute-start.2 = (bf16[256,128]{1,0:T(8,128)(2,1)}, bf16[256,128]{1,0:T(8,128)(2,1)S(1)}, u32[]{:S(2)}, u32[]{:S(2)}) collective-permute-start(bf16[256,128]{1,0:T(8,128)(2,1)} %shard_map.106.refs_3_.refs_11_), channel_id=1, source_target_pairs={{0,2},{1,3},{2,0},{3,1},{4,6},{5,7},{6,4},{7,5},{8,10},{9,11},{10,... | collective-permute-start | bytes 196616 | tf_op jit(solution)/shard_map/ppermute | solution.py:25
  23.0 21.2 %collective-permute-start.5 = (bf16[1024,128]{1,0:T(8,128)(2,1)S(1)}, bf16[1024,128]{1,0:T(8,128)(2,1)S(1)}, u32[]{:S(2)}, u32[]{:S(2)}) collective-permute-start(bf16[1024,128]{1,0:T(8,128)(2,1)S(1)} %pad_maximum_fusion), channel_id=1, source_target_pairs={{0,1},{1,0},{2,3},{3,2},{4,5},{5,4},{6,7},{7,6},{8,9},{9,8},{10,11... | collective-permute-start | bytes 786440 | tf_op jit(solution)/shard_map/ppermute | solution.py:25
  37.5 8.5 %collective-permute-start.8 = (bf16[256,128]{1,0:T(8,128)(2,1)}, bf16[256,128]{1,0:T(8,128)(2,1)S(1)}, u32[]{:S(2)}, u32[]{:S(2)}) collective-permute-start(bf16[256,128]{1,0:T(8,128)(2,1)} %shard_map.106.refs_3_.refs_11_), channel_id=1, source_target_pairs={{0,24},{8,16},{16,8},{24,0},{1,25},{9,17},{17,9},{25,1},{2,26},{10... | collective-permute-start | bytes 196616 | tf_op jit(solution)/shard_map/ppermute | solution.py:25
  43.5 4.5 %collective-permute-start.7 = (bf16[256,128]{1,0:T(8,128)(2,1)}, bf16[256,128]{1,0:T(8,128)(2,1)S(1)}, u32[]{:S(2)}, u32[]{:S(2)}) collective-permute-start(bf16[256,128]{1,0:T(8,128)(2,1)} %shard_map.106.refs_3_.refs_11_), channel_id=1, source_target_pairs={{0,16},{8,24},{16,0},{24,8},{1,17},{9,25},{17,1},{25,9},{2,18},{10... | collective-permute-start | bytes 196616 | tf_op jit(solution)/shard_map/ppermute | solution.py:25
  43.5 4.5 %collective-permute-start.6 = (bf16[256,128]{1,0:T(8,128)(2,1)}, bf16[256,128]{1,0:T(8,128)(2,1)S(1)}, u32[]{:S(2)}, u32[]{:S(2)}) collective-permute-start(bf16[256,128]{1,0:T(8,128)(2,1)} %shard_map.106.refs_3_.refs_11_), channel_id=1, source_target_pairs={{0,8},{8,0},{16,24},{24,16},{1,9},{9,1},{17,25},{25,17},{2,10},{10... | collective-permute-start | bytes 196616 | tf_op jit(solution)/shard_map/ppermute | solution.py:25
  58.6 2.2 %collective-permute-start.9 = (bf16[1152,128]{1,0:T(8,128)(2,1)S(1)}, bf16[1152,128]{1,0:T(8,128)(2,1)S(1)}, u32[]{:S(2)}, u32[]{:S(2)}) collective-permute-start(bf16[1152,128]{1,0:T(8,128)(2,1)S(1)} %constant_dynamic-update-slice_fusion), channel_id=1, source_target_pairs={{0,1},{1,0},{2,3},{3,2},{4,5},{5,4},{6,7},{7,6},{8,9},{9,8},{10,11... | collective-permute-start | bytes 884744 | tf_op jit(solution)/shard_map/ppermute | solution.py:25
  58.7 6.5 %collective-permute-start.13 = (bf16[256,128]{1,0:T(8,128)(2,1)S(1)}, bf16[256,128]{1,0:T(8,128)(2,1)S(1)}, u32[]{:S(2)}, u32[]{:S(2)}) collective-permute-start(bf16[256,128]{1,0:T(8,128)(2,1)S(1)} %get-tuple-element.31), channel_id=1, source_target_pairs={{0,8},{8,0},{16,24},{24,16},{1,9},{9,1},{17,25},{25,17},{2,10},{10... | collective-permute-start | bytes 196616 | tf_op jit(solution)/shard_map/ppermute | solution.py:25
  59.5 11.4 %collective-permute-start.14 = (bf16[256,128]{1,0:T(8,128)(2,1)S(1)}, bf16[256,128]{1,0:T(8,128)(2,1)S(1)}, u32[]{:S(2)}, u32[]{:S(2)}) collective-permute-start(bf16[256,128]{1,0:T(8,128)(2,1)S(1)} %get-tuple-element.32), channel_id=1, source_target_pairs={{0,16},{8,24},{16,0},{24,8},{1,17},{9,25},{17,1},{25,9},{2,18},{10... | collective-permute-start | bytes 196616 | tf_op jit(solution)/shard_map/ppermute | solution.py:25
  60.9 5.7 %collective-permute-start.20 = (bf16[128,128]{1,0:T(8,128)(2,1)S(1)}, bf16[128,128]{1,0:T(8,128)(2,1)S(1)}, u32[]{:S(2)}, u32[]{:S(2)}) collective-permute-start(bf16[128,128]{1,0:T(8,128)(2,1)S(1)} %add_convert_fusion.5), channel_id=1, source_target_pairs={{0,24},{8,16},{16,8},{24,0},{1,25},{9,17},{17,9},{25,1},{2,26},{10... | collective-permute-start | bytes 98312 | tf_op jit(solution)/shard_map/ppermute | solution.py:25
  62.3 5.1 %collective-permute-start.19 = (bf16[128,128]{1,0:T(8,128)(2,1)S(1)}, bf16[128,128]{1,0:T(8,128)(2,1)S(1)}, u32[]{:S(2)}, u32[]{:S(2)}) collective-permute-start(bf16[128,128]{1,0:T(8,128)(2,1)S(1)} %add_convert_fusion.5), channel_id=1, source_target_pairs={{0,16},{8,24},{16,0},{24,8},{1,17},{9,25},{17,1},{25,9},{2,18},{10... | collective-permute-start | bytes 98312 | tf_op jit(solution)/shard_map/ppermute | solution.py:25
  64.3 4.3 %collective-permute-start.18 = (bf16[128,128]{1,0:T(8,128)(2,1)S(1)}, bf16[128,128]{1,0:T(8,128)(2,1)S(1)}, u32[]{:S(2)}, u32[]{:S(2)}) collective-permute-start(bf16[128,128]{1,0:T(8,128)(2,1)S(1)} %add_convert_fusion.5), channel_id=1, source_target_pairs={{0,8},{8,0},{16,24},{24,16},{1,9},{9,1},{17,25},{25,17},{2,10},{10... | collective-permute-start | bytes 98312 | tf_op jit(solution)/shard_map/ppermute | solution.py:25
  65.1 6.8 %collective-permute-start.15 = (bf16[256,128]{1,0:T(8,128)(2,1)S(1)}, bf16[256,128]{1,0:T(8,128)(2,1)S(1)}, u32[]{:S(2)}, u32[]{:S(2)}) collective-permute-start(bf16[256,128]{1,0:T(8,128)(2,1)S(1)} %get-tuple-element.33), channel_id=1, source_target_pairs={{0,24},{8,16},{16,8},{24,0},{1,25},{9,17},{17,9},{25,1},{2,26},{10... | collective-permute-start | bytes 196616 | tf_op jit(solution)/shard_map/ppermute | solution.py:25
  66.5 6.4 %collective-permute-start.12 = (bf16[256,128]{1,0:T(8,128)(2,1)S(1)}, bf16[256,128]{1,0:T(8,128)(2,1)S(1)}, u32[]{:S(2)}, u32[]{:S(2)}) collective-permute-start(bf16[256,128]{1,0:T(8,128)(2,1)S(1)} %get-tuple-element.36), channel_id=1, source_target_pairs={{0,6},{1,7},{2,4},{3,5},{4,2},{5,3},{6,0},{7,1},{8,14},{9,15},{10,... | collective-permute-start | bytes 196616 | tf_op jit(solution)/shard_map/ppermute | solution.py:25
  67.4 8.0 %collective-permute-start.11 = (bf16[256,128]{1,0:T(8,128)(2,1)S(1)}, bf16[256,128]{1,0:T(8,128)(2,1)S(1)}, u32[]{:S(2)}, u32[]{:S(2)}) collective-permute-start(bf16[256,128]{1,0:T(8,128)(2,1)S(1)} %get-tuple-element.37), channel_id=1, source_target_pairs={{0,4},{1,5},{2,6},{3,7},{4,0},{5,1},{6,2},{7,3},{8,12},{9,13},{10,... | collective-permute-start | bytes 196616 | tf_op jit(solution)/shard_map/ppermute | solution.py:25
  68.6 6.8 %collective-permute-start.10 = (bf16[256,128]{1,0:T(8,128)(2,1)S(1)}, bf16[256,128]{1,0:T(8,128)(2,1)S(1)}, u32[]{:S(2)}, u32[]{:S(2)}) collective-permute-start(bf16[256,128]{1,0:T(8,128)(2,1)S(1)} %get-tuple-element.38), channel_id=1, source_target_pairs={{0,2},{1,3},{2,0},{3,1},{4,6},{5,7},{6,4},{7,5},{8,10},{9,11},{10,... | collective-permute-start | bytes 196616 | tf_op jit(solution)/shard_map/ppermute | solution.py:25
  71.0 9.1 %collective-permute-start.23 = (bf16[128,128]{1,0:T(8,128)(2,1)S(1)}, bf16[128,128]{1,0:T(8,128)(2,1)S(1)}, u32[]{:S(2)}, u32[]{:S(2)}) collective-permute-start(bf16[128,128]{1,0:T(8,128)(2,1)S(1)} %add_convert_fusion.4), channel_id=1, source_target_pairs={{0,6},{1,7},{2,4},{3,5},{4,2},{5,3},{6,0},{7,1},{8,14},{9,15},{10,... | collective-permute-start | bytes 98312 | tf_op jit(solution)/shard_map/ppermute | solution.py:25
  71.9 8.2 %collective-permute-start.22 = (bf16[128,128]{1,0:T(8,128)(2,1)S(1)}, bf16[128,128]{1,0:T(8,128)(2,1)S(1)}, u32[]{:S(2)}, u32[]{:S(2)}) collective-permute-start(bf16[128,128]{1,0:T(8,128)(2,1)S(1)} %add_convert_fusion.4), channel_id=1, source_target_pairs={{0,4},{1,5},{2,6},{3,7},{4,0},{5,1},{6,2},{7,3},{8,12},{9,13},{10,... | collective-permute-start | bytes 98312 | tf_op jit(solution)/shard_map/ppermute | solution.py:25
  73.0 7.1 %collective-permute-start.21 = (bf16[128,128]{1,0:T(8,128)(2,1)S(1)}, bf16[128,128]{1,0:T(8,128)(2,1)S(1)}, u32[]{:S(2)}, u32[]{:S(2)}) collective-permute-start(bf16[128,128]{1,0:T(8,128)(2,1)S(1)} %add_convert_fusion.4), channel_id=1, source_target_pairs={{0,2},{1,3},{2,0},{3,1},{4,6},{5,7},{6,4},{7,5},{8,10},{9,11},{10,... | collective-permute-start | bytes 98312 | tf_op jit(solution)/shard_map/ppermute | solution.py:25
  78.0 8.7 %collective-permute-start.17 = (bf16[16,128]{1,0:T(8,128)(2,1)}, bf16[16,128]{1,0:T(8,128)(2,1)S(1)}, u32[]{:S(2)}, u32[]{:S(2)}) collective-permute-start(bf16[16,128]{1,0:T(8,128)(2,1)} %get-tuple-element.35), channel_id=1, source_target_pairs={{1,2},{2,1},{3,4},{4,3},{5,6},{6,5},{7,8},{8,7},{9,10},{10,9},{11,... | collective-permute-start | bytes 12296 | tf_op jit(solution)/shard_map/ppermute | solution.py:33
  79.9 6.8 %collective-permute-start.16 = (bf16[16,128]{1,0:T(8,128)(2,1)}, bf16[16,128]{1,0:T(8,128)(2,1)S(1)}, u32[]{:S(2)}, u32[]{:S(2)}) collective-permute-start(bf16[16,128]{1,0:T(8,128)(2,1)} %get-tuple-element.35), channel_id=1, source_target_pairs={{0,1},{1,0},{2,3},{3,2},{4,5},{5,4},{6,7},{7,6},{8,9},{9,8},{10,11... | collective-permute-start | bytes 12296 | tf_op jit(solution)/shard_map/ppermute | solution.py:25
  (18 other events, 31.9 us)

commit v2 on v0

v2 whole, which is shorter than its diff:
```python
import functools

import jax
import jax.numpy as jnp
from jax import lax
from jax.experimental import pallas as pl
from jax.experimental.pallas import tpu as pltpu
from jax.sharding import PartitionSpec as P

BLOCK = 128
AXES = ("row", "col")
INV5 = -858993459
ANY = pl.BlockSpec(memory_space=pl.ANY)
VMEM = pl.BlockSpec(memory_space=pltpu.VMEM)
HBM = pl.BlockSpec(memory_space=pltpu.HBM)
SMEM = pl.BlockSpec(memory_space=pltpu.SMEM)
CHUNK_CELLS = 128
PARTS = 3


def params(mib):
    return pltpu.CompilerParams(vmem_limit_bytes=mib * 2**20)


def swap(x, axis, step):
    count = lax.axis_size(axis)
    return lax.ppermute(x, axis, [(i, i ^ step) for i in range(count)])


def swap_next(x):
    count = lax.axis_size("row") * lax.axis_size("col")
    pairs = []
    for s in range(1, count - 1, 2):
        pairs += [(s, s + 1), (s + 1, s)]
    return lax.ppermute(x, AXES, pairs)


def swap_mixed(x, step):
    nrow, ncol = lax.axis_size("row"), lax.axis_size("col")
    pairs = []
    for r in range(nrow):
        for c in range(ncol):
            if c % 2 == 0 and step < ncol // 2:
                pairs.append((r * ncol + c, r * ncol + (c ^ (2 * step))))
            if c % 2 == 1 and step < nrow:
                pairs.append((r * ncol + c, (r ^ step) * ncol + c))
    return lax.ppermute(x, AXES, pairs)


def links(cuts_ref, rows, width):
    node = lax.broadcasted_iota(jnp.int32, (rows, width), 0)
    cut = node == cuts_ref[0, 0]
    for t in range(1, cuts_ref.shape[1]):
        cut = jnp.logical_or(cut, node == cuts_ref[0, t])
    return jnp.where(cut, 0.0, 1.0).astype(jnp.float32)


def edges(values, link, out_ref):
    rows, width = values.shape
    head = link[0:8] * values[0:8]
    tail = values[rows - 8 : rows]
    out_ref[...] = jnp.concatenate([head, tail], axis=0).astype(out_ref.dtype)


def stencil(values, link, prev, nxt):
    rows, width = values.shape
    node = lax.broadcasted_iota(jnp.int32, (rows, width), 0)
    before = jnp.where(node == 0, prev, pltpu.roll(values, 1, 0))
    after = jnp.where(node == rows - 1, nxt, pltpu.roll(link * values, rows - 1, 0))
    return 0.5 * values + 0.25 * (link * before + after)


def edge_kernel(cuts_ref, features_ref, out_ref):
    values = features_ref[...].astype(jnp.float32)
    edges(values, links(cuts_ref, *values.shape), out_ref)


def pair_kernel(cuts_ref, sib_cuts_ref, features_ref, sib_ref, far_ref, sib_far_ref, out_ref):
    shard = features_ref.shape[0]

    def both(first_cuts, second_cuts, first_ref, second_ref, before_ref, after_ref):
        first = first_ref[...].astype(jnp.float32)
        second = second_ref[...].astype(jnp.float32)
        first_link = links(first_cuts, *first.shape)
        second_link = links(second_cuts, *second.shape)
        prev = before_ref[...].astype(jnp.float32)[15:16]
        nxt = after_ref[...].astype(jnp.float32)[0:1]
        head = second_link[0:1] * second[0:1]
        tail = first[shard - 1 : shard]
        out_ref[0:shard, :] = stencil(first, first_link, prev, head).astype(out_ref.dtype)
        out_ref[shard:, :] = stencil(second, second_link, tail, nxt).astype(out_ref.dtype)

    odd = lax.rem(lax.axis_index("col"), 2)

    @pl.when(odd == 0)
    def _():
        both(cuts_ref, sib_cuts_ref, features_ref, sib_ref, far_ref, sib_far_ref)

    @pl.when(odd == 1)
    def _():
        both(sib_cuts_ref, cuts_ref, sib_ref, features_ref, sib_far_ref, far_ref)


def agg_kernel(cuts_ref, features_ref, near_ref, far_ref, out_ref):
    values = features_ref[...].astype(jnp.float32)
    link = links(cuts_ref, *values.shape)
    odd = lax.rem(lax.axis_index("col"), 2) == 1
    near = near_ref[...].astype(jnp.float32)
    far = far_ref[...].astype(jnp.float32)
    prev = jnp.where(odd, near[15:16], far[15:16])
    nxt = jnp.where(odd, far[0:1], near[0:1])
    out_ref[...] = stencil(values, link, prev, nxt).astype(out_ref.dtype)


class Slots:
    def __init__(self, slots, negatives, cut_count):
        self.slots, self.negatives = slots, negatives
        self.rows, self.cols, self.keys = 0, slots, 2 * slots
        self.nrows = 3 * slots
        self.ncols = self.nrows + negatives
        self.count = self.ncols + negatives
        self.cuts = self.count + 1
        self.cut_count = cut_count
        self.end = self.cuts + cut_count


def count_kernel(at, base, blocks, cols, per, meta_ref, n_ref):
    here_rows = per * 2 * (lax.axis_index("col") // 2)
    here_cols = per * lax.axis_index("row")
    width = cols * BLOCK
    total = jnp.zeros((blocks, width), jnp.float32)
    count = meta_ref[0:1, at.count : at.count + 1]
    for rows_at, cols_at, slots, positive in (
        (at.rows, at.cols, at.slots, True),
        (at.nrows, at.ncols, at.negatives, False),
    ):
        rows = jnp.bitwise_xor(meta_ref[0:1, rows_at : rows_at + slots], here_rows) - base
        cols_of = jnp.bitwise_xor(meta_ref[0:1, cols_at : cols_at + slots], here_cols)
        hit = lax.broadcasted_iota(jnp.int32, (blocks, slots), 0) == rows
        if positive:
            live = lax.broadcasted_iota(jnp.int32, (blocks, slots), 1) < count
            hit = jnp.logical_and(hit, live)
        lane = lax.shift_right_logical(lax.broadcasted_iota(jnp.int32, (width, slots), 0), 7)
        spread = jnp.where(lane == cols_of, 1.0, 0.0).astype(jnp.bfloat16)
        total += lax.dot_general(
            jnp.where(hit, 0.5, 0.0).astype(jnp.bfloat16), spread,
            (((1,), (1,)), ((), ())), preferred_element_type=jnp.float32,
        )
    n_ref[...] = total


def counts(at, base, blocks, cols, per, meta):
    return pl.pallas_call(
        functools.partial(count_kernel, at, base, blocks, cols, per),
        out_shape=jax.ShapeDtypeStruct((blocks, cols * BLOCK), jnp.float32),
        in_specs=[VMEM],
        out_specs=VMEM,
        compiler_params=params(8),
    )(meta)


def target_kernel(at, base, blocks, cols, per, part, parts, filtered, meta_s, *refs):
    t_ref, step_ref = refs[-2:]
    a = lax.broadcasted_iota(jnp.int32, (BLOCK, BLOCK), 0)
    b = lax.broadcasted_iota(jnp.int32, (BLOCK, BLOCK), 1)
    step_ref[...] = (a * BLOCK + b) * jnp.int32(4 * 40503)
    if part == 0:

        def clear(i, _):
            row = pl.multiple_of(i * BLOCK, BLOCK)
            t_ref[pl.ds(row, BLOCK), :] = jnp.zeros((BLOCK, cols * BLOCK), jnp.float32)
            return 0

        lax.fori_loop(0, blocks, clear, 0)
    here_rows = per * 2 * (lax.axis_index("col") // 2)
    here_cols = per * lax.axis_index("row")
    count = meta_s[0, at.count]
    unroll = 8 if at.slots % 8 == 0 else 1

    def positive(s):
        i = jnp.bitwise_xor(meta_s[0, at.rows + s], here_rows) - base
        j = jnp.bitwise_xor(meta_s[0, at.cols + s], here_cols)
        key = meta_s[0, at.keys + s] * 4
        one = jnp.where(s < count, 1.0, 0.0).astype(jnp.float32)

        def add():
            row = pl.multiple_of(i * BLOCK, BLOCK)
            col = pl.multiple_of(j * BLOCK, BLOCK)
            mixed = step_ref[...] + key
            mixed = jnp.bitwise_xor(mixed, lax.shift_right_logical(mixed, 11))
            fifth = lax.shift_right_logical(mixed, 9) * jnp.int32(INV5)
            hit = fifth.astype(jnp.uint32) < jnp.uint32(2**21)
            t_ref[pl.ds(row, BLOCK), pl.ds(col, BLOCK)] += jnp.where(hit, one, 0.0)

        if filtered:
            pl.when(jnp.logical_and(i >= 0, i < blocks))(add)
        else:
            add()

    def positives(g, _):
        for u in range(unroll):
            positive(g * unroll + u)
        return 0

    trips = (count + unroll - 1) // unroll
    lax.fori_loop(trips * part // parts, trips * (part + 1) // parts, positives, 0)


def targets(at, base, blocks, cols, per, part, parts, filtered, meta, before):
    shape = (blocks * BLOCK, cols * BLOCK)
    old = [] if before is None else [before]
    return pl.pallas_call(
        functools.partial(target_kernel, at, base, blocks, cols, per, part, parts, filtered),
        out_shape=jax.ShapeDtypeStruct(shape, jnp.float32),
        in_specs=[SMEM] + [VMEM] * len(old),
        out_specs=VMEM,
        input_output_aliases={1: 0} if old else {},
        scratch_shapes=[pltpu.VMEM((BLOCK, BLOCK), jnp.int32)],
        compiler_params=params(10),
        cost_estimate=pl.CostEstimate(
            flops=at.slots * BLOCK * BLOCK * 10 // parts,
            bytes_accessed=at.slots * BLOCK * BLOCK * 8 // parts,
            transcendentals=0,
        ),
    )(meta, *old)


def decode_kernel(nz, nrow, first, count, refs):
    steps = max(nz, nrow) - 1
    t_ref, n_ref, weight_ref, pair_ref = refs[:4]
    recv = refs[4 : 4 + steps]
    other = refs[4 + steps : 4 + 2 * steps]
    refs = refs[4 + 2 * steps :]
    keep_ref, give_ref = refs[:2]
    messages = refs[2 : 2 + nrow]
    row_agg, col_agg, row_z, col_z, col_acc = refs[2 + nrow :]
    shard = pair_ref.shape[0] // 2
    per = shard // BLOCK
    core = lax.rem(lax.axis_index("col"), 2)

    def gather(z_refs, row_refs, side):
        for k in range(count):
            ref = pair_ref if first + k == 0 else z_refs[first + k - 1]
            row_agg[2 * k * shard : 2 * (k + 1) * shard, :] = ref[...]
        for q in range(nrow):
            ref = pair_ref if q == 0 else row_refs[q - 1]
            col_agg[q * shard : (q + 1) * shard, :] = ref[side * shard : (side + 1) * shard, :]

    pl.when(core == 0)(lambda: gather(recv, other, 0))
    pl.when(core == 1)(lambda: gather(other, recv, 1))

    weight = weight_ref[...]
    dots = functools.partial(lax.dot_general, preferred_element_type=jnp.float32)
    nn = (((1,), (0,)), ((), ()))
    nt = (((1,), (1,)), ((), ()))
    tn = (((0,), (0,)), ((), ()))
    for q in range(nrow):
        at = slice(q * shard, (q + 1) * shard)
        col_z[at, :] = dots(col_agg[at, :], weight, nn).astype(jnp.bfloat16)
    for p in range(2 * count):
        at = slice(p * shard, (p + 1) * shard)
        row_z[at, :] = dots(row_agg[at, :], weight, nn).astype(jnp.bfloat16)
    share = jnp.zeros(weight.shape, jnp.float32)
    for k in range(count):
        drows = []
        for p in (2 * k, 2 * k + 1):
            near = row_z[p * shard : (p + 1) * shard, :]
            half = near * jnp.bfloat16(0.5)
            drow = None
            for q in range(nrow):
                far = col_z[q * shard : (q + 1) * shard, :]
                curve = jnp.tanh(dots(half, far, nt))
                bands = []
                for i in range(per):
                    band = slice(i * BLOCK, (i + 1) * BLOCK)
                    n = n_ref[p * per + i : p * per + i + 1, q * shard : (q + 1) * shard]
                    row = p * shard + i * BLOCK
                    tile = t_ref[row : row + BLOCK, q * shard : (q + 1) * shard]
                    bands.append((n * curve[band] + (n - tile)).astype(jnp.bfloat16))
                grad = jnp.concatenate(bands, axis=0)
                term = dots(grad, far, nn)
                drow = term if drow is None else drow + term
                back = dots(grad, near, tn)
                if p == 0:
                    col_acc[q * shard : (q + 1) * shard, :] = back
                else:
                    col_acc[q * shard : (q + 1) * shard, :] += back
            drow = drow * (1.0 / 32.0)
            share += dots(row_agg[p * shard : (p + 1) * shard, :], drow.astype(jnp.bfloat16), tn)
            drows.append(drow)
        at = slice(k * shard, (k + 1) * shard)
        keep_ref[at, :] = jnp.where(core == 0, drows[0], drows[1])
        give_ref[at, :] = jnp.where(core == 0, drows[1], drows[0]).astype(give_ref.dtype)
    for q in range(nrow):
        at = slice(q * shard, (q + 1) * shard)
        rounded = (col_acc[at, :] * (1.0 / 32.0)).astype(jnp.bfloat16)
        messages[q][0:shard, :] = rounded
        share += dots(col_agg[at, :], rounded, tn)
    for q in range(nrow):
        messages[q][shard:, :] = share.astype(messages[q].dtype)


def decode(t, n, weight, pair, recv, other, nz, nrow, first, count):
    shard = pair.shape[0] // 2
    width = weight.shape[1]
    bf16, real = jnp.bfloat16, jnp.float32
    outs = [
        jax.ShapeDtypeStruct((count * shard, width), real),
        jax.ShapeDtypeStruct((count * shard, width), bf16),
    ]
    outs += [jax.ShapeDtypeStruct((shard + weight.shape[0], width), bf16)] * nrow
    result = pl.pallas_call(
        lambda *refs: decode_kernel(nz, nrow, first, count, refs),
        out_shape=outs,
        in_specs=[VMEM] * (4 + len(recv) + len(other)),
        out_specs=[VMEM] * len(outs),
        scratch_shapes=[
            pltpu.VMEM((2 * count * shard, width), bf16),
            pltpu.VMEM((nrow * shard, width), bf16),
            pltpu.VMEM((2 * count * shard, width), bf16),
            pltpu.VMEM((nrow * shard, width), bf16),
            pltpu.VMEM((nrow * shard, width), real),
        ],
        compiler_params=params(24),
        cost_estimate=pl.CostEstimate(
            flops=6 * t.shape[0] * t.shape[1] * width,
            bytes_accessed=t.shape[0] * t.shape[1] * 2,
            transcendentals=t.shape[0] * t.shape[1],
        ),
    )(t, n, weight, pair, *recv, *other)
    return result[0], result[1], result[2:]


def latent_kernel(nz, nrow, cuts_ref, weight_ref, *refs):
    shard = refs[0].shape[0]
    dagg_ref, edge_ref = refs[nz + nrow :]
    total = refs[0][...].astype(jnp.float32)
    for part in refs[1:nz]:
        total += part[...].astype(jnp.float32)
    for part in refs[nz : nz + nrow]:
        total += part[0:shard, :].astype(jnp.float32)
    dlatent = total.astype(jnp.bfloat16)
    dagg = lax.dot_general(
        dlatent, weight_ref[...], (((1,), (1,)), ((), ())), preferred_element_type=jnp.float32
    ).astype(jnp.bfloat16)
    dagg_ref[...] = dagg
    values = dagg.astype(jnp.float32)
    edges(values, links(cuts_ref, *values.shape), edge_ref)


def f32(x):
    return x.astype(jnp.float32)


def tree_sum(parts):
    parts = [f32(x) for x in parts]
    while len(parts) > 1:
        parts = [a + b for a, b in zip(parts[::2], parts[1::2])]
    return parts[0]


def local(features, weight, cuts, pos_rows, pos_cols, pos_keys, pos_count, neg_rows, neg_cols):
    shard, width = features.shape
    ncol = lax.axis_size("col")
    nrow = lax.axis_size("row")
    nz = ncol // 2
    per = shard // BLOCK
    steps = max(nz, nrow)
    bf16 = jnp.bfloat16
    message = jax.ShapeDtypeStruct((16, width), bf16)
    sib, sib_cuts = swap(features, "col", 1), swap(cuts, "col", 1)
    ends = pl.pallas_call(
        edge_kernel, out_shape=message, in_specs=[SMEM, VMEM], out_specs=VMEM,
        compiler_params=params(2),
    )(cuts, features)
    far = swap_next(ends)
    cols = nrow * per
    pieces = max(1, ncol * per * cols // CHUNK_CELLS)
    blocks = ncol * per // pieces
    parts = PARTS if pieces == 1 else 1
    slots = [x.reshape(1, -1) for x in (pos_rows, pos_cols, pos_keys, neg_rows, neg_cols, pos_count)]
    at = Slots(slots[0].shape[1], slots[3].shape[1], 0)
    meta = jnp.concatenate(slots + [jnp.zeros((1, -at.end % BLOCK), jnp.int32)], axis=1)
    found = [
        targets(at, k * blocks, blocks, cols, per, 0, parts, pieces > 1, meta, None)
        for k in range(pieces)
    ]
    number = [counts(at, k * blocks, blocks, cols, per, meta) for k in range(pieces)]
    if pieces == 1:
        far, found = lax.optimization_barrier((far, found))
    sib_far = swap(far, "col", 1)
    pair = pl.pallas_call(
        pair_kernel,
        out_shape=jax.ShapeDtypeStruct((2 * shard, width), bf16),
        in_specs=[SMEM, SMEM] + [VMEM] * 4,
        out_specs=VMEM,
        compiler_params=params(4),
    )(cuts, sib_cuts, features, sib, far, sib_far)
    recv = [swap_mixed(pair, k) for k in range(1, steps)]
    if pieces == 1:
        t = targets(at, 0, blocks, cols, per, 1, parts, False, meta, found[0])
        recv, t = lax.optimization_barrier((recv, t))
        other = [swap(x, "col", 1) for x in recv]
        t = targets(at, 0, blocks, cols, per, 2, parts, False, meta, t)
        found = [t]
    else:
        other = [swap(x, "col", 1) for x in recv]
    count = nz // pieces
    keeps, gives, messages = [], [], []
    for k, (t, n) in enumerate(zip(found, number)):
        out = decode(t, n, weight, pair, recv, other, nz, nrow, k * count, count)
        keeps.append(out[0])
        gives.append(out[1])
        messages.append(out[2])
    messages = messages[0] if pieces == 1 else [tree_sum(x).astype(bf16) for x in zip(*messages)]
    give = gives[0] if pieces == 1 else jnp.concatenate(gives, axis=0)
    keep = keeps[0] if pieces == 1 else jnp.concatenate(keeps, axis=0)
    got = swap(give, "col", 1)
    columns = [messages[0]] + [swap(messages[k], "row", k) for k in range(1, nrow)]
    kept = [
        (keep[k * shard : (k + 1) * shard] + f32(got[k * shard : (k + 1) * shard])).astype(bf16)
        for k in range(nz)
    ]
    rows = [kept[0]] + [swap(kept[k], "col", 2 * k) for k in range(1, nz)]
    share = tree_sum([x[shard:] for x in columns])
    share = (share + swap(share, "col", 1)).astype(bf16)
    dagg, dends = pl.pallas_call(
        functools.partial(latent_kernel, nz, nrow),
        out_shape=(jax.ShapeDtypeStruct(features.shape, bf16), message),
        in_specs=[SMEM, VMEM] + [VMEM] * (nz + nrow),
        out_specs=(VMEM, VMEM),
        compiler_params=params(6),
    )(cuts, weight, *rows, *columns)
    near, far = swap(dends, "col", 1), swap_next(dends)
    share = tree_sum([share] + [swap(share, "col", 2 * k) for k in range(1, nz)])
    grad_features = pl.pallas_call(
        agg_kernel,
        out_shape=jax.ShapeDtypeStruct(features.shape, bf16),
        in_specs=[SMEM, VMEM, VMEM, VMEM],
        out_specs=VMEM,
        compiler_params=params(4),
    )(cuts, dagg, near, far)
    grad_weight = share * (shard * ncol * nrow) ** (-0.5)
    return (grad_features, grad_weight)


def solution(mesh):
    placed = (
        P(AXES, None),
        P(),
        P(AXES, None),
        P("row", "col", None),
        P("row", "col", None),
        P("row", "col", None),
        P("row", "col"),
        P("row", "col", None),
        P("row", "col", None),
    )
    return jax.shard_map(
        local, mesh=mesh, in_specs=placed, out_specs=(P(AXES, None), P()), check_vma=False
    )
```

time: 587 us -> 65.3 us (0.11)
  the two profiles are of different devices: /device:TPU:0 before, /device:TPU:4 now
where the time goes in v2:
time: 65.3 us; the launch traced here: 65.7 us
  starting transfers between devices  30.7 us (47%)
  Pallas kernels  17.5 us (27%)
  waiting for transfers between devices  12.9 us (20%)
  local copies, waits for them, and re-layouts  2.33 us (4%)
  between operations  1.53 us (2%)
  other arithmetic  0.74 us (1%)
    ppermute x18, starting transfers between devices, swap(): return lax.ppermute(x, axis, [(i, i ^ step) for i in range(count)])  15.1 us
    ppermute x2, starting transfers between devices, swap_next(): return lax.ppermute(x, AXES, pairs)  11.2 us
    ppermute x18, waiting for transfers between devices, swap(): return lax.ppermute(x, axis, [(i, i ^ step) for i in range(count)])  7.36 us
    pallas_call x1, Pallas kernels, decode(): pl.pallas_call(lambda *refs: decode_kernel(nz, nrow, first, count, refs),...  7.06 us
    pallas_call x3, Pallas kernels, targets(): pl.pallas_call(functools.partial(target_kernel, at, base, blocks, cols, p...  6.62 us
    ppermute x3, starting transfers between devices, swap_mixed(): return lax.ppermute(x, AXES, pairs)  4.44 us
    ppermute x2, waiting for transfers between devices, swap_next(): return lax.ppermute(x, AXES, pairs)  3.13 us
    ppermute x3, waiting for transfers between devices, swap_mixed(): return lax.ppermute(x, AXES, pairs)  2.42 us
  transfers between devices with their start and end apart: 23, of which 6 were waited for; matrix products, arithmetic and copies ran while one was open for 2% of the time, Pallas kernels for 13%

profile of v2, /device:TPU:4, one launch (start us, length us, event | category | flops | bytes accessed | tf_op | source)
XLA Modules:
  0.0 65.7 jit_solution(1438679608031899876)
XLA Ops:
  0.7 0.8 %copy-done = bf16[256,128]{1,0:T(8,128)(2,1)S(1)} copy-done((bf16[256,128]{1,0:T(8,128)(2,1)S(1)}, bf16[256,128]{1,0:T(8,128)(2,1)}, u32[]{:S(2)}) %copy-start) | copy-done | bytes 65560
  2.8 6.5 %collective-permute-start.2 = (bf16[16,128]{1,0:T(8,128)(2,1)S(1)}, bf16[16,128]{1,0:T(8,128)(2,1)S(1)}, u32[]{:S(2)}, u32[]{:S(2)}) collective-permute-start(bf16[16,128]{1,0:T(8,128)(2,1)S(1)} %shard_map.104), channel_id=1, source_target_pairs={{1,2},{2,1},{3,4},{4,3},{5,6},{6,5},{7,8},{8,7},{9,10},{10,9},{11,... | collective-permute-start | bytes 12296 | tf_op jit(solution)/shard_map/ppermute | solution.py:35
  9.9 0.8 %concatenate.3.meta_s.meta_ref = s32[1,1536]{1,0:T(1,128)S(1)} concatenate(s32[1,384]{1,0:T(1,128)} %bitcast.5, s32[1,384]{1,0:T(1,128)} %bitcast.6, s32[1,384]{1,0:T(1,128)} %bitcast.7, s32[1,128]{1,0:T(1,128)} %bitcast.8, s32[1,128]{1,0:T(1,128)} %bitcast.9, s32[1,1]{1,0:T(1,128)S(6)} %copy.15, s32[1,127]{1,0:T(1,128)S(1)} %broadcast_in_dim.3), dimensions={1} | concatenate | bytes 12288 | tf_op jit(solution)/shard_map/concatenate | solution.py:383
  10.7 2.6 %shard_map.105.refs_0_ = f32[2048,1024]{1,0:T(8,128)S(1)} custom-call(s32[1,1536]{1,0:T(1,128)S(1)} %concatenate.3.meta_s.meta_ref), custom_call_target="tpu_custom_call" | custom-call | flops 20971520 | bytes 16777216 | tf_op jit(solution)/shard_map/pallas_call | solution.py:212
  13.9 0.8 %collective-permute-done.sib_cuts_ref = s32[1,8]{1,0:T(1,128)S(1)} collective-permute-done((s32[1,8]{1,0:T(1,128)S(1)}, s32[1,8]{1,0:T(1,128)S(1)}, u32[]{:S(2)}, u32[]{:S(2)}) %collective-permute-start) | collective-permute-done | bytes 64 | tf_op jit(solution)/shard_map/ppermute | solution.py:27
  14.8 0.8 %shard_map.106.refs_3_ = bf16[512,128]{1,0:T(8,128)(2,1)S(1)} custom-call(s32[1,8]{1,0:T(1,128)S(1)} %copy-done.4, s32[1,8]{1,0:T(1,128)S(1)} %collective-permute-done.sib_cuts_ref, bf16[256,128]{1,0:T(8,128)(2,1)S(1)} %copy-done.1, bf16[256,128]{1,0:T(8,128)(2,1)S(1)} %collective-permute-done.1.sib_ref, bf16[16,128]{1,0:T(8,128)(2,1)S(1)} %collective-permute-done.2.far_ref, ...), custom_call_target="tpu_custom_call" | custom-call | tf_op jit(solution)/shard_map/pallas_call | solution.py:392
  15.7 1.4 %collective-permute-start.5 = (bf16[512,128]{1,0:T(8,128)(2,1)S(1)}, bf16[512,128]{1,0:T(8,128)(2,1)S(1)}, u32[]{:S(2)}, u32[]{:S(2)}) collective-permute-start(bf16[512,128]{1,0:T(8,128)(2,1)S(1)} %shard_map.106.refs_3_), channel_id=1, source_target_pairs={{0,4},{1,17},{2,6},{3,19},{4,0},{5,21},{6,2},{7,23},{8,12},{9,25},... | collective-permute-start | bytes 393224 | tf_op jit(solution)/shard_map/ppermute | solution.py:47
  17.1 3.0 %collective-permute-start.6 = (bf16[512,128]{1,0:T(8,128)(2,1)S(1)}, bf16[512,128]{1,0:T(8,128)(2,1)S(1)}, u32[]{:S(2)}, u32[]{:S(2)}) collective-permute-start(bf16[512,128]{1,0:T(8,128)(2,1)S(1)} %shard_map.106.refs_3_), channel_id=1, source_target_pairs={{0,6},{1,25},{2,4},{3,27},{4,2},{5,29},{6,0},{7,31},{8,14},{9,17},... | collective-permute-start | bytes 393224 | tf_op jit(solution)/shard_map/ppermute | solution.py:47
  20.0 2.0 %shard_map.107.refs_0_ = f32[2048,1024]{1,0:T(8,128)S(1)} custom-call(s32[1,1536]{1,0:T(1,128)S(1)} %concatenate.3.meta_s.meta_ref, f32[2048,1024]{1,0:T(8,128)S(1)} %shard_map.105.refs_0_), custom_call_target="tpu_custom_call", output_to_operand_aliasing={{}: (1, {})} | custom-call | flops 20971520 | bytes 16777216 | tf_op jit(solution)/shard_map/pallas_call | solution.py:212
  22.1 2.4 %collective-permute-done.6.refs_6_ = bf16[512,128]{1,0:T(8,128)(2,1)S(1)} collective-permute-done((bf16[512,128]{1,0:T(8,128)(2,1)S(1)}, bf16[512,128]{1,0:T(8,128)(2,1)S(1)}, u32[]{:S(2)}, u32[]{:S(2)}) %collective-permute-start.6) | collective-permute-done | bytes 131104 | tf_op jit(solution)/shard_map/ppermute | solution.py:47
  25.4 2.0 %shard_map.108.refs_0_ = f32[2048,1024]{1,0:T(8,128)S(1)} custom-call(s32[1,1536]{1,0:T(1,128)S(1)} %concatenate.3.meta_s.meta_ref, f32[2048,1024]{1,0:T(8,128)S(1)} %shard_map.107.refs_0_), custom_call_target="tpu_custom_call", output_to_operand_aliasing={{}: (1, {})} | custom-call | flops 20971520 | bytes 16777216 | tf_op jit(solution)/shard_map/pallas_call | solution.py:212
  27.5 7.1 %shard_map.110 = (f32[1024,128]{1,0:T(8,128)S(1)}, bf16[1024,128]{1,0:T(8,128)(2,1)S(1)}, bf16[384,128]{1,0:T(8,128)(2,1)S(1)}, bf16[384,128]{1,0:T(8,128)(2,1)S...) custom-call(f32[2048,1024]{1,0:T(8,128)S(1)} %shard_map.108.refs_0_, f32[16,1024]{1,0:T(8,128)S(1)} %shard_map.109.refs_1_, ...), custom_call_target="tpu_custom_call" | custom-call | flops 1610612736 | bytes 4194304 | tf_op jit(solution)/shard_map/pallas_call | solution.py:312
  34.5 3.4 %collective-permute-start.14 = (bf16[384,128]{1,0:T(8,128)(2,1)S(1)}, bf16[384,128]{1,0:T(8,128)(2,1)S(1)}, u32[]{:S(2)}, u32[]{:S(2)}) collective-permute-start(bf16[384,128]{1,0:T(8,128)(2,1)S(1)} %get-tuple-element.25), channel_id=1, source_target_pairs={{0,8},{8,0},{16,24},{24,16},{1,9},{9,1},{17,25},{25,17},{2,10},{10... | collective-permute-start | bytes 294920 | tf_op jit(solution)/shard_map/ppermute | solution.py:27
  37.9 1.5 %collective-permute-start.16 = (bf16[384,128]{1,0:T(8,128)(2,1)S(1)}, bf16[384,128]{1,0:T(8,128)(2,1)S(1)}, u32[]{:S(2)}, u32[]{:S(2)}) collective-permute-start(bf16[384,128]{1,0:T(8,128)(2,1)S(1)} %get-tuple-element.27), channel_id=1, source_target_pairs={{0,24},{8,16},{16,8},{24,0},{1,25},{9,17},{17,9},{25,1},{2,26},{10... | collective-permute-start | bytes 294920 | tf_op jit(solution)/shard_map/ppermute | solution.py:27
  39.4 1.9 %collective-permute-done.14.refs_5_ = bf16[384,128]{1,0:T(8,128)(2,1)S(1)} collective-permute-done((bf16[384,128]{1,0:T(8,128)(2,1)S(1)}, bf16[384,128]{1,0:T(8,128)(2,1)S(1)}, u32[]{:S(2)}, u32[]{:S(2)}) %collective-permute-start.14) | collective-permute-done | bytes 98336 | tf_op jit(solution)/shard_map/ppermute | solution.py:27
  41.3 3.6 %collective-permute-done.15.refs_6_ = bf16[384,128]{1,0:T(8,128)(2,1)S(1)} collective-permute-done((bf16[384,128]{1,0:T(8,128)(2,1)S(1)}, bf16[384,128]{1,0:T(8,128)(2,1)S(1)}, u32[]{:S(2)}, u32[]{:S(2)}) %collective-permute-start.15) | collective-permute-done | bytes 98336 | tf_op jit(solution)/shard_map/ppermute | solution.py:27
  45.1 1.5 %collective-permute-start.11 = (bf16[256,128]{1,0:T(8,128)(2,1)S(1)}, bf16[256,128]{1,0:T(8,128)(2,1)S(1)}, u32[]{:S(2)}, u32[]{:S(2)}) collective-permute-start(bf16[256,128]{1,0:T(8,128)(2,1)S(1)} %get-tuple-element.32), channel_id=1, source_target_pairs={{0,2},{1,3},{2,0},{3,1},{4,6},{5,7},{6,4},{7,5},{8,10},{9,11},{10,... | collective-permute-start | bytes 196616 | tf_op jit(solution)/shard_map/ppermute | solution.py:27
  47.0 2.5 %collective-permute-start.13 = (bf16[256,128]{1,0:T(8,128)(2,1)S(1)}, bf16[256,128]{1,0:T(8,128)(2,1)S(1)}, u32[]{:S(2)}, u32[]{:S(2)}) collective-permute-start(bf16[256,128]{1,0:T(8,128)(2,1)S(1)} %get-tuple-element.30), channel_id=1, source_target_pairs={{0,6},{1,7},{2,4},{3,5},{4,2},{5,3},{6,0},{7,1},{8,14},{9,15},{10,... | collective-permute-start | bytes 196616 | tf_op jit(solution)/shard_map/ppermute | solution.py:27
  50.2 1.3 %collective-permute-start.21 = (bf16[128,128]{1,0:T(8,128)(2,1)S(1)}, bf16[128,128]{1,0:T(8,128)(2,1)S(1)}, u32[]{:S(2)}, u32[]{:S(2)}) collective-permute-start(bf16[128,128]{1,0:T(8,128)(2,1)S(1)} %add_convert_fusion.4), channel_id=1, source_target_pairs={{0,4},{1,5},{2,6},{3,7},{4,0},{5,1},{6,2},{7,3},{8,12},{9,13},{10,... | collective-permute-start | bytes 98312 | tf_op jit(solution)/shard_map/ppermute | solution.py:27
  51.5 2.5 %collective-permute-start.22 = (bf16[128,128]{1,0:T(8,128)(2,1)S(1)}, bf16[128,128]{1,0:T(8,128)(2,1)S(1)}, u32[]{:S(2)}, u32[]{:S(2)}) collective-permute-start(bf16[128,128]{1,0:T(8,128)(2,1)S(1)} %add_convert_fusion.4), channel_id=1, source_target_pairs={{0,6},{1,7},{2,4},{3,5},{4,2},{5,3},{6,0},{7,1},{8,14},{9,15},{10,... | collective-permute-start | bytes 98312 | tf_op jit(solution)/shard_map/ppermute | solution.py:27
  54.0 1.0 %collective-permute-done.12.refs_2_ = bf16[256,128]{1,0:T(8,128)(2,1)S(1)} collective-permute-done((bf16[256,128]{1,0:T(8,128)(2,1)S(1)}, bf16[256,128]{1,0:T(8,128)(2,1)S(1)}, u32[]{:S(2)}, u32[]{:S(2)}) %collective-permute-start.12) | collective-permute-done | bytes 65568 | tf_op jit(solution)/shard_map/ppermute | solution.py:27
  55.9 4.7 %collective-permute-start.18 = (bf16[16,128]{1,0:T(8,128)(2,1)S(1)}, bf16[16,128]{1,0:T(8,128)(2,1)S(1)}, u32[]{:S(2)}, u32[]{:S(2)}) collective-permute-start(bf16[16,128]{1,0:T(8,128)(2,1)S(1)} %get-tuple-element.29), channel_id=1, source_target_pairs={{1,2},{2,1},{3,4},{4,3},{5,6},{6,5},{7,8},{8,7},{9,10},{10,9},{11,... | collective-permute-start | bytes 12296 | tf_op jit(solution)/shard_map/ppermute | solution.py:35
  61.3 3.1 %collective-permute-done.18.far_ref = bf16[16,128]{1,0:T(8,128)(2,1)S(1)} collective-permute-done((bf16[16,128]{1,0:T(8,128)(2,1)S(1)}, bf16[16,128]{1,0:T(8,128)(2,1)S(1)}, u32[]{:S(2)}, u32[]{:S(2)}) %collective-permute-start.18) | collective-permute-done | bytes 4128 | tf_op jit(solution)/shard_map/ppermute | solution.py:35
  64.4 1.3 %shard_map.112 = bf16[256,128]{1,0:T(8,128)(2,1)} custom-call(s32[1,8]{1,0:T(1,128)S(1)} %copy-done.4, bf16[256,128]{1,0:T(8,128)(2,1)S(1)} %get-tuple-element.28.features_ref, bf16[16,128]{1,0:T(8,128)(2,1)S(1)} %collective-permute-done.17.near_ref, bf16[16,128]{1,0:T(8,128)(2,1)S(1)} %collective-permute-done.18.far_ref), custom_call_target="tpu_custom_call" | custom-call | tf_op jit(solution)/shard_map/pallas_call | solution.py:436
  (47 shorter events, 5.5 us)
Async XLA Ops:
  0.6 14.1 %collective-permute-start.1 = (bf16[256,128]{1,0:T(8,128)(2,1)}, bf16[256,128]{1,0:T(8,128)(2,1)S(1)}, u32[]{:S(2)}, u32[]{:S(2)}) collective-permute-start(bf16[256,128]{1,0:T(8,128)(2,1)} %features_ref.3), channel_id=1, source_target_pairs={{0,1},{1,0},{2,3},{3,2},{4,5},{5,4},{6,7},{7,6},{8,9},{9,8},{10,11... | collective-permute-start | bytes 196616 | tf_op jit(solution)/shard_map/ppermute | solution.py:27
  2.2 12.5 %copy-start.1 = (bf16[256,128]{1,0:T(8,128)(2,1)S(1)}, bf16[256,128]{1,0:T(8,128)(2,1)}, u32[]{:S(2)}) copy-start(bf16[256,128]{1,0:T(8,128)(2,1)} %features_ref.3) | copy-start | bytes 196612
  2.8 10.6 %collective-permute-start.2 = (bf16[16,128]{1,0:T(8,128)(2,1)S(1)}, bf16[16,128]{1,0:T(8,128)(2,1)S(1)}, u32[]{:S(2)}, u32[]{:S(2)}) collective-permute-start(bf16[16,128]{1,0:T(8,128)(2,1)S(1)} %shard_map.104), channel_id=1, source_target_pairs={{1,2},{2,1},{3,4},{4,3},{5,6},{6,5},{7,8},{8,7},{9,10},{10,9},{11,... | collective-permute-start | bytes 12296 | tf_op jit(solution)/shard_map/ppermute | solution.py:35
  13.3 1.4 %collective-permute-start.3 = (bf16[16,128]{1,0:T(8,128)(2,1)S(1)}, bf16[16,128]{1,0:T(8,128)(2,1)S(1)}, u32[]{:S(2)}, u32[]{:S(2)}) collective-permute-start(bf16[16,128]{1,0:T(8,128)(2,1)S(1)} %collective-permute-done.2.far_ref), channel_id=1, source_target_pairs={{0,1},{1,0},{2,3},{3,2},{4,5},{5,4},{6,7},{7,6},{8,9},{9,8},{10,11... | collective-permute-start | bytes 12296 | tf_op jit(solution)/shard_map/ppermute | solution.py:27
  13.4 1.3 %collective-permute-start = (s32[1,8]{1,0:T(1,128)S(1)}, s32[1,8]{1,0:T(1,128)S(1)}, u32[]{:S(2)}, u32[]{:S(2)}) collective-permute-start(s32[1,8]{1,0:T(1,128)S(1)} %copy-done.4), channel_id=1, source_target_pairs={{0,1},{1,0},{2,3},{3,2},{4,5},{5,4},{6,7},{7,6},{8,9},{9,8},{10,11... | collective-permute-start | bytes 104 | tf_op jit(solution)/shard_map/ppermute | solution.py:27
  15.6 6.5 %collective-permute-start.4 = (bf16[512,128]{1,0:T(8,128)(2,1)S(1)}, bf16[512,128]{1,0:T(8,128)(2,1)S(1)}, u32[]{:S(2)}, u32[]{:S(2)}) collective-permute-start(bf16[512,128]{1,0:T(8,128)(2,1)S(1)} %shard_map.106.refs_3_), channel_id=1, source_target_pairs={{0,2},{1,9},{2,0},{3,11},{4,6},{5,13},{6,4},{7,15},{8,10},{9,1},{1... | collective-permute-start | bytes 393224 | tf_op jit(solution)/shard_map/ppermute | solution.py:47
  15.7 6.4 %collective-permute-start.5 = (bf16[512,128]{1,0:T(8,128)(2,1)S(1)}, bf16[512,128]{1,0:T(8,128)(2,1)S(1)}, u32[]{:S(2)}, u32[]{:S(2)}) collective-permute-start(bf16[512,128]{1,0:T(8,128)(2,1)S(1)} %shard_map.106.refs_3_), channel_id=1, source_target_pairs={{0,4},{1,17},{2,6},{3,19},{4,0},{5,21},{6,2},{7,23},{8,12},{9,25},... | collective-permute-start | bytes 393224 | tf_op jit(solution)/shard_map/ppermute | solution.py:47
  17.1 7.4 %collective-permute-start.6 = (bf16[512,128]{1,0:T(8,128)(2,1)S(1)}, bf16[512,128]{1,0:T(8,128)(2,1)S(1)}, u32[]{:S(2)}, u32[]{:S(2)}) collective-permute-start(bf16[512,128]{1,0:T(8,128)(2,1)S(1)} %shard_map.106.refs_3_), channel_id=1, source_target_pairs={{0,6},{1,25},{2,4},{3,27},{4,2},{5,29},{6,0},{7,31},{8,14},{9,17},... | collective-permute-start | bytes 393224 | tf_op jit(solution)/shard_map/ppermute | solution.py:47
  24.5 2.9 %collective-permute-start.7 = (bf16[512,128]{1,0:T(8,128)(2,1)S(1)}, bf16[512,128]{1,0:T(8,128)(2,1)S(1)}, u32[]{:S(2)}, u32[]{:S(2)}) collective-permute-start(bf16[512,128]{1,0:T(8,128)(2,1)S(1)} %collective-permute-done.4.refs_4_), channel_id=1, source_target_pairs={{0,1},{1,0},{2,3},{3,2},{4,5},{5,4},{6,7},{7,6},{8,9},{9,8},{10,11... | collective-permute-start | bytes 393224 | tf_op jit(solution)/shard_map/ppermute | solution.py:27
  24.5 2.9 %collective-permute-start.8 = (bf16[512,128]{1,0:T(8,128)(2,1)S(1)}, bf16[512,128]{1,0:T(8,128)(2,1)S(1)}, u32[]{:S(2)}, u32[]{:S(2)}) collective-permute-start(bf16[512,128]{1,0:T(8,128)(2,1)S(1)} %collective-permute-done.5.refs_5_), channel_id=1, source_target_pairs={{0,1},{1,0},{2,3},{3,2},{4,5},{5,4},{6,7},{7,6},{8,9},{9,8},{10,11... | collective-permute-start | bytes 393224 | tf_op jit(solution)/shard_map/ppermute | solution.py:27
  25.0 2.4 %collective-permute-start.9 = (bf16[512,128]{1,0:T(8,128)(2,1)S(1)}, bf16[512,128]{1,0:T(8,128)(2,1)S(1)}, u32[]{:S(2)}, u32[]{:S(2)}) collective-permute-start(bf16[512,128]{1,0:T(8,128)(2,1)S(1)} %collective-permute-done.6.refs_6_), channel_id=1, source_target_pairs={{0,1},{1,0},{2,3},{3,2},{4,5},{5,4},{6,7},{7,6},{8,9},{9,8},{10,11... | collective-permute-start | bytes 393224 | tf_op jit(solution)/shard_map/ppermute | solution.py:27
  34.5 6.8 %collective-permute-start.14 = (bf16[384,128]{1,0:T(8,128)(2,1)S(1)}, bf16[384,128]{1,0:T(8,128)(2,1)S(1)}, u32[]{:S(2)}, u32[]{:S(2)}) collective-permute-start(bf16[384,128]{1,0:T(8,128)(2,1)S(1)} %get-tuple-element.25), channel_id=1, source_target_pairs={{0,8},{8,0},{16,24},{24,16},{1,9},{9,1},{17,25},{25,17},{2,10},{10... | collective-permute-start | bytes 294920 | tf_op jit(solution)/shard_map/ppermute | solution.py:27
  37.9 7.0 %collective-permute-start.15 = (bf16[384,128]{1,0:T(8,128)(2,1)S(1)}, bf16[384,128]{1,0:T(8,128)(2,1)S(1)}, u32[]{:S(2)}, u32[]{:S(2)}) collective-permute-start(bf16[384,128]{1,0:T(8,128)(2,1)S(1)} %get-tuple-element.26), channel_id=1, source_target_pairs={{0,16},{8,24},{16,0},{24,8},{1,17},{9,25},{17,1},{25,9},{2,18},{10... | collective-permute-start | bytes 294920 | tf_op jit(solution)/shard_map/ppermute | solution.py:27
  37.9 7.0 %collective-permute-start.16 = (bf16[384,128]{1,0:T(8,128)(2,1)S(1)}, bf16[384,128]{1,0:T(8,128)(2,1)S(1)}, u32[]{:S(2)}, u32[]{:S(2)}) collective-permute-start(bf16[384,128]{1,0:T(8,128)(2,1)S(1)} %get-tuple-element.27), channel_id=1, source_target_pairs={{0,24},{8,16},{16,8},{24,0},{1,25},{9,17},{17,9},{25,1},{2,26},{10... | collective-permute-start | bytes 294920 | tf_op jit(solution)/shard_map/ppermute | solution.py:27
  39.4 5.6 %collective-permute-start.10 = (bf16[1024,128]{1,0:T(8,128)(2,1)S(1)}, bf16[1024,128]{1,0:T(8,128)(2,1)S(1)}, u32[]{:S(2)}, u32[]{:S(2)}) collective-permute-start(bf16[1024,128]{1,0:T(8,128)(2,1)S(1)} %get-tuple-element.23), channel_id=1, source_target_pairs={{0,1},{1,0},{2,3},{3,2},{4,5},{5,4},{6,7},{7,6},{8,9},{9,8},{10,11... | collective-permute-start | bytes 786440 | tf_op jit(solution)/shard_map/ppermute | solution.py:27
  44.9 4.6 %collective-permute-start.19 = (f32[128,128]{1,0:T(8,128)S(1)}, f32[128,128]{1,0:T(8,128)S(1)}, u32[]{:S(2)}, u32[]{:S(2)}) collective-permute-start(f32[128,128]{1,0:T(8,128)S(1)} %add_add_fusion), channel_id=1, source_target_pairs={{0,1},{1,0},{2,3},{3,2},{4,5},{5,4},{6,7},{7,6},{8,9},{9,8},{10,11... | collective-permute-start | bytes 196616 | tf_op jit(solution)/shard_map/ppermute | solution.py:27
  45.1 6.4 %collective-permute-start.11 = (bf16[256,128]{1,0:T(8,128)(2,1)S(1)}, bf16[256,128]{1,0:T(8,128)(2,1)S(1)}, u32[]{:S(2)}, u32[]{:S(2)}) collective-permute-start(bf16[256,128]{1,0:T(8,128)(2,1)S(1)} %get-tuple-element.32), channel_id=1, source_target_pairs={{0,2},{1,3},{2,0},{3,1},{4,6},{5,7},{6,4},{7,5},{8,10},{9,11},{10,... | collective-permute-start | bytes 196616 | tf_op jit(solution)/shard_map/ppermute | solution.py:27
  46.6 8.5 %collective-permute-start.12 = (bf16[256,128]{1,0:T(8,128)(2,1)S(1)}, bf16[256,128]{1,0:T(8,128)(2,1)S(1)}, u32[]{:S(2)}, u32[]{:S(2)}) collective-permute-start(bf16[256,128]{1,0:T(8,128)(2,1)S(1)} %get-tuple-element.31), channel_id=1, source_target_pairs={{0,4},{1,5},{2,6},{3,7},{4,0},{5,1},{6,2},{7,3},{8,12},{9,13},{10,... | collective-permute-start | bytes 196616 | tf_op jit(solution)/shard_map/ppermute | solution.py:27
  47.0 8.0 %collective-permute-start.13 = (bf16[256,128]{1,0:T(8,128)(2,1)S(1)}, bf16[256,128]{1,0:T(8,128)(2,1)S(1)}, u32[]{:S(2)}, u32[]{:S(2)}) collective-permute-start(bf16[256,128]{1,0:T(8,128)(2,1)S(1)} %get-tuple-element.30), channel_id=1, source_target_pairs={{0,6},{1,7},{2,4},{3,5},{4,2},{5,3},{6,0},{7,1},{8,14},{9,15},{10,... | collective-permute-start | bytes 196616 | tf_op jit(solution)/shard_map/ppermute | solution.py:27
  49.6 11.0 %collective-permute-start.20 = (bf16[128,128]{1,0:T(8,128)(2,1)S(1)}, bf16[128,128]{1,0:T(8,128)(2,1)S(1)}, u32[]{:S(2)}, u32[]{:S(2)}) collective-permute-start(bf16[128,128]{1,0:T(8,128)(2,1)S(1)} %add_convert_fusion.4), channel_id=1, source_target_pairs={{0,2},{1,3},{2,0},{3,1},{4,6},{5,7},{6,4},{7,5},{8,10},{9,11},{10,... | collective-permute-start | bytes 98312 | tf_op jit(solution)/shard_map/ppermute | solution.py:27
  50.2 10.4 %collective-permute-start.21 = (bf16[128,128]{1,0:T(8,128)(2,1)S(1)}, bf16[128,128]{1,0:T(8,128)(2,1)S(1)}, u32[]{:S(2)}, u32[]{:S(2)}) collective-permute-start(bf16[128,128]{1,0:T(8,128)(2,1)S(1)} %add_convert_fusion.4), channel_id=1, source_target_pairs={{0,4},{1,5},{2,6},{3,7},{4,0},{5,1},{6,2},{7,3},{8,12},{9,13},{10,... | collective-permute-start | bytes 98312 | tf_op jit(solution)/shard_map/ppermute | solution.py:27
  51.5 9.1 %collective-permute-start.22 = (bf16[128,128]{1,0:T(8,128)(2,1)S(1)}, bf16[128,128]{1,0:T(8,128)(2,1)S(1)}, u32[]{:S(2)}, u32[]{:S(2)}) collective-permute-start(bf16[128,128]{1,0:T(8,128)(2,1)S(1)} %add_convert_fusion.4), channel_id=1, source_target_pairs={{0,6},{1,7},{2,4},{3,5},{4,2},{5,3},{6,0},{7,1},{8,14},{9,15},{10,... | collective-permute-start | bytes 98312 | tf_op jit(solution)/shard_map/ppermute | solution.py:27
  55.8 5.5 %collective-permute-start.17 = (bf16[16,128]{1,0:T(8,128)(2,1)S(1)}, bf16[16,128]{1,0:T(8,128)(2,1)S(1)}, u32[]{:S(2)}, u32[]{:S(2)}) collective-permute-start(bf16[16,128]{1,0:T(8,128)(2,1)S(1)} %get-tuple-element.29), channel_id=1, source_target_pairs={{0,1},{1,0},{2,3},{3,2},{4,5},{5,4},{6,7},{7,6},{8,9},{9,8},{10,11... | collective-permute-start | bytes 12296 | tf_op jit(solution)/shard_map/ppermute | solution.py:27
  55.9 8.5 %collective-permute-start.18 = (bf16[16,128]{1,0:T(8,128)(2,1)S(1)}, bf16[16,128]{1,0:T(8,128)(2,1)S(1)}, u32[]{:S(2)}, u32[]{:S(2)}) collective-permute-start(bf16[16,128]{1,0:T(8,128)(2,1)S(1)} %get-tuple-element.29), channel_id=1, source_target_pairs={{1,2},{2,1},{3,4},{4,3},{5,6},{6,5},{7,8},{8,7},{9,10},{10,9},{11,... | collective-permute-start | bytes 12296 | tf_op jit(solution)/shard_map/ppermute | solution.py:35
  (4 other events, 14.8 us)

commit v3 on v2

v3 whole, which is shorter than its diff:
```python
import functools

import jax
import jax.numpy as jnp
from jax import lax
from jax.experimental import pallas as pl
from jax.experimental.pallas import tpu as pltpu
from jax.sharding import PartitionSpec as P

BLOCK = 128
AXES = ("row", "col")
INV5 = -858993459
VMEM = pl.BlockSpec(memory_space=pltpu.VMEM)
SMEM = pl.BlockSpec(memory_space=pltpu.SMEM)
CHUNK_CELLS = 128
BOUNDS = (0, 11, 52, 64)


def params(mib):
    return pltpu.CompilerParams(vmem_limit_bytes=mib * 2**20)


def swap(x, axis, step):
    count = lax.axis_size(axis)
    return lax.ppermute(x, axis, [(i, i ^ step) for i in range(count)])


def swap_next(x):
    count = lax.axis_size("row") * lax.axis_size("col")
    pairs = [(0, 0), (count - 1, count - 1)]
    for s in range(1, count - 1, 2):
        pairs += [(s, s + 1), (s + 1, s)]
    return lax.ppermute(x, AXES, pairs)


def inner(axis_end):
    chips = lax.axis_size("row") * lax.axis_size("col") // 2
    chip = (lax.axis_index("row") * lax.axis_size("col") + lax.axis_index("col")) // 2
    return jnp.where(chip == (chips - 1 if axis_end else 0), 0.0, 1.0).astype(jnp.float32)


def swap_mixed(x, step):
    nrow, ncol = lax.axis_size("row"), lax.axis_size("col")
    pairs = []
    for r in range(nrow):
        for c in range(ncol):
            if c % 2 == 0 and step < ncol // 2:
                pairs.append((r * ncol + c, r * ncol + (c ^ (2 * step))))
            if c % 2 == 1 and step < nrow:
                pairs.append((r * ncol + c, (r ^ step) * ncol + c))
    return lax.ppermute(x, AXES, pairs)


def edges(values, link, out_ref):
    rows, width = values.shape
    head = link[0:8] * values[0:8]
    tail = values[rows - 8 : rows]
    out_ref[...] = jnp.concatenate([head, tail], axis=0).astype(out_ref.dtype)


def stencil(values, link, prev, nxt):
    rows, width = values.shape
    node = lax.broadcasted_iota(jnp.int32, (rows, width), 0)
    before = jnp.where(node == 0, prev, pltpu.roll(values, 1, 0))
    after = jnp.where(node == rows - 1, nxt, pltpu.roll(link * values, rows - 1, 0))
    return 0.5 * values + 0.25 * (link * before + after)


def parity(even, odd):
    side = lax.rem(lax.axis_index("col"), 2)
    pl.when(side == 0)(even)
    pl.when(side == 1)(odd)


def body_kernel(at, features_hbm, rows, cols, keys, nrows, ncols, cuts_hbm, count_s, *refs):
    body_ref, ends_ref, meta_ref, cuts_s, sems = refs
    shard, width = features_hbm.shape
    pairs = [(cuts_hbm, cuts_s), (features_hbm, body_ref.at[pl.ds(0, shard), :])]
    for source, spot in (
        (rows, at.rows), (cols, at.cols), (keys, at.keys), (nrows, at.nrows), (ncols, at.ncols),
    ):
        pairs.append((source.at[0], meta_ref.at[:, pl.ds(spot, source.shape[2])]))
    copies = [pltpu.make_async_copy(a, b, sems.at[t]) for t, (a, b) in enumerate(pairs)]
    for copy in copies:
        copy.start()
    meta_ref[:, at.count :] = jnp.full((1, meta_ref.shape[1] - at.count), count_s[0, 0], jnp.int32)
    node = lax.broadcasted_iota(jnp.int32, (shard, width), 0)
    copies[0].wait()
    cut = node == cuts_s[0, 0]
    for t in range(1, cuts_s.shape[1]):
        cut = jnp.logical_or(cut, node == cuts_s[0, t])
    link = jnp.where(cut, 0.0, 1.0).astype(jnp.float32)
    body_ref[shard:, :] = link.astype(body_ref.dtype)
    for copy in copies[1:]:
        copy.wait()
    edges(body_ref[0:shard, :].astype(jnp.float32), link, ends_ref)


def bodies(at, features, slots, cuts, count):
    shard, width = features.shape
    pinned = [pltpu.with_memory_space_constraint(x, pltpu.HBM) for x in (features, *slots, cuts)]
    hbm = pl.BlockSpec(memory_space=pltpu.HBM)
    return pl.pallas_call(
        functools.partial(body_kernel, at),
        out_shape=(
            jax.ShapeDtypeStruct((2 * shard, width), features.dtype),
            jax.ShapeDtypeStruct((16, width), features.dtype),
            jax.ShapeDtypeStruct((1, at.end), jnp.int32),
        ),
        in_specs=[hbm] * len(pinned) + [SMEM],
        out_specs=(VMEM, VMEM, VMEM),
        scratch_shapes=[
            pltpu.SMEM(cuts.shape, jnp.int32),
            pltpu.SemaphoreType.DMA((len(pinned),)),
        ],
        compiler_params=params(4),
    )(*pinned, count)


def pair_kernel(body_ref, sib_ref, far_ref, sib_far_ref, out_ref):
    shard = body_ref.shape[0] // 2

    def both(first_ref, second_ref, before_ref, after_ref):
        first = first_ref[0:shard, :].astype(jnp.float32)
        second = second_ref[0:shard, :].astype(jnp.float32)
        first_link = first_ref[shard:, :].astype(jnp.float32)
        second_link = second_ref[shard:, :].astype(jnp.float32)
        prev = before_ref[...].astype(jnp.float32)[15:16] * inner(False)
        nxt = after_ref[...].astype(jnp.float32)[0:1] * inner(True)
        head = second_link[0:1] * second[0:1]
        tail = first[shard - 1 : shard]
        out_ref[0:shard, :] = stencil(first, first_link, prev, head).astype(out_ref.dtype)
        out_ref[shard:, :] = stencil(second, second_link, tail, nxt).astype(out_ref.dtype)

    parity(
        lambda: both(body_ref, sib_ref, far_ref, sib_far_ref),
        lambda: both(sib_ref, body_ref, sib_far_ref, far_ref),
    )


class Slots:
    def __init__(self, slots, negatives):
        self.slots, self.negatives = slots, negatives
        self.rows, self.cols, self.keys = 0, slots, 2 * slots
        self.nrows = 3 * slots
        self.ncols = self.nrows + negatives
        self.count = self.ncols + negatives
        self.end = self.count + BLOCK


def count_kernel(at, base, blocks, cols, per, meta_ref, n_ref):
    here_rows = per * 2 * (lax.axis_index("col") // 2)
    here_cols = per * lax.axis_index("row")
    width = cols * BLOCK
    total = jnp.zeros((blocks, width), jnp.float32)
    count = meta_ref[0:1, at.count : at.count + 1]
    for rows_at, cols_at, slots, positive in (
        (at.rows, at.cols, at.slots, True),
        (at.nrows, at.ncols, at.negatives, False),
    ):
        rows = jnp.bitwise_xor(meta_ref[0:1, rows_at : rows_at + slots], here_rows) - base
        cols_of = jnp.bitwise_xor(meta_ref[0:1, cols_at : cols_at + slots], here_cols)
        hit = lax.broadcasted_iota(jnp.int32, (blocks, slots), 0) == rows
        if positive:
            live = lax.broadcasted_iota(jnp.int32, (blocks, slots), 1) < count
            hit = jnp.logical_and(hit, live)
        lane = lax.shift_right_logical(lax.broadcasted_iota(jnp.int32, (width, slots), 0), 7)
        spread = jnp.where(lane == cols_of, 1.0, 0.0).astype(jnp.bfloat16)
        total += lax.dot_general(
            jnp.where(hit, 0.5, 0.0).astype(jnp.bfloat16), spread,
            (((1,), (1,)), ((), ())), preferred_element_type=jnp.float32,
        )
    n_ref[...] = total


def counts(at, base, blocks, cols, per, meta):
    return pl.pallas_call(
        functools.partial(count_kernel, at, base, blocks, cols, per),
        out_shape=jax.ShapeDtypeStruct((blocks, cols * BLOCK), jnp.float32),
        in_specs=[VMEM],
        out_specs=VMEM,
        compiler_params=params(8),
    )(meta)


def target_kernel(at, base, blocks, cols, per, part, bounds, filtered, meta_s, *refs):
    t_ref, step_ref = refs[-2:]
    a = lax.broadcasted_iota(jnp.int32, (BLOCK, BLOCK), 0)
    b = lax.broadcasted_iota(jnp.int32, (BLOCK, BLOCK), 1)
    step_ref[...] = (a * BLOCK + b) * jnp.int32(4 * 40503)
    if part == 0:

        def clear(i, _):
            row = pl.multiple_of(i * BLOCK, BLOCK)
            t_ref[pl.ds(row, BLOCK), :] = jnp.zeros((BLOCK, cols * BLOCK), jnp.float32)
            return 0

        lax.fori_loop(0, blocks, clear, 0)
    here_rows = per * 2 * (lax.axis_index("col") // 2)
    here_cols = per * lax.axis_index("row")
    count = meta_s[0, at.count]
    unroll = 8 if at.slots % 8 == 0 else 1

    def positive(s):
        i = jnp.bitwise_xor(meta_s[0, at.rows + s], here_rows) - base
        j = jnp.bitwise_xor(meta_s[0, at.cols + s], here_cols)
        key = meta_s[0, at.keys + s] * 4
        one = jnp.where(s < count, 1.0, 0.0).astype(jnp.float32)

        def add():
            row = pl.multiple_of(i * BLOCK, BLOCK)
            col = pl.multiple_of(j * BLOCK, BLOCK)
            mixed = step_ref[...] + key
            mixed = jnp.bitwise_xor(mixed, lax.shift_right_logical(mixed, 11))
            fifth = lax.shift_right_logical(mixed, 9) * jnp.int32(INV5)
            hit = fifth.astype(jnp.uint32) < jnp.uint32(2**21)
            t_ref[pl.ds(row, BLOCK), pl.ds(col, BLOCK)] += jnp.where(hit, one, 0.0)

        if filtered:
            pl.when(jnp.logical_and(i >= 0, i < blocks))(add)
        else:
            add()

    def positives(g, _):
        for u in range(unroll):
            positive(g * unroll + u)
        return 0

    trips = (count + unroll - 1) // unroll
    first, last = bounds[part], bounds[part + 1]
    lax.fori_loop(trips * first // 64, trips * last // 64, positives, 0)


def targets(at, base, blocks, cols, per, part, bounds, filtered, meta, before):
    shape = (blocks * BLOCK, cols * BLOCK)
    old = [] if before is None else [before]
    return pl.pallas_call(
        functools.partial(target_kernel, at, base, blocks, cols, per, part, bounds, filtered),
        out_shape=jax.ShapeDtypeStruct(shape, jnp.float32),
        in_specs=[SMEM] + [VMEM] * len(old),
        out_specs=VMEM,
        input_output_aliases={1: 0} if old else {},
        scratch_shapes=[pltpu.VMEM((BLOCK, BLOCK), jnp.int32)],
        compiler_params=params(10),
        cost_estimate=pl.CostEstimate(
            flops=at.slots * BLOCK * BLOCK * 4,
            bytes_accessed=at.slots * BLOCK * BLOCK * 4,
            transcendentals=0,
        ),
    )(meta, *old)


def decode_kernel(nz, nrow, first, count, refs):
    steps = max(nz, nrow) - 1
    t_ref, n_ref, weight_ref, pair_ref = refs[:4]
    recv = refs[4 : 4 + steps]
    other = refs[4 + steps : 4 + 2 * steps]
    refs = refs[4 + 2 * steps :]
    drow_ref, give_ref, grad_ref, row_agg, col_agg, row_z = refs[:6]
    (col_z,) = refs[6:]
    pair = pair_ref.shape[0]
    shard = pair // 2
    columns = nrow * shard
    bf16 = jnp.bfloat16

    def gather(z_refs, row_refs, side):
        for k in range(count):
            ref = pair_ref if first + k == 0 else z_refs[first + k - 1]
            row_agg[k * pair : (k + 1) * pair, :] = ref[...]
        for q in range(nrow):
            ref = pair_ref if q == 0 else row_refs[q - 1]
            col_agg[q * shard : (q + 1) * shard, :] = ref[side * shard : (side + 1) * shard, :]

    parity(lambda: gather(recv, other, 0), lambda: gather(other, recv, 1))
    weight = weight_ref[...]
    dots = functools.partial(lax.dot_general, preferred_element_type=jnp.float32)
    nn = (((1,), (0,)), ((), ()))
    nt = (((1,), (1,)), ((), ()))
    tn = (((0,), (0,)), ((), ()))
    col_z[...] = dots(col_agg[...], weight, nn).astype(bf16)
    for k in range(count):
        at = slice(k * pair, (k + 1) * pair)
        row_z[at, :] = dots(row_agg[at, :], weight, nn).astype(bf16)
        half = row_z[at, :] * bf16(0.5)
        for c in range(0, columns, pair):
            cut = slice(c, min(c + pair, columns))
            curve = jnp.tanh(dots(half, col_z[cut, :], nt))
            for i in range(pair // BLOCK):
                row = k * pair + i * BLOCK
                n = n_ref[row // BLOCK : row // BLOCK + 1, cut]
                tile = t_ref[row : row + BLOCK, cut]
                part = n * curve[i * BLOCK : (i + 1) * BLOCK] + (n - tile)
                grad_ref[row : row + BLOCK, cut] = part.astype(bf16)
        drow = dots(grad_ref[at, :], col_z[...], nn) * (1.0 / 32.0)
        drow_ref[at, :] = drow
        give_ref[at, :] = drow.astype(bf16)


def column_kernel(grad_ref, row_agg, col_agg, row_z, drow_ref, dcol_ref, give_ref, share_ref):
    dots = functools.partial(lax.dot_general, preferred_element_type=jnp.float32)
    nn = (((1,), (0,)), ((), ()))
    tn = (((0,), (0,)), ((), ()))
    bf16 = jnp.bfloat16
    columns = dcol_ref.shape[0]
    row_t = row_z[...].T
    step = min(columns, 4 * BLOCK)
    for c in range(0, columns, step):
        cut = slice(c, c + step)
        dcol = dots(row_t, grad_ref[:, cut], nn).T * (1.0 / 32.0)
        dcol_ref[cut, :] = dcol
        give_ref[cut, :] = dcol.astype(bf16)
    share = dots(row_agg[...], drow_ref[...].astype(bf16), tn)
    share += dots(col_agg[...], give_ref[0:columns, :], tn)
    share_ref[...] = share
    give_ref[columns:, :] = share.astype(bf16)


def decode(t, n, weight, pair, recv, other, nz, nrow, first, count):
    rows, columns = t.shape
    width = weight.shape[1]
    bf16, real = jnp.bfloat16, jnp.float32
    shape = jax.ShapeDtypeStruct
    outs = [
        shape((rows, width), real),
        shape((rows, width), bf16),
        shape((rows, columns), bf16),
        shape((rows, width), bf16),
        shape((columns, width), bf16),
        shape((rows, width), bf16),
    ]
    drow, give_rows, grad, row_agg, col_agg, row_z = pl.pallas_call(
        lambda *refs: decode_kernel(nz, nrow, first, count, refs),
        out_shape=outs,
        in_specs=[VMEM] * (4 + len(recv) + len(other)),
        out_specs=[VMEM] * len(outs),
        scratch_shapes=[pltpu.VMEM((columns, width), bf16)],
        compiler_params=params(12),
        cost_estimate=pl.CostEstimate(
            flops=4 * rows * columns * width,
            bytes_accessed=rows * columns * 4,
            transcendentals=rows * columns,
        ),
    )(t, n, weight, pair, *recv, *other)
    dcol, give_columns, share = call(
        column_kernel,
        (
            shape((columns, width), real),
            shape((columns + weight.shape[0], width), bf16),
            shape(weight.shape, real),
        ),
        (grad, row_agg, col_agg, row_z, drow), 10,
    )
    return drow, give_rows, dcol, give_columns, share


def merge_kernel(nz, nrow, drow_ref, dcol_ref, share_ref, rows_ref, columns_ref, *messages):
    messages, chip_ref = messages[:-1], messages[-1]
    width = share_ref.shape[0]
    pair = messages[0].shape[0]
    shard = pair // 2
    bf16 = jnp.bfloat16

    def rows():
        for k in range(nz):
            at = slice(k * pair, (k + 1) * pair)
            total = drow_ref[at, :] + rows_ref[at, :].astype(jnp.float32)
            messages[k][...] = total.astype(bf16)

    def columns():
        for q in range(nrow):
            at = slice(q * shard, (q + 1) * shard)
            messages[q][0:shard, :] = columns_ref[at, :]
            messages[q][shard:pair, :] = dcol_ref[at, :].astype(bf16)

    parity(rows, columns)
    share = columns_ref[columns_ref.shape[0] - width :, :].astype(jnp.float32)
    chip_ref[...] = (share_ref[...].astype(bf16).astype(jnp.float32) + share).astype(bf16)


def tree_sum(parts):
    parts = [x.astype(jnp.float32) for x in parts]
    while len(parts) > 1:
        parts = [a + b for a, b in zip(parts[::2], parts[1::2])]
    return parts[0]


def sum_kernel(*refs):
    refs[-1][...] = tree_sum([x[...] for x in refs[:-1]]).astype(refs[-1].dtype)


def latent_kernel(mine_ref, theirs_ref, weight_ref, body_ref, dagg_ref, ends_ref):
    shard = mine_ref.shape[0] // 2
    dlatent = (mine_ref[...] + theirs_ref[...]).astype(jnp.bfloat16)
    dagg = lax.dot_general(
        dlatent, weight_ref[...], (((1,), (1,)), ((), ())), preferred_element_type=jnp.float32
    ).astype(jnp.bfloat16)
    dagg_ref[...] = dagg
    link = body_ref[shard:, :].astype(jnp.float32)

    def side(which):
        values = dagg[which * shard : (which + 1) * shard].astype(jnp.float32)
        edges(values, link, ends_ref)

    parity(lambda: side(0), lambda: side(1))


def final_kernel(scale, dagg_ref, body_ref, sib_ref, far_ref, *refs):
    shares, (features_ref, weight_ref) = refs[:-2], refs[-2:]
    shard = features_ref.shape[0]
    link = body_ref[shard:, :].astype(jnp.float32)

    def even():
        values = dagg_ref[0:shard, :].astype(jnp.float32)
        prev = far_ref[...].astype(jnp.float32)[15:16] * inner(False)
        nxt = sib_ref[shard : shard + 8, :].astype(jnp.float32)[0:1]
        nxt = nxt * dagg_ref[shard : shard + 8, :].astype(jnp.float32)[0:1]
        features_ref[...] = stencil(values, link, prev, nxt).astype(features_ref.dtype)

    def odd():
        values = dagg_ref[shard:, :].astype(jnp.float32)
        prev = dagg_ref[shard - 8 : shard, :].astype(jnp.float32)[7:8]
        nxt = far_ref[...].astype(jnp.float32)[0:1] * inner(True)
        features_ref[...] = stencil(values, link, prev, nxt).astype(features_ref.dtype)

    parity(even, odd)
    weight_ref[...] = tree_sum([x[...] for x in shares]) * scale


def call(kernel, outs, operands, mib, specs=None):
    return pl.pallas_call(
        kernel,
        out_shape=outs,
        in_specs=specs or [VMEM] * len(operands),
        out_specs=jax.tree.map(lambda _: VMEM, outs),
        compiler_params=params(mib),
    )(*operands)


def local(features, weight, cuts, pos_rows, pos_cols, pos_keys, pos_count, neg_rows, neg_cols):
    shard, width = features.shape
    ncol = lax.axis_size("col")
    nrow = lax.axis_size("row")
    nz = ncol // 2
    per = shard // BLOCK
    steps = max(nz, nrow)
    bf16, real = jnp.bfloat16, jnp.float32
    shape = jax.ShapeDtypeStruct
    message = shape((16, width), bf16)

    at = Slots(pos_rows.shape[2], neg_rows.shape[2])
    slots = (pos_rows, pos_cols, pos_keys, neg_rows, neg_cols)
    body, ends, meta = bodies(at, features, slots, cuts, pos_count)
    far = swap_next(ends)
    sib = swap(body, "col", 1)
    cols = nrow * per
    pieces = max(1, ncol * per * cols // CHUNK_CELLS)
    blocks = ncol * per // pieces
    bounds = BOUNDS if pieces == 1 else (0, 64)
    found = [
        targets(at, k * blocks, blocks, cols, per, 0, bounds, pieces > 1, meta, None)
        for k in range(pieces)
    ]
    number = [counts(at, k * blocks, blocks, cols, per, meta) for k in range(pieces)]
    if pieces == 1:
        far, found, number = lax.optimization_barrier((far, found, number))
    sib_far = swap(far, "col", 1)
    pair = call(pair_kernel, shape((2 * shard, width), bf16), (body, sib, far, sib_far), 4)
    recv = [swap_mixed(pair, k) for k in range(steps - 1, 0, -1)][::-1]
    if pieces == 1:
        t = targets(at, 0, blocks, cols, per, 1, bounds, False, meta, found[0])
        recv, t = lax.optimization_barrier((recv, t))
        other = [swap(x, "col", 1) for x in recv]
        found = [targets(at, 0, blocks, cols, per, 2, bounds, False, meta, t)]
    else:
        other = [swap(x, "col", 1) for x in recv]
    count = nz // pieces
    outs = [
        decode(t, n, weight, pair, recv, other, nz, nrow, k * count, count)
        for k, (t, n) in enumerate(zip(found, number))
    ]
    if pieces == 1:
        drow, give_rows, dcol, give_columns, share = outs[0]
    else:
        drow = jnp.concatenate([x[0] for x in outs], axis=0)
        give_rows = jnp.concatenate([x[1] for x in outs], axis=0)
        dcol, share = (tree_sum([x[k] for x in outs]) for k in (2, 4))
        give_columns = jnp.concatenate([dcol, share], axis=0).astype(bf16)
    got_rows, got_columns = swap(give_rows, "col", 1), swap(give_columns, "col", 1)
    *messages, share = call(
        functools.partial(merge_kernel, nz, nrow),
        [shape((2 * shard, width), bf16)] * steps + [shape(weight.shape, bf16)],
        (drow, dcol, share, got_rows, got_columns), 8,
    )
    arrived = [swap_mixed(messages[k], k) for k in range(steps - 1, 0, -1)]
    arrived = [messages[0]] + arrived[::-1]
    shares = [share] + [swap(share, "row", k) for k in range(1, nrow)]
    share = call(sum_kernel, shape(weight.shape, bf16), shares, 4)
    if pieces == 1:
        arrived, share = lax.optimization_barrier((arrived, share))
    shares = [share] + [swap(share, "col", 2 * k) for k in range(1, nz)]
    mine = call(sum_kernel, shape((2 * shard, width), real), arrived, 8)
    theirs = swap(mine, "col", 1)
    dagg, dends = call(
        latent_kernel, (shape((2 * shard, width), bf16), message),
        (mine, theirs, weight, body), 8,
    )
    dfar = swap_next(dends)
    scale = (shard * ncol * nrow) ** (-0.5)
    return call(
        functools.partial(final_kernel, scale),
        (shape(features.shape, bf16), shape(weight.shape, real)),
        (dagg, body, sib, dfar, *shares), 8,
    )


def solution(mesh):
    placed = (
        P(AXES, None),
        P(),
        P(AXES, None),
        P("row", "col", None),
        P("row", "col", None),
        P("row", "col", None),
        P("row", "col"),
        P("row", "col", None),
        P("row", "col", None),
    )
    return jax.shard_map(
        local, mesh=mesh, in_specs=placed, out_specs=(P(AXES, None), P()), check_vma=False
    )
```

time: 65.3 us -> 58.7 us (0.90); the launches traced: 65.7 us -> 58.3 us
  Pallas kernels: 17.5 us -> 14 us
  starting transfers between devices: 30.7 us -> 27.5 us
  waiting for transfers between devices: 12.9 us -> 15.3 us
  local copies, waits for them, and re-layouts: 2.33 us -> 0.01 us
  other arithmetic: 0.74 us -> 0 us
    ppermute x18 -> x14, starting transfers between devices: 15.1 us -> 7.38 us  [swap(): return lax.ppermute(x, axis, [(i, i ^ step) for i in range(count)])]
    ppermute x3 -> x6, starting transfers between devices: 4.44 us -> 8.9 us  [swap_mixed(): return lax.ppermute(x, AXES, pairs)]
    pallas_call x1, Pallas kernels: 7.06 us -> 3 us  [decode(): pl.pallas_call(lambda *refs: decode_kernel(nz, nrow, first, count, refs),...]
    ppermute x18 -> x14, waiting for transfers between devices: 7.36 us -> 10.1 us  [swap(): return lax.ppermute(x, axis, [(i, i ^ step) for i in range(count)])]
    unnamed x10 -> x2, local copies, waits for them, and re-layouts: 1.5 us -> 0.01 us
    ppermute x3 -> x6, waiting for transfers between devices: 2.42 us -> 1.48 us  [swap_mixed(): return lax.ppermute(x, AXES, pairs)]
    concatenate x1 -> x0, local copies, waits for them, and re-layouts: 0.83 us -> none  [local(): jnp.concatenate(slots + [jnp.zeros((1, -at.end % BLOCK), jnp.int32)], axi...]
    pallas_call x3, Pallas kernels: 6.62 us -> 7.3 us  [targets(): pl.pallas_call(functools.partial(target_kernel, at, base, blocks, cols, p...]
  transfers between devices with their start and end apart: 23 -> 22, of which waited for: 6 -> 7; matrix products, arithmetic and copies ran while one was open for 2% -> 0% of each run, Pallas kernels for 13% -> 16%
where the time goes in v3:
time: 58.7 us; the launch traced here: 58.3 us
  starting transfers between devices  27.5 us (47%)
  waiting for transfers between devices  15.3 us (26%)
  Pallas kernels  14 us (24%)
  between operations  1.51 us (3%)
    ppermute x2, starting transfers between devices, swap_next(): return lax.ppermute(x, AXES, pairs)  11.2 us
    ppermute x14, waiting for transfers between devices, swap(): return lax.ppermute(x, axis, [(i, i ^ step) for i in range(count)])  10.1 us
    ppermute x6, starting transfers between devices, swap_mixed(): return lax.ppermute(x, AXES, pairs)  8.9 us
    ppermute x14, starting transfers between devices, swap(): return lax.ppermute(x, axis, [(i, i ^ step) for i in range(count)])  7.38 us
    pallas_call x3, Pallas kernels, targets(): pl.pallas_call(functools.partial(target_kernel, at, base, blocks, cols, p...  7.3 us
    ppermute x2, waiting for transfers between devices, swap_next(): return lax.ppermute(x, AXES, pairs)  3.76 us
    pallas_call x1, Pallas kernels, decode(): pl.pallas_call(lambda *refs: decode_kernel(nz, nrow, first, count, refs),...  3 us
    pallas_call x7, Pallas kernels, call(): pl.pallas_call(kernel, out_shape=outs, in_specs=specs or [VMEM] * len(ope...  2.39 us
  transfers between devices with their start and end apart: 22, of which 7 were waited for; matrix products, arithmetic and copies ran while one was open for 0% of the time, Pallas kernels for 16%

profile of v3, /device:TPU:4, one launch (start us, length us, event | category | flops | bytes accessed | tf_op | source)
XLA Modules:
  0.0 58.3 jit_solution(12785936901560763939)
XLA Ops:
  1.3 0.9 %shard_map.104 = (bf16[512,128]{1,0:T(8,128)(2,1)S(1)}, bf16[16,128]{1,0:T(8,128)(2,1)S(1)}, s32[1,1536]{1,0:T(1,128)S(1)}) custom-call(bf16[256,128]{1,0:T(8,128)(2,1)} %features_hbm.1, s32[1,1,384]{2,1,0:T(1,128)} %rows.1, s32[1,1,384]{2,1,0:T(1,128)} %cols.1, s32[1,1,384]{2,1,0:T(1,128)} %keys.1, s32[1,1,128]{2,1,0:T(1,128)} %nrows.1, ...), custom_call_target="tpu_custom_call" | custom-call | tf_op jit(solution)/shard_map/pallas_call | solution.py:103
  2.3 6.5 %collective-permute-start.1 = (bf16[16,128]{1,0:T(8,128)(2,1)S(1)}, bf16[16,128]{1,0:T(8,128)(2,1)S(1)}, u32[]{:S(2)}, u32[]{:S(2)}) collective-permute-start(bf16[16,128]{1,0:T(8,128)(2,1)S(1)} %get-tuple-element.35), channel_id=1, source_target_pairs={{0,0},{31,31},{1,2},{2,1},{3,4},{4,3},{5,6},{6,5},{7,8},{8,7},{9,1... | collective-permute-start | bytes 12296 | tf_op jit(solution)/shard_map/ppermute | solution.py:33
  9.1 1.9 %shard_map.105.refs_0_ = f32[2048,1024]{1,0:T(8,128)S(1)} custom-call(s32[1,1536]{1,0:T(1,128)S(1)} %get-tuple-element.33.meta_s.meta_ref), custom_call_target="tpu_custom_call" | custom-call | flops 25165824 | bytes 25165824 | tf_op jit(solution)/shard_map/pallas_call | solution.py:237
  11.2 1.2 %collective-permute-done.2.sib_far_ref = bf16[16,128]{1,0:T(8,128)(2,1)S(1)} collective-permute-done((bf16[16,128]{1,0:T(8,128)(2,1)S(1)}, bf16[16,128]{1,0:T(8,128)(2,1)S(1)}, u32[]{:S(2)}, u32[]{:S(2)}) %collective-permute-start.2) | collective-permute-done | bytes 4128 | tf_op jit(solution)/shard_map/ppermute | solution.py:25
  12.5 2.6 %collective-permute-start.5 = (bf16[512,128]{1,0:T(8,128)(2,1)S(1)}, bf16[512,128]{1,0:T(8,128)(2,1)S(1)}, u32[]{:S(2)}, u32[]{:S(2)}) collective-permute-start(bf16[512,128]{1,0:T(8,128)(2,1)S(1)} %shard_map.107.refs_3_), channel_id=1, source_target_pairs={{0,6},{1,25},{2,4},{3,27},{4,2},{5,29},{6,0},{7,31},{8,14},{9,17},... | collective-permute-start | bytes 393224 | tf_op jit(solution)/shard_map/ppermute | solution.py:51
  15.0 1.9 %collective-permute-start.3 = (bf16[512,128]{1,0:T(8,128)(2,1)S(1)}, bf16[512,128]{1,0:T(8,128)(2,1)S(1)}, u32[]{:S(2)}, u32[]{:S(2)}) collective-permute-start(bf16[512,128]{1,0:T(8,128)(2,1)S(1)} %shard_map.107.refs_3_), channel_id=1, source_target_pairs={{0,2},{1,9},{2,0},{3,11},{4,6},{5,13},{6,4},{7,15},{8,10},{9,1},{1... | collective-permute-start | bytes 393224 | tf_op jit(solution)/shard_map/ppermute | solution.py:51
  16.9 3.7 %shard_map.108.refs_0_ = f32[2048,1024]{1,0:T(8,128)S(1)} custom-call(s32[1,1536]{1,0:T(1,128)S(1)} %get-tuple-element.33.meta_s.meta_ref, f32[2048,1024]{1,0:T(8,128)S(1)} %shard_map.105.refs_0_), custom_call_target="tpu_custom_call", output_to_operand_aliasing={{}: (1, {})} | custom-call | flops 25165824 | bytes 25165824 | tf_op jit(solution)/shard_map/pallas_call | solution.py:237
  20.6 1.5 %collective-permute-done.4.refs_5_ = bf16[512,128]{1,0:T(8,128)(2,1)S(1)} collective-permute-done((bf16[512,128]{1,0:T(8,128)(2,1)S(1)}, bf16[512,128]{1,0:T(8,128)(2,1)S(1)}, u32[]{:S(2)}, u32[]{:S(2)}) %collective-permute-start.4) | collective-permute-done | bytes 131104 | tf_op jit(solution)/shard_map/ppermute | solution.py:51
  22.6 1.7 %shard_map.109.refs_0_ = f32[2048,1024]{1,0:T(8,128)S(1)} custom-call(s32[1,1536]{1,0:T(1,128)S(1)} %get-tuple-element.33.meta_s.meta_ref, f32[2048,1024]{1,0:T(8,128)S(1)} %shard_map.108.refs_0_), custom_call_target="tpu_custom_call", output_to_operand_aliasing={{}: (1, {})} | custom-call | flops 25165824 | bytes 25165824 | tf_op jit(solution)/shard_map/pallas_call | solution.py:237
  24.3 3.0 %shard_map.110 = (f32[2048,128]{1,0:T(8,128)S(1)}, bf16[2048,128]{1,0:T(8,128)(2,1)S(1)}, bf16[2048,1024]{1,0:T(8,128)(2,1)S(1)}, bf16[2048,128]{1,0:T(8,128)(2,...) custom-call(f32[2048,1024]{1,0:T(8,128)S(1)} %shard_map.109.refs_0_, ...), custom_call_target="tpu_custom_call" | custom-call | flops 1073741824 | bytes 8388608 | tf_op jit(solution)/shard_map/pallas_call | solution.py:331
  27.3 0.7 %collective-permute-start.9 = (bf16[2048,128]{1,0:T(8,128)(2,1)S(1)}, bf16[2048,128]{1,0:T(8,128)(2,1)S(1)}, u32[]{:S(2)}, u32[]{:S(2)}) collective-permute-start(bf16[2048,128]{1,0:T(8,128)(2,1)S(1)} %get-tuple-element.50), channel_id=1, source_target_pairs={{0,1},{1,0},{2,3},{3,2},{4,5},{5,4},{6,7},{7,6},{8,9},{9,8},{10,11... | collective-permute-start | bytes 1572872 | tf_op jit(solution)/shard_map/ppermute | solution.py:25
  28.1 1.2 %shard_map.111 = (f32[1024,128]{1,0:T(8,128)S(1)}, bf16[1152,128]{1,0:T(8,128)(2,1)S(1)}, f32[128,128]{1,0:T(8,128)S(1)}) custom-call(bf16[2048,1024]{1,0:T(8,128)(2,1)S(1)} %get-tuple-element.44.grad_ref, bf16[2048,128]{1,0:T(8,128)(2,1)S(1)} %get-tuple-element.45.row_agg, bf16[1024,128]{1,0:T(8,128)(2,1)S(1)} %get-tuple-element.46.col_agg, ...), custom_call_target="tpu_custom_call" | custom-call | tf_op jit(solution)/shard_map/pallas_call | solution.py:430
  29.3 1.6 %collective-permute-done.10.columns_ref = bf16[1152,128]{1,0:T(8,128)(2,1)S(1)} collective-permute-done((bf16[1152,128]{1,0:T(8,128)(2,1)S(1)}, bf16[1152,128]{1,0:T(8,128)(2,1)S(1)}, u32[]{:S(2)}, u32[]{:S(2)}) %collective-permute-start.10) | collective-permute-done | bytes 294944 | tf_op jit(solution)/shard_map/ppermute | solution.py:25
  31.0 1.1 %collective-permute-start.11 = (bf16[512,128]{1,0:T(8,128)(2,1)S(1)}, bf16[512,128]{1,0:T(8,128)(2,1)S(1)}, u32[]{:S(2)}, u32[]{:S(2)}) collective-permute-start(bf16[512,128]{1,0:T(8,128)(2,1)S(1)} %get-tuple-element.53), channel_id=1, source_target_pairs={{0,2},{1,9},{2,0},{3,11},{4,6},{5,13},{6,4},{7,15},{8,10},{9,1},{1... | collective-permute-start | bytes 393224 | tf_op jit(solution)/shard_map/ppermute | solution.py:51
  32.1 2.7 %collective-permute-start.12 = (bf16[512,128]{1,0:T(8,128)(2,1)S(1)}, bf16[512,128]{1,0:T(8,128)(2,1)S(1)}, u32[]{:S(2)}, u32[]{:S(2)}) collective-permute-start(bf16[512,128]{1,0:T(8,128)(2,1)S(1)} %get-tuple-element.54), channel_id=1, source_target_pairs={{0,4},{1,17},{2,6},{3,19},{4,0},{5,21},{6,2},{7,23},{8,12},{9,25},... | collective-permute-start | bytes 393224 | tf_op jit(solution)/shard_map/ppermute | solution.py:51
  34.8 0.7 %collective-permute-start.13 = (bf16[512,128]{1,0:T(8,128)(2,1)S(1)}, bf16[512,128]{1,0:T(8,128)(2,1)S(1)}, u32[]{:S(2)}, u32[]{:S(2)}) collective-permute-start(bf16[512,128]{1,0:T(8,128)(2,1)S(1)} %get-tuple-element.55), channel_id=1, source_target_pairs={{0,6},{1,25},{2,4},{3,27},{4,2},{5,29},{6,0},{7,31},{8,14},{9,17},... | collective-permute-start | bytes 393224 | tf_op jit(solution)/shard_map/ppermute | solution.py:51
  35.5 1.3 %collective-permute-start.16 = (bf16[128,128]{1,0:T(8,128)(2,1)S(1)}, bf16[128,128]{1,0:T(8,128)(2,1)S(1)}, u32[]{:S(2)}, u32[]{:S(2)}) collective-permute-start(bf16[128,128]{1,0:T(8,128)(2,1)S(1)} %get-tuple-element.56.refs_0_), channel_id=1, source_target_pairs={{0,24},{8,16},{16,8},{24,0},{1,25},{9,17},{17,9},{25,1},{2,26},{10... | collective-permute-start | bytes 98312 | tf_op jit(solution)/shard_map/ppermute | solution.py:25
  36.8 3.4 %collective-permute-done.16.refs_3_ = bf16[128,128]{1,0:T(8,128)(2,1)S(1)} collective-permute-done((bf16[128,128]{1,0:T(8,128)(2,1)S(1)}, bf16[128,128]{1,0:T(8,128)(2,1)S(1)}, u32[]{:S(2)}, u32[]{:S(2)}) %collective-permute-start.16) | collective-permute-done | bytes 32800 | tf_op jit(solution)/shard_map/ppermute | solution.py:25
  40.7 3.5 %collective-permute-done.14.refs_1_ = bf16[128,128]{1,0:T(8,128)(2,1)S(1)} collective-permute-done((bf16[128,128]{1,0:T(8,128)(2,1)S(1)}, bf16[128,128]{1,0:T(8,128)(2,1)S(1)}, u32[]{:S(2)}, u32[]{:S(2)}) %collective-permute-start.14) | collective-permute-done | bytes 32800 | tf_op jit(solution)/shard_map/ppermute | solution.py:25
  44.4 3.3 %collective-permute-start.21 = (bf16[128,128]{1,0:T(8,128)(2,1)S(1)}, bf16[128,128]{1,0:T(8,128)(2,1)S(1)}, u32[]{:S(2)}, u32[]{:S(2)}) collective-permute-start(bf16[128,128]{1,0:T(8,128)(2,1)S(1)} %shard_map.113.refs_0_), channel_id=1, source_target_pairs={{0,6},{1,7},{2,4},{3,5},{4,2},{5,3},{6,0},{7,1},{8,14},{9,15},{10,... | collective-permute-start | bytes 98312 | tf_op jit(solution)/shard_map/ppermute | solution.py:25
  47.7 1.2 %collective-permute-start.19 = (bf16[128,128]{1,0:T(8,128)(2,1)S(1)}, bf16[128,128]{1,0:T(8,128)(2,1)S(1)}, u32[]{:S(2)}, u32[]{:S(2)}) collective-permute-start(bf16[128,128]{1,0:T(8,128)(2,1)S(1)} %shard_map.113.refs_0_), channel_id=1, source_target_pairs={{0,2},{1,3},{2,0},{3,1},{4,6},{5,7},{6,4},{7,5},{8,10},{9,11},{10,... | collective-permute-start | bytes 98312 | tf_op jit(solution)/shard_map/ppermute | solution.py:25
  49.1 4.7 %collective-permute-start.18 = (bf16[16,128]{1,0:T(8,128)(2,1)S(1)}, bf16[16,128]{1,0:T(8,128)(2,1)S(1)}, u32[]{:S(2)}, u32[]{:S(2)}) collective-permute-start(bf16[16,128]{1,0:T(8,128)(2,1)S(1)} %get-tuple-element.62), channel_id=1, source_target_pairs={{0,0},{31,31},{1,2},{2,1},{3,4},{4,3},{5,6},{6,5},{7,8},{8,7},{9,1... | collective-permute-start | bytes 12296 | tf_op jit(solution)/shard_map/ppermute | solution.py:33
  53.8 3.8 %collective-permute-done.18.far_ref = bf16[16,128]{1,0:T(8,128)(2,1)S(1)} collective-permute-done((bf16[16,128]{1,0:T(8,128)(2,1)S(1)}, bf16[16,128]{1,0:T(8,128)(2,1)S(1)}, u32[]{:S(2)}, u32[]{:S(2)}) %collective-permute-start.18) | collective-permute-done | bytes 4128 | tf_op jit(solution)/shard_map/ppermute | solution.py:33
  57.6 0.7 %shard_map.116 = (bf16[256,128]{1,0:T(8,128)(2,1)}, f32[128,128]{1,0:T(8,128)}) custom-call(bf16[512,128]{1,0:T(8,128)(2,1)S(1)} %get-tuple-element.61.dagg_ref, bf16[512,128]{1,0:T(8,128)(2,1)S(1)} %get-tuple-element.34.body_ref, bf16[512,128]{1,0:T(8,128)(2,1)S(1)} %collective-permute-done.sib_ref, bf16[16,128]{1,0:T(8,128)(2,1)S(1)} %collective-permute-done.18.far_ref, ...), custom_call_target="tpu_custom_call" | custom-call | tf_op jit(solution)/shard_map/pallas_call | solution.py:430
  (35 shorter events, 2.2 us)
Async XLA Ops:
  2.2 10.1 %collective-permute-start = (bf16[512,128]{1,0:T(8,128)(2,1)S(1)}, bf16[512,128]{1,0:T(8,128)(2,1)S(1)}, u32[]{:S(2)}, u32[]{:S(2)}) collective-permute-start(bf16[512,128]{1,0:T(8,128)(2,1)S(1)} %get-tuple-element.34.body_ref), channel_id=1, source_target_pairs={{0,1},{1,0},{2,3},{3,2},{4,5},{5,4},{6,7},{7,6},{8,9},{9,8},{10,11... | collective-permute-start | bytes 393224 | tf_op jit(solution)/shard_map/ppermute | solution.py:25
  2.3 8.8 %collective-permute-start.1 = (bf16[16,128]{1,0:T(8,128)(2,1)S(1)}, bf16[16,128]{1,0:T(8,128)(2,1)S(1)}, u32[]{:S(2)}, u32[]{:S(2)}) collective-permute-start(bf16[16,128]{1,0:T(8,128)(2,1)S(1)} %get-tuple-element.35), channel_id=1, source_target_pairs={{0,0},{31,31},{1,2},{2,1},{3,4},{4,3},{5,6},{6,5},{7,8},{8,7},{9,1... | collective-permute-start | bytes 12296 | tf_op jit(solution)/shard_map/ppermute | solution.py:33
  11.1 1.2 %collective-permute-start.2 = (bf16[16,128]{1,0:T(8,128)(2,1)S(1)}, bf16[16,128]{1,0:T(8,128)(2,1)S(1)}, u32[]{:S(2)}, u32[]{:S(2)}) collective-permute-start(bf16[16,128]{1,0:T(8,128)(2,1)S(1)} %collective-permute-done.1.far_ref), channel_id=1, source_target_pairs={{0,1},{1,0},{2,3},{3,2},{4,5},{5,4},{6,7},{7,6},{8,9},{9,8},{10,11... | collective-permute-start | bytes 12296 | tf_op jit(solution)/shard_map/ppermute | solution.py:25
  12.5 8.2 %collective-permute-start.5 = (bf16[512,128]{1,0:T(8,128)(2,1)S(1)}, bf16[512,128]{1,0:T(8,128)(2,1)S(1)}, u32[]{:S(2)}, u32[]{:S(2)}) collective-permute-start(bf16[512,128]{1,0:T(8,128)(2,1)S(1)} %shard_map.107.refs_3_), channel_id=1, source_target_pairs={{0,6},{1,25},{2,4},{3,27},{4,2},{5,29},{6,0},{7,31},{8,14},{9,17},... | collective-permute-start | bytes 393224 | tf_op jit(solution)/shard_map/ppermute | solution.py:51
  15.0 7.1 %collective-permute-start.4 = (bf16[512,128]{1,0:T(8,128)(2,1)S(1)}, bf16[512,128]{1,0:T(8,128)(2,1)S(1)}, u32[]{:S(2)}, u32[]{:S(2)}) collective-permute-start(bf16[512,128]{1,0:T(8,128)(2,1)S(1)} %shard_map.107.refs_3_), channel_id=1, source_target_pairs={{0,4},{1,17},{2,6},{3,19},{4,0},{5,21},{6,2},{7,23},{8,12},{9,25},... | collective-permute-start | bytes 393224 | tf_op jit(solution)/shard_map/ppermute | solution.py:51
  15.0 7.1 %collective-permute-start.3 = (bf16[512,128]{1,0:T(8,128)(2,1)S(1)}, bf16[512,128]{1,0:T(8,128)(2,1)S(1)}, u32[]{:S(2)}, u32[]{:S(2)}) collective-permute-start(bf16[512,128]{1,0:T(8,128)(2,1)S(1)} %shard_map.107.refs_3_), channel_id=1, source_target_pairs={{0,2},{1,9},{2,0},{3,11},{4,6},{5,13},{6,4},{7,15},{8,10},{9,1},{1... | collective-permute-start | bytes 393224 | tf_op jit(solution)/shard_map/ppermute | solution.py:51
  20.6 3.7 %copy-start = (bf16[128,128]{1,0:T(8,128)(2,1)S(1)}, bf16[128,128]{1,0:T(8,128)(2,1)}, u32[]{:S(2)}) copy-start(bf16[128,128]{1,0:T(8,128)(2,1)} %weight_ref.1) | copy-start | bytes 98308
  22.1 2.2 %collective-permute-start.6 = (bf16[512,128]{1,0:T(8,128)(2,1)S(1)}, bf16[512,128]{1,0:T(8,128)(2,1)S(1)}, u32[]{:S(2)}, u32[]{:S(2)}) collective-permute-start(bf16[512,128]{1,0:T(8,128)(2,1)S(1)} %collective-permute-done.3.refs_4_), channel_id=1, source_target_pairs={{0,1},{1,0},{2,3},{3,2},{4,5},{5,4},{6,7},{7,6},{8,9},{9,8},{10,11... | collective-permute-start | bytes 393224 | tf_op jit(solution)/shard_map/ppermute | solution.py:25
  22.1 2.2 %collective-permute-start.7 = (bf16[512,128]{1,0:T(8,128)(2,1)S(1)}, bf16[512,128]{1,0:T(8,128)(2,1)S(1)}, u32[]{:S(2)}, u32[]{:S(2)}) collective-permute-start(bf16[512,128]{1,0:T(8,128)(2,1)S(1)} %collective-permute-done.4.refs_5_), channel_id=1, source_target_pairs={{0,1},{1,0},{2,3},{3,2},{4,5},{5,4},{6,7},{7,6},{8,9},{9,8},{10,11... | collective-permute-start | bytes 393224 | tf_op jit(solution)/shard_map/ppermute | solution.py:25
  22.6 1.7 %collective-permute-start.8 = (bf16[512,128]{1,0:T(8,128)(2,1)S(1)}, bf16[512,128]{1,0:T(8,128)(2,1)S(1)}, u32[]{:S(2)}, u32[]{:S(2)}) collective-permute-start(bf16[512,128]{1,0:T(8,128)(2,1)S(1)} %collective-permute-done.5.refs_6_), channel_id=1, source_target_pairs={{0,1},{1,0},{2,3},{3,2},{4,5},{5,4},{6,7},{7,6},{8,9},{9,8},{10,11... | collective-permute-start | bytes 393224 | tf_op jit(solution)/shard_map/ppermute | solution.py:25
  27.3 3.6 %collective-permute-start.9 = (bf16[2048,128]{1,0:T(8,128)(2,1)S(1)}, bf16[2048,128]{1,0:T(8,128)(2,1)S(1)}, u32[]{:S(2)}, u32[]{:S(2)}) collective-permute-start(bf16[2048,128]{1,0:T(8,128)(2,1)S(1)} %get-tuple-element.50), channel_id=1, source_target_pairs={{0,1},{1,0},{2,3},{3,2},{4,5},{5,4},{6,7},{7,6},{8,9},{9,8},{10,11... | collective-permute-start | bytes 1572872 | tf_op jit(solution)/shard_map/ppermute | solution.py:25
  29.2 1.6 %collective-permute-start.10 = (bf16[1152,128]{1,0:T(8,128)(2,1)S(1)}, bf16[1152,128]{1,0:T(8,128)(2,1)S(1)}, u32[]{:S(2)}, u32[]{:S(2)}) collective-permute-start(bf16[1152,128]{1,0:T(8,128)(2,1)S(1)} %get-tuple-element.51), channel_id=1, source_target_pairs={{0,1},{1,0},{2,3},{3,2},{4,5},{5,4},{6,7},{7,6},{8,9},{9,8},{10,11... | collective-permute-start | bytes 884744 | tf_op jit(solution)/shard_map/ppermute | solution.py:25
  31.0 13.2 %collective-permute-start.11 = (bf16[512,128]{1,0:T(8,128)(2,1)S(1)}, bf16[512,128]{1,0:T(8,128)(2,1)S(1)}, u32[]{:S(2)}, u32[]{:S(2)}) collective-permute-start(bf16[512,128]{1,0:T(8,128)(2,1)S(1)} %get-tuple-element.53), channel_id=1, source_target_pairs={{0,2},{1,9},{2,0},{3,11},{4,6},{5,13},{6,4},{7,15},{8,10},{9,1},{1... | collective-permute-start | bytes 393224 | tf_op jit(solution)/shard_map/ppermute | solution.py:51
  32.1 12.1 %collective-permute-start.12 = (bf16[512,128]{1,0:T(8,128)(2,1)S(1)}, bf16[512,128]{1,0:T(8,128)(2,1)S(1)}, u32[]{:S(2)}, u32[]{:S(2)}) collective-permute-start(bf16[512,128]{1,0:T(8,128)(2,1)S(1)} %get-tuple-element.54), channel_id=1, source_target_pairs={{0,4},{1,17},{2,6},{3,19},{4,0},{5,21},{6,2},{7,23},{8,12},{9,25},... | collective-permute-start | bytes 393224 | tf_op jit(solution)/shard_map/ppermute | solution.py:51
  34.8 9.4 %collective-permute-start.13 = (bf16[512,128]{1,0:T(8,128)(2,1)S(1)}, bf16[512,128]{1,0:T(8,128)(2,1)S(1)}, u32[]{:S(2)}, u32[]{:S(2)}) collective-permute-start(bf16[512,128]{1,0:T(8,128)(2,1)S(1)} %get-tuple-element.55), channel_id=1, source_target_pairs={{0,6},{1,25},{2,4},{3,27},{4,2},{5,29},{6,0},{7,31},{8,14},{9,17},... | collective-permute-start | bytes 393224 | tf_op jit(solution)/shard_map/ppermute | solution.py:51
  35.5 4.8 %collective-permute-start.16 = (bf16[128,128]{1,0:T(8,128)(2,1)S(1)}, bf16[128,128]{1,0:T(8,128)(2,1)S(1)}, u32[]{:S(2)}, u32[]{:S(2)}) collective-permute-start(bf16[128,128]{1,0:T(8,128)(2,1)S(1)} %get-tuple-element.56.refs_0_), channel_id=1, source_target_pairs={{0,24},{8,16},{16,8},{24,0},{1,25},{9,17},{17,9},{25,1},{2,26},{10... | collective-permute-start | bytes 98312 | tf_op jit(solution)/shard_map/ppermute | solution.py:25
  36.7 3.9 %collective-permute-start.15 = (bf16[128,128]{1,0:T(8,128)(2,1)S(1)}, bf16[128,128]{1,0:T(8,128)(2,1)S(1)}, u32[]{:S(2)}, u32[]{:S(2)}) collective-permute-start(bf16[128,128]{1,0:T(8,128)(2,1)S(1)} %get-tuple-element.56.refs_0_), channel_id=1, source_target_pairs={{0,16},{8,24},{16,0},{24,8},{1,17},{9,25},{17,1},{25,9},{2,18},{10... | collective-permute-start | bytes 98312 | tf_op jit(solution)/shard_map/ppermute | solution.py:25
  40.3 3.9 %collective-permute-start.14 = (bf16[128,128]{1,0:T(8,128)(2,1)S(1)}, bf16[128,128]{1,0:T(8,128)(2,1)S(1)}, u32[]{:S(2)}, u32[]{:S(2)}) collective-permute-start(bf16[128,128]{1,0:T(8,128)(2,1)S(1)} %get-tuple-element.56.refs_0_), channel_id=1, source_target_pairs={{0,8},{8,0},{16,24},{24,16},{1,9},{9,1},{17,25},{25,17},{2,10},{10... | collective-permute-start | bytes 98312 | tf_op jit(solution)/shard_map/ppermute | solution.py:25
  44.3 4.5 %collective-permute-start.17 = (f32[512,128]{1,0:T(8,128)S(1)}, f32[512,128]{1,0:T(8,128)S(1)}, u32[]{:S(2)}, u32[]{:S(2)}) collective-permute-start(f32[512,128]{1,0:T(8,128)S(1)} %shard_map.114.mine_ref), channel_id=1, source_target_pairs={{0,1},{1,0},{2,3},{3,2},{4,5},{5,4},{6,7},{7,6},{8,9},{9,8},{10,11... | collective-permute-start | bytes 786440 | tf_op jit(solution)/shard_map/ppermute | solution.py:25
  44.4 9.4 %collective-permute-start.21 = (bf16[128,128]{1,0:T(8,128)(2,1)S(1)}, bf16[128,128]{1,0:T(8,128)(2,1)S(1)}, u32[]{:S(2)}, u32[]{:S(2)}) collective-permute-start(bf16[128,128]{1,0:T(8,128)(2,1)S(1)} %shard_map.113.refs_0_), channel_id=1, source_target_pairs={{0,6},{1,7},{2,4},{3,5},{4,2},{5,3},{6,0},{7,1},{8,14},{9,15},{10,... | collective-permute-start | bytes 98312 | tf_op jit(solution)/shard_map/ppermute | solution.py:25
  47.7 6.2 %collective-permute-start.20 = (bf16[128,128]{1,0:T(8,128)(2,1)S(1)}, bf16[128,128]{1,0:T(8,128)(2,1)S(1)}, u32[]{:S(2)}, u32[]{:S(2)}) collective-permute-start(bf16[128,128]{1,0:T(8,128)(2,1)S(1)} %shard_map.113.refs_0_), channel_id=1, source_target_pairs={{0,4},{1,5},{2,6},{3,7},{4,0},{5,1},{6,2},{7,3},{8,12},{9,13},{10,... | collective-permute-start | bytes 98312 | tf_op jit(solution)/shard_map/ppermute | solution.py:25
  47.7 6.2 %collective-permute-start.19 = (bf16[128,128]{1,0:T(8,128)(2,1)S(1)}, bf16[128,128]{1,0:T(8,128)(2,1)S(1)}, u32[]{:S(2)}, u32[]{:S(2)}) collective-permute-start(bf16[128,128]{1,0:T(8,128)(2,1)S(1)} %shard_map.113.refs_0_), channel_id=1, source_target_pairs={{0,2},{1,3},{2,0},{3,1},{4,6},{5,7},{6,4},{7,5},{8,10},{9,11},{10,... | collective-permute-start | bytes 98312 | tf_op jit(solution)/shard_map/ppermute | solution.py:25
  49.1 8.5 %collective-permute-start.18 = (bf16[16,128]{1,0:T(8,128)(2,1)S(1)}, bf16[16,128]{1,0:T(8,128)(2,1)S(1)}, u32[]{:S(2)}, u32[]{:S(2)}) collective-permute-start(bf16[16,128]{1,0:T(8,128)(2,1)S(1)} %get-tuple-element.62), channel_id=1, source_target_pairs={{0,0},{31,31},{1,2},{2,1},{3,4},{4,3},{5,6},{6,5},{7,8},{8,7},{9,1... | collective-permute-start | bytes 12296 | tf_op jit(solution)/shard_map/ppermute | solution.py:33

commit v4 on v3

v4 whole, which is shorter than its diff:
```python
import functools

import jax
import jax.numpy as jnp
from jax import lax
from jax.experimental import pallas as pl
from jax.experimental.pallas import tpu as pltpu
from jax.sharding import PartitionSpec as P

BLOCK = 128
AXES = ("row", "col")
INV5 = -858993459
VMEM = pl.BlockSpec(memory_space=pltpu.VMEM)
SMEM = pl.BlockSpec(memory_space=pltpu.SMEM)
CHUNK_CELLS = 128
BOUNDS = (0, 18, 62, 64)


def params(mib):
    return pltpu.CompilerParams(vmem_limit_bytes=mib * 2**20)


def swap(x, axis, step):
    count = lax.axis_size(axis)
    return lax.ppermute(x, axis, [(i, i ^ step) for i in range(count)])


def swap_next(x):
    count = lax.axis_size("row") * lax.axis_size("col")
    pairs = []
    for s in range(1, count, 2):
        pairs += [(s, (s + 1) % count), ((s + 1) % count, s)]
    return lax.ppermute(x, AXES, pairs)


def inner(axis_end):
    chips = lax.axis_size("row") * lax.axis_size("col") // 2
    chip = (lax.axis_index("row") * lax.axis_size("col") + lax.axis_index("col")) // 2
    return jnp.where(chip == (chips - 1 if axis_end else 0), 0.0, 1.0).astype(jnp.float32)


def swap_mixed(x, step, along_z=0):
    nrow, ncol = lax.axis_size("row"), lax.axis_size("col")
    pairs = []
    for r in range(nrow):
        for c in range(ncol):
            if c % 2 == along_z and step < ncol // 2:
                pairs.append((r * ncol + c, r * ncol + (c ^ (2 * step))))
            if c % 2 != along_z and step < nrow:
                pairs.append((r * ncol + c, (r ^ step) * ncol + c))
    return lax.ppermute(x, AXES, pairs)


def stencil(values, link, prev, nxt):
    rows, width = values.shape
    node = lax.broadcasted_iota(jnp.int32, (rows, width), 0)
    before = jnp.where(node == 0, prev, pltpu.roll(values, 1, 0))
    after = jnp.where(node == rows - 1, nxt, pltpu.roll(link * values, rows - 1, 0))
    return 0.5 * values + 0.25 * (link * before + after)


def parity(even, odd):
    side = lax.rem(lax.axis_index("col"), 2)
    pl.when(side == 0)(even)
    pl.when(side == 1)(odd)


def cut_links(cuts_s, node):
    cut = node == cuts_s[0, 0]
    for t in range(1, cuts_s.shape[1]):
        cut = jnp.logical_or(cut, node == cuts_s[0, t])
    return jnp.where(cut, 0.0, 1.0).astype(jnp.float32)


def pinned(arrays):
    return [pltpu.with_memory_space_constraint(x, pltpu.HBM) for x in arrays]


def body_kernel(at, features_hbm, rows, cols, keys, nrows, ncols, cuts_hbm, *refs):
    body_ref, meta_ref, ends_ref, cuts_s, sems = refs
    shard, width = features_hbm.shape
    pairs = [(cuts_hbm, cuts_s), (features_hbm, body_ref.at[pl.ds(0, shard), :])]
    for source, spot in (
        (rows, at.rows), (cols, at.cols), (keys, at.keys), (nrows, at.nrows), (ncols, at.ncols),
    ):
        pairs.append((source.at[0], meta_ref.at[:, pl.ds(spot, source.shape[2])]))
    copies = [pltpu.make_async_copy(a, b, sems.at[t]) for t, (a, b) in enumerate(pairs)]
    for copy in copies:
        copy.start()
    copies[0].wait()
    link = cut_links(cuts_s, lax.broadcasted_iota(jnp.int32, (shard, width), 0))
    body_ref[shard:, :] = link.astype(body_ref.dtype)
    copies[1].wait()
    spot = lax.broadcasted_iota(jnp.int32, (16, width), 0)
    first = link[0:1] * body_ref[0:16, :].astype(jnp.float32)[0:1]
    tail = body_ref[shard - 16 : shard, :].astype(jnp.float32)
    rows = jnp.where(spot == 0, first, jnp.where(spot == 1, link[0:1], tail))
    ends_ref[...] = rows.astype(ends_ref.dtype)
    for copy in copies[2:]:
        copy.wait()


def bodies(at, features, slots, cuts):
    shard, width = features.shape
    arrays = pinned([features, *slots, cuts])
    return pl.pallas_call(
        functools.partial(body_kernel, at),
        out_shape=(
            jax.ShapeDtypeStruct((2 * shard, width), features.dtype),
            jax.ShapeDtypeStruct((1, at.end), jnp.int32),
            jax.ShapeDtypeStruct((16, width), features.dtype),
        ),
        in_specs=[pl.BlockSpec(memory_space=pltpu.HBM)] * len(arrays),
        out_specs=(VMEM, VMEM, VMEM),
        scratch_shapes=[
            pltpu.SMEM(cuts.shape, jnp.int32),
            pltpu.SemaphoreType.DMA((len(arrays),)),
        ],
        compiler_params=params(4),
    )(*arrays)


def pair_kernel(body_ref, sib_ref, far_ref, sib_far_ref, out_ref):
    shard = body_ref.shape[0] // 2

    def both(first_ref, second_ref, before_ref, after_ref):
        first = first_ref[0:shard, :].astype(jnp.float32)
        second = second_ref[0:shard, :].astype(jnp.float32)
        first_link = first_ref[shard:, :].astype(jnp.float32)
        second_link = second_ref[shard:, :].astype(jnp.float32)
        prev = before_ref[...].astype(jnp.float32)[15:16] * inner(False)
        nxt = after_ref[...].astype(jnp.float32)[0:1] * inner(True)
        head = second_link[0:1] * second[0:1]
        tail = first[shard - 1 : shard]
        out_ref[0:shard, :] = stencil(first, first_link, prev, head).astype(out_ref.dtype)
        out_ref[shard:, :] = stencil(second, second_link, tail, nxt).astype(out_ref.dtype)

    parity(
        lambda: both(body_ref, sib_ref, far_ref, sib_far_ref),
        lambda: both(sib_ref, body_ref, sib_far_ref, far_ref),
    )


class Slots:
    def __init__(self, slots, negatives):
        self.slots, self.negatives = slots, negatives
        self.rows, self.cols, self.keys = 0, slots, 2 * slots
        self.nrows = 3 * slots
        self.ncols = self.nrows + negatives
        self.end = self.ncols + negatives


def count_kernel(at, base, blocks, cols, per, meta_ref, count_s, n_ref):
    here_rows = per * 2 * (lax.axis_index("col") // 2)
    here_cols = per * lax.axis_index("row")
    width = cols * BLOCK
    total = jnp.zeros((blocks, width), jnp.float32)
    count = count_s[0, 0]
    for rows_at, cols_at, slots, positive in (
        (at.rows, at.cols, at.slots, True),
        (at.nrows, at.ncols, at.negatives, False),
    ):
        rows = jnp.bitwise_xor(meta_ref[0:1, rows_at : rows_at + slots], here_rows) - base
        cols_of = jnp.bitwise_xor(meta_ref[0:1, cols_at : cols_at + slots], here_cols)
        hit = lax.broadcasted_iota(jnp.int32, (blocks, slots), 0) == rows
        if positive:
            live = lax.broadcasted_iota(jnp.int32, (blocks, slots), 1) < count
            hit = jnp.logical_and(hit, live)
        lane = lax.shift_right_logical(lax.broadcasted_iota(jnp.int32, (width, slots), 0), 7)
        spread = jnp.where(lane == cols_of, 1.0, 0.0).astype(jnp.bfloat16)
        total += lax.dot_general(
            jnp.where(hit, 0.5, 0.0).astype(jnp.bfloat16), spread,
            (((1,), (1,)), ((), ())), preferred_element_type=jnp.float32,
        )
    n_ref[...] = total


def counts(at, base, blocks, cols, per, meta, count):
    return pl.pallas_call(
        functools.partial(count_kernel, at, base, blocks, cols, per),
        out_shape=jax.ShapeDtypeStruct((blocks, cols * BLOCK), jnp.float32),
        in_specs=[VMEM, SMEM],
        out_specs=VMEM,
        compiler_params=params(8),
    )(meta, count)


def target_kernel(at, base, blocks, cols, per, part, bounds, filtered, meta_s, count_s, *refs):
    t_ref, step_ref = refs[-2:]
    a = lax.broadcasted_iota(jnp.int32, (BLOCK, BLOCK), 0)
    b = lax.broadcasted_iota(jnp.int32, (BLOCK, BLOCK), 1)
    step_ref[...] = (a * BLOCK + b) * jnp.int32(4 * 40503)
    if part == 0:

        def clear(i, _):
            row = pl.multiple_of(i * BLOCK, BLOCK)
            t_ref[pl.ds(row, BLOCK), :] = jnp.zeros((BLOCK, cols * BLOCK), jnp.float32)
            return 0

        lax.fori_loop(0, blocks, clear, 0)
    here_rows = per * 2 * (lax.axis_index("col") // 2)
    here_cols = per * lax.axis_index("row")
    count = count_s[0, 0]
    unroll = 8 if at.slots % 8 == 0 else 1

    def positive(s):
        i = jnp.bitwise_xor(meta_s[0, at.rows + s], here_rows) - base
        j = jnp.bitwise_xor(meta_s[0, at.cols + s], here_cols)
        key = meta_s[0, at.keys + s] * 4
        one = jnp.where(s < count, 1.0, 0.0).astype(jnp.float32)

        def add():
            row = pl.multiple_of(i * BLOCK, BLOCK)
            col = pl.multiple_of(j * BLOCK, BLOCK)
            mixed = step_ref[...] + key
            mixed = jnp.bitwise_xor(mixed, lax.shift_right_logical(mixed, 11))
            fifth = lax.shift_right_logical(mixed, 9) * jnp.int32(INV5)
            hit = fifth.astype(jnp.uint32) < jnp.uint32(2**21)
            t_ref[pl.ds(row, BLOCK), pl.ds(col, BLOCK)] += jnp.where(hit, one, 0.0)

        if filtered:
            pl.when(jnp.logical_and(i >= 0, i < blocks))(add)
        else:
            add()

    def positives(g, _):
        for u in range(unroll):
            positive(g * unroll + u)
        return 0

    trips = (count + unroll - 1) // unroll
    first, last = bounds[part], bounds[part + 1]
    lax.fori_loop(trips * first // 64, trips * last // 64, positives, 0)


def targets(at, base, blocks, cols, per, part, bounds, filtered, meta, count, before):
    shape = (blocks * BLOCK, cols * BLOCK)
    old = [] if before is None else [before]
    return pl.pallas_call(
        functools.partial(target_kernel, at, base, blocks, cols, per, part, bounds, filtered),
        out_shape=jax.ShapeDtypeStruct(shape, jnp.float32),
        in_specs=[SMEM, SMEM] + [VMEM] * len(old),
        out_specs=VMEM,
        input_output_aliases={2: 0} if old else {},
        scratch_shapes=[pltpu.VMEM((BLOCK, BLOCK), jnp.int32)],
        compiler_params=params(10),
        cost_estimate=pl.CostEstimate(
            flops=at.slots * BLOCK * BLOCK * 4,
            bytes_accessed=at.slots * BLOCK * BLOCK * 4,
            transcendentals=0,
        ),
    )(meta, count, *old)


def decode_kernel(nz, nrow, first, count, refs):
    steps = max(nz, nrow) - 1
    t_ref, n_ref, weight_ref, pair_ref = refs[:4]
    recv = refs[4 : 4 + steps]
    other = refs[4 + steps : 4 + 2 * steps]
    refs = refs[4 + 2 * steps :]
    drow_ref, early_ref, late_ref, grad_ref, row_agg, col_agg, row_z = refs[:7]
    (col_z,) = refs[7:]
    split = early_ref.shape[0]
    pair = pair_ref.shape[0]
    shard = pair // 2
    columns = nrow * shard
    bf16 = jnp.bfloat16

    def gather(z_refs, row_refs, side):
        for k in range(count):
            ref = pair_ref if first + k == 0 else z_refs[first + k - 1]
            row_agg[k * pair : (k + 1) * pair, :] = ref[...]
        for q in range(nrow):
            ref = pair_ref if q == 0 else row_refs[q - 1]
            col_agg[q * shard : (q + 1) * shard, :] = ref[side * shard : (side + 1) * shard, :]

    parity(lambda: gather(recv, other, 0), lambda: gather(other, recv, 1))
    weight = weight_ref[...]
    dots = functools.partial(lax.dot_general, preferred_element_type=jnp.float32)
    nn = (((1,), (0,)), ((), ()))
    nt = (((1,), (1,)), ((), ()))
    tn = (((0,), (0,)), ((), ()))
    col_z[...] = dots(col_agg[...], weight, nn).astype(bf16)
    for k in range(count):
        at = slice(k * pair, (k + 1) * pair)
        row_z[at, :] = dots(row_agg[at, :], weight, nn).astype(bf16)
        half = row_z[at, :] * bf16(0.5)
        for c in range(0, columns, pair):
            cut = slice(c, min(c + pair, columns))
            curve = jnp.tanh(dots(half, col_z[cut, :], nt))
            for i in range(pair // BLOCK):
                row = k * pair + i * BLOCK
                n = n_ref[row // BLOCK : row // BLOCK + 1, cut]
                tile = t_ref[row : row + BLOCK, cut]
                part = n * curve[i * BLOCK : (i + 1) * BLOCK] + (n - tile)
                grad_ref[row : row + BLOCK, cut] = part.astype(bf16)
        drow = dots(grad_ref[at, :], col_z[...], nn) * (1.0 / 32.0)
        drow_ref[at, :] = drow
        low = k * pair
        if low < split:
            early_ref[at, :] = drow.astype(bf16)
        else:
            late_ref[low - split : low - split + pair, :] = drow.astype(bf16)


def column_kernel(
    nz, grad_ref, row_agg, col_agg, row_z, drow_ref, late_ref, dcol_ref, give_ref, share_ref
):
    dots = functools.partial(lax.dot_general, preferred_element_type=jnp.float32)
    nn = (((1,), (0,)), ((), ()))
    tn = (((0,), (0,)), ((), ()))
    bf16 = jnp.bfloat16
    columns = dcol_ref.shape[0]
    row_t = row_z[...].T
    step = min(columns, 4 * BLOCK)
    for c in range(0, columns, step):
        cut = slice(c, c + step)
        dcol = dots(row_t, grad_ref[:, cut], nn).T * (1.0 / 32.0)
        dcol_ref[cut, :] = dcol
    share = dots(row_agg[...], drow_ref[...].astype(bf16), tn)
    share += dots(col_agg[...], dcol_ref[...].astype(bf16), tn)
    share_ref[...] = share
    width = share.shape[0]
    body = give_ref.shape[0] - width - 16
    give_ref[body : body + width, :] = share.astype(bf16)
    rows = drow_ref.shape[0]
    pair = rows // nz
    z = lax.axis_index("col") // 2

    def first():
        give_ref[0:columns, :] = dcol_ref[...].astype(bf16)
        top = pl.multiple_of(z * pair, 8)
        bottom = pl.multiple_of(jnp.bitwise_xor(z, nz - 1) * pair + pair - 8, 8)
        edge = [drow_ref[pl.ds(top, 8), :], drow_ref[pl.ds(bottom, 8), :]]
        give_ref[body + width :, :] = jnp.concatenate(edge, axis=0).astype(bf16)

    def second():
        give_ref[0 : late_ref.shape[0], :] = late_ref[...]
        give_ref[body + width :, :] = jnp.zeros((16, share.shape[1]), bf16)

    parity(first, second)


def decode(t, n, weight, pair, recv, other, nz, nrow, first, count):
    rows, columns = t.shape
    width = weight.shape[1]
    bf16, real = jnp.bfloat16, jnp.float32
    shape = jax.ShapeDtypeStruct
    early = max(count // 2, 1)
    outs = [
        shape((rows, width), real),
        shape((early * rows // count, width), bf16),
        shape((max(count - early, 1) * rows // count, width), bf16),
        shape((rows, columns), bf16),
        shape((rows, width), bf16),
        shape((columns, width), bf16),
        shape((rows, width), bf16),
    ]
    return pl.pallas_call(
        lambda *refs: decode_kernel(nz, nrow, first, count, refs),
        out_shape=outs,
        in_specs=[VMEM] * (4 + len(recv) + len(other)),
        out_specs=[VMEM] * len(outs),
        scratch_shapes=[pltpu.VMEM((columns, width), bf16)],
        compiler_params=params(12),
        cost_estimate=pl.CostEstimate(
            flops=4 * rows * columns * width,
            bytes_accessed=rows * columns * 4,
            transcendentals=rows * columns,
        ),
    )(t, n, weight, pair, *recv, *other)


def column_parts(nz, parts, width):
    drow, early, late, grad, row_agg, col_agg, row_z = parts
    rows, columns = grad.shape
    bf16, real = jnp.bfloat16, jnp.float32
    shape = jax.ShapeDtypeStruct
    return call(
        functools.partial(column_kernel, nz),
        (
            shape((columns, width), real),
            shape((max(columns, rows // 2) + width + 16, width), bf16),
            shape((width, width), real),
        ),
        (grad, row_agg, col_agg, row_z, drow, late), 10,
    )


def merge_kernel(nz, nrow, drow_ref, dcol_ref, share_ref, early_ref, late_ref, *messages):
    width = share_ref.shape[0]
    half = width // 2
    pair = messages[0].shape[0] - half - 16
    shard = pair // 2
    bf16, real = jnp.bfloat16, jnp.float32
    r = lax.axis_index("row")
    z = lax.axis_index("col") // 2
    spot = lax.broadcasted_iota(jnp.int32, (16, width), 0)

    split = early_ref.shape[0]
    tail = late_ref.shape[0] - width - 16

    def rows_of_other(start, size):
        ref, start = (early_ref, start) if start < split else (late_ref, start - split)
        return ref[start : start + size, :].astype(real)

    def chip_row(k, low):
        row = 0 if low else pair - 1
        found = jnp.zeros((1, width), real)
        for t in range(nz):
            near = t * pair + (0 if low else pair - 16)
            at = row % 16 if not low else 0
            value = drow_ref[near : near + 16, :] + rows_of_other(near, 16)
            found = jnp.where(k == t, value[at : at + 1], found)
        return found

    def block(prev, nxt):
        return jnp.where(spot == 0, prev, jnp.where(spot == 8, nxt, 0.0)).astype(bf16)

    def on(flag):
        return jnp.where(flag, 1.0, 0.0).astype(real)

    def rows():
        share = share_ref[0:half, :] + late_ref[tail : tail + half, :].astype(real)
        for k in range(len(messages)):
            if k < nz:
                at = slice(k * pair, (k + 1) * pair)
                total = drow_ref[at, :] + rows_of_other(k * pair, pair)
                messages[k][0:pair, :] = total.astype(bf16)
            to = jnp.bitwise_xor(z, k)
            prev = jnp.bitwise_xor(jnp.maximum(to - 1, 0), z)
            nxt = jnp.bitwise_xor(jnp.minimum(to + 1, nz - 1), z)
            messages[k][pair : pair + half, :] = share.astype(bf16)
            messages[k][pair + half :, :] = block(
                chip_row(prev, False) * on(to > 0),
                chip_row(nxt, True) * on(to < nz - 1),
            )

    def columns():
        share = share_ref[half:, :] + late_ref[tail + half : tail + width, :].astype(real)
        edge = late_ref[tail + width :, :].astype(real)
        top = pl.multiple_of(z * pair, 8)
        bottom = pl.multiple_of(jnp.bitwise_xor(z, nz - 1) * pair + pair - 8, 8)
        first = drow_ref[pl.ds(top, 8), :][0:1] + edge[0:1]
        last = drow_ref[pl.ds(bottom, 8), :][7:8] + edge[15:16]
        for q in range(len(messages)):
            if q < nrow:
                at = slice(q * shard, (q + 1) * shard)
                messages[q][0:shard, :] = late_ref[at, :]
                messages[q][shard:pair, :] = dcol_ref[at, :].astype(bf16)
            to = jnp.bitwise_xor(r, q)
            before = jnp.bitwise_xor(jnp.maximum(to - 1, 0), r)
            after = jnp.bitwise_xor(jnp.minimum(to + 1, nrow - 1), r)
            mine = dcol_ref[pl.ds(pl.multiple_of(before * shard + shard - 8, 8), 8), :][7:8]
            theirs = late_ref[pl.ds(pl.multiple_of(after * shard, 16), 16), :][0:1]
            prev = last * on(r == to - 1) + mine * on(z == nz - 1)
            nxt = first * on(r == to + 1) + theirs.astype(real) * on(z == 0)
            messages[q][pair : pair + half, :] = share.astype(bf16)
            messages[q][pair + half :, :] = block(prev * on(to > 0), nxt * on(to < nrow - 1))

    parity(rows, columns)


def tree_sum(parts):
    parts = [x.astype(jnp.float32) for x in parts]
    while len(parts) > 1:
        parts = [a + b for a, b in zip(parts[::2], parts[1::2])]
    return parts[0]


def sum_kernel(*refs):
    mine_ref, on_ref = refs[-2:]
    half = on_ref.shape[0] - 32
    pair = mine_ref.shape[0] - half - 16
    total = tree_sum([x[...] for x in refs[:-2]])
    mine_ref[...] = total
    edge = jnp.concatenate([total[0:8], total[pair - 8 : pair]], axis=0)
    on_ref[...] = jnp.concatenate([total[pair:], edge], axis=0).astype(on_ref.dtype)


def last_kernel(nz, *refs):
    parts, out_ref = refs[:-1], refs[-1]
    half = parts[0].shape[0] - 32
    z = lax.axis_index("col") // 2
    total = tree_sum([x[0 : half + 16, :] for x in parts])
    out_ref[0:half, :] = total[0:half]
    spot = lax.broadcasted_iota(jnp.int32, (16, total.shape[1]), 0)
    prev = jnp.where(z == 0, total[half : half + 1], 0.0)
    nxt = jnp.where(z == nz - 1, total[half + 8 : half + 9], 0.0)
    for k in range(1, nz):
        edge = parts[k][half + 16 :, :].astype(jnp.float32)
        to = jnp.bitwise_xor(z, k)
        prev = jnp.where(to == z - 1, edge[15:16], prev)
        nxt = jnp.where(to == z + 1, edge[0:1], nxt)
    out_ref[half:, :] = jnp.where(spot == 0, prev, jnp.where(spot == 8, nxt, 0.0))


def back(dlatent, weight_ref):
    dagg = lax.dot_general(
        dlatent.astype(jnp.bfloat16), weight_ref[...], (((1,), (1,)), ((), ())),
        preferred_element_type=jnp.float32,
    )
    return dagg.astype(jnp.bfloat16).astype(jnp.float32)


def inner_kernel(mine_ref, theirs_ref, weight_ref, body_ref, sib_ref, out_ref):
    shard = out_ref.shape[0]
    pair = 2 * shard
    real = jnp.float32
    link = body_ref[shard:, :].astype(real)
    dagg = back(mine_ref[0:pair, :] + theirs_ref[0:pair, :], weight_ref)
    none = jnp.zeros((1, dagg.shape[1]), real)

    def even():
        nxt = sib_ref[shard : shard + 16, :].astype(real)[0:1] * dagg[shard : shard + 1]
        out_ref[...] = stencil(dagg[0:shard], link, none, nxt)

    def odd():
        out_ref[...] = stencil(dagg[shard:], link, dagg[shard - 1 : shard], none)

    parity(even, odd)


def final_kernel(
    scale, inner_ref, mine_ref, theirs_ref, last_ref, got_ref, weight_ref, body_ref, far_ref,
    features_ref, grad_ref,
):
    half = last_ref.shape[0] - 16
    shard = inner_ref.shape[0]
    at = mine_ref.shape[0] - 16
    real = jnp.float32
    kind = features_ref.dtype
    spot = lax.broadcasted_iota(jnp.int32, (16, inner_ref.shape[1]), 0)

    def even():
        near = back(mine_ref[at:, :] + got_ref[half:, :], weight_ref)[0:1]
        near = near * body_ref[shard : shard + 16, :].astype(real)[0:1]
        head = inner_ref[0:16, :] + jnp.where(spot == 0, 0.25 * near, 0.0)
        features_ref[0:16, :] = head.astype(kind)
        features_ref[16:, :] = inner_ref[16:, :].astype(kind)
        grad_ref[0:half, :] = last_ref[0:half, :] * scale
        grad_ref[half:, :] = got_ref[0:half, :] * scale

    def odd():
        near = back(theirs_ref[at:, :] + last_ref[half:, :], weight_ref)[8:9]
        near = near * far_ref[...].astype(real)[1:2]
        foot = inner_ref[shard - 16 :, :] + jnp.where(spot == 15, 0.25 * near, 0.0)
        features_ref[0 : shard - 16, :] = inner_ref[0 : shard - 16, :].astype(kind)
        features_ref[shard - 16 :, :] = foot.astype(kind)
        grad_ref[0:half, :] = got_ref[0:half, :] * scale
        grad_ref[half:, :] = last_ref[0:half, :] * scale

    parity(even, odd)


def call(kernel, outs, operands, mib, specs=None):
    return pl.pallas_call(
        kernel,
        out_shape=outs,
        in_specs=specs or [VMEM] * len(operands),
        out_specs=jax.tree.map(lambda _: VMEM, outs),
        compiler_params=params(mib),
    )(*operands)


def local(features, weight, cuts, pos_rows, pos_cols, pos_keys, pos_count, neg_rows, neg_cols):
    shard, width = features.shape
    ncol = lax.axis_size("col")
    nrow = lax.axis_size("row")
    nz = ncol // 2
    per = shard // BLOCK
    steps = max(nz, nrow)
    bf16, real = jnp.bfloat16, jnp.float32
    shape = jax.ShapeDtypeStruct

    at = Slots(pos_rows.shape[2], neg_rows.shape[2])
    slots = (pos_rows, pos_cols, pos_keys, neg_rows, neg_cols)
    body, meta, ends = bodies(at, features, slots, cuts)
    far = swap_next(ends)
    cols = nrow * per
    pieces = max(1, ncol * per * cols // CHUNK_CELLS)
    blocks = ncol * per // pieces
    bounds = BOUNDS if pieces == 1 else (0, 64)
    found = [
        targets(at, k * blocks, blocks, cols, per, 0, bounds, pieces > 1, meta, pos_count, None)
        for k in range(pieces)
    ]
    number = [counts(at, k * blocks, blocks, cols, per, meta, pos_count) for k in range(pieces)]
    if pieces == 1:
        far, found, number, body = lax.optimization_barrier((far, found, number, body))
    sib = swap(body, "col", 1)
    sib_far = swap(far, "col", 1)
    pair = call(pair_kernel, shape((2 * shard, width), bf16), (body, sib, far, sib_far), 4)
    recv = [swap_mixed(pair, k) for k in range(steps - 1, 0, -1)][::-1]
    if pieces == 1:
        t = targets(at, 0, blocks, cols, per, 1, bounds, False, meta, pos_count, found[0])
        recv, t = lax.optimization_barrier((recv, t))
        other = [swap(x, "col", 1) for x in recv]
        found = [targets(at, 0, blocks, cols, per, 2, bounds, False, meta, pos_count, t)]
    else:
        other = [swap(x, "col", 1) for x in recv]
    count = nz // pieces
    outs = [
        decode(t, n, weight, pair, recv, other, nz, nrow, k * count, count)
        for k, (t, n) in enumerate(zip(found, number))
    ]
    if pieces == 1:
        drow = outs[0][0]
        early = swap(outs[0][1], "col", 1)
        dcol, late, share = column_parts(nz, outs[0], width)
    else:
        found = [column_parts(count, x, width) for x in outs]
        drow = jnp.concatenate([x[0] for x in outs], axis=0)
        dcol, share = (tree_sum([x[k] for x in found]) for k in (0, 2))
        split = drow.shape[0] // 2
        early = swap(drow[0:split].astype(bf16), "col", 1)
        z = lax.axis_index("col") // 2
        pair_rows = drow.shape[0] // nz
        top = lax.dynamic_slice_in_dim(drow, z * pair_rows, 8)
        bottom = jnp.bitwise_xor(z, nz - 1) * pair_rows + pair_rows - 8
        edge = jnp.concatenate([top, lax.dynamic_slice_in_dim(drow, bottom, 8)], axis=0)
        long = max(dcol.shape[0], split)
        even = jnp.concatenate([dcol, jnp.zeros((long - dcol.shape[0], width), real)], axis=0)
        odd = jnp.concatenate([drow[split:], jnp.zeros((long - split, width), real)], axis=0)
        late = jnp.where(lax.rem(lax.axis_index("col"), 2) == 0, even, odd)
        late = jnp.concatenate([late, share, edge], axis=0).astype(bf16)
    late = swap(late, "col", 1)
    half = weight.shape[0] // 2
    messages = call(
        functools.partial(merge_kernel, nz, nrow),
        [shape((2 * shard + half + 16, width), bf16)] * steps,
        (drow, dcol, share, early, late), 8,
    )
    arrived = [swap_mixed(messages[k], k) for k in range(steps - 1, 0, -1)]
    mine, on = call(
        sum_kernel,
        (shape(messages[0].shape, real), shape((half + 32, width), bf16)),
        [messages[0]] + arrived[::-1], 8,
    )
    theirs = swap(mine, "col", 1)
    arrived = [swap_mixed(on, k, 1) for k in range(steps - 1, 0, -1)]
    last = call(
        functools.partial(last_kernel, nz), shape((half + 16, width), real),
        [on] + arrived[::-1], 4,
    )
    got = swap(last, "col", 1)
    inner_part = call(
        inner_kernel, shape(features.shape, real), (mine, theirs, weight, body, sib), 8
    )
    scale = (shard * ncol * nrow) ** (-0.5)
    return call(
        functools.partial(final_kernel, scale),
        (shape(features.shape, bf16), shape(weight.shape, real)),
        (inner_part, mine, theirs, last, got, weight, body, far), 8,
    )


def solution(mesh):
    placed = (
        P(AXES, None),
        P(),
        P(AXES, None),
        P("row", "col", None),
        P("row", "col", None),
        P("row", "col", None),
        P("row", "col"),
        P("row", "col", None),
        P("row", "col", None),
    )
    return jax.shard_map(
        local, mesh=mesh, in_specs=placed, out_specs=(P(AXES, None), P()), check_vma=False
    )
```

time: 58.7 us -> 50.4 us (0.86)
  the two profiles are of different devices: /device:TPU:4 before, /device:TPU:0 now
where the time goes in v4:
time: 50.4 us; the launch traced here: 49.6 us
  starting transfers between devices  21.3 us (42%)
  waiting for transfers between devices  13.8 us (27%)
  Pallas kernels  13.1 us (26%)
  between operations  1.44 us (3%)
    ppermute x9, starting transfers between devices, swap_mixed(): return lax.ppermute(x, AXES, pairs)  13 us
    ppermute x9, waiting for transfers between devices, swap_mixed(): return lax.ppermute(x, AXES, pairs)  10 us
    ppermute x1, starting transfers between devices, swap_next(): return lax.ppermute(x, AXES, pairs)  6.44 us
    pallas_call x3, Pallas kernels, targets(): pl.pallas_call(functools.partial(target_kernel, at, base, blocks, cols, p...  6.26 us
    ppermute x9, waiting for transfers between devices, swap(): return lax.ppermute(x, axis, [(i, i ^ step) for i in range(count)])  3.76 us
    pallas_call x1, Pallas kernels, decode(): pl.pallas_call(lambda *refs: decode_kernel(nz, nrow, first, count, refs),...  2.98 us
    pallas_call x7, Pallas kernels, call(): pl.pallas_call(kernel, out_shape=outs, in_specs=specs or [VMEM] * len(ope...  2.56 us
    ppermute x9, starting transfers between devices, swap(): return lax.ppermute(x, axis, [(i, i ^ step) for i in range(count)])  1.8 us
  transfers between devices with their start and end apart: 19, of which 10 were waited for; matrix products, arithmetic and copies ran while one was open for 0% of the time, Pallas kernels for 14%

profile of v4, /device:TPU:0, one launch (start us, length us, event | category | flops | bytes accessed | tf_op | source)
XLA Modules:
  0.0 49.6 jit_solution(10368725263230237367)
XLA Ops:
  0.6 0.9 %shard_map.104 = (bf16[512,128]{1,0:T(8,128)(2,1)S(1)}, s32[1,1408]{1,0:T(1,128)S(1)}, bf16[16,128]{1,0:T(8,128)(2,1)S(1)}) custom-call(bf16[256,128]{1,0:T(8,128)(2,1)} %features_hbm.1, s32[1,1,384]{2,1,0:T(1,128)} %rows.1, s32[1,1,384]{2,1,0:T(1,128)} %cols.1, s32[1,1,384]{2,1,0:T(1,128)} %keys.1, s32[1,1,128]{2,1,0:T(1,128)} %nrows.1, ...), custom_call_target="tpu_custom_call" | custom-call | tf_op jit(solution)/shard_map/pallas_call | solution.py:106
  1.6 6.4 %collective-permute-start = (bf16[16,128]{1,0:T(8,128)(2,1)S(1)}, bf16[16,128]{1,0:T(8,128)(2,1)S(1)}, u32[]{:S(2)}, u32[]{:S(2)}) collective-permute-start(bf16[16,128]{1,0:T(8,128)(2,1)S(1)} %get-tuple-element.30), channel_id=1, source_target_pairs={{1,2},{2,1},{3,4},{4,3},{5,6},{6,5},{7,8},{8,7},{9,10},{10,9},{11,... | collective-permute-start | bytes 12296 | tf_op jit(solution)/shard_map/ppermute | solution.py:33
  9.0 2.3 %shard_map.105.refs_0_ = f32[2048,1024]{1,0:T(8,128)S(1)} custom-call(s32[1,1408]{1,0:T(1,128)S(1)} %get-tuple-element.29.meta_s.meta_ref, s32[1,1]{1,0:T(1,128)S(6)} %copy.15.count_s), custom_call_target="tpu_custom_call" | custom-call | flops 25165824 | bytes 25165824 | tf_op jit(solution)/shard_map/pallas_call | solution.py:239
  11.4 0.5 %collective-permute-start.2 = (bf16[16,128]{1,0:T(8,128)(2,1)S(1)}, bf16[16,128]{1,0:T(8,128)(2,1)S(1)}, u32[]{:S(2)}, u32[]{:S(2)}) collective-permute-start(bf16[16,128]{1,0:T(8,128)(2,1)S(1)} %collective-permute-done.far_ref), channel_id=1, source_target_pairs={{0,1},{1,0},{2,3},{3,2},{4,5},{5,4},{6,7},{7,6},{8,9},{9,8},{10,11... | collective-permute-start | bytes 12296 | tf_op jit(solution)/shard_map/ppermute | solution.py:25
  11.9 0.8 %collective-permute-done.2.sib_far_ref = bf16[16,128]{1,0:T(8,128)(2,1)S(1)} collective-permute-done((bf16[16,128]{1,0:T(8,128)(2,1)S(1)}, bf16[16,128]{1,0:T(8,128)(2,1)S(1)}, u32[]{:S(2)}, u32[]{:S(2)}) %collective-permute-start.2) | collective-permute-done | bytes 4128 | tf_op jit(solution)/shard_map/ppermute | solution.py:25
  12.9 0.7 %collective-permute-start.5 = (bf16[512,128]{1,0:T(8,128)(2,1)S(1)}, bf16[512,128]{1,0:T(8,128)(2,1)S(1)}, u32[]{:S(2)}, u32[]{:S(2)}) collective-permute-start(bf16[512,128]{1,0:T(8,128)(2,1)S(1)} %shard_map.107.refs_3_), channel_id=1, source_target_pairs={{0,6},{1,25},{2,4},{3,27},{4,2},{5,29},{6,0},{7,31},{8,14},{9,17},... | collective-permute-start | bytes 393224 | tf_op jit(solution)/shard_map/ppermute | solution.py:51
  13.6 3.7 %collective-permute-start.3 = (bf16[512,128]{1,0:T(8,128)(2,1)S(1)}, bf16[512,128]{1,0:T(8,128)(2,1)S(1)}, u32[]{:S(2)}, u32[]{:S(2)}) collective-permute-start(bf16[512,128]{1,0:T(8,128)(2,1)S(1)} %shard_map.107.refs_3_), channel_id=1, source_target_pairs={{0,2},{1,9},{2,0},{3,11},{4,6},{5,13},{6,4},{7,15},{8,10},{9,1},{1... | collective-permute-start | bytes 393224 | tf_op jit(solution)/shard_map/ppermute | solution.py:51
  17.3 3.2 %shard_map.108.refs_0_ = f32[2048,1024]{1,0:T(8,128)S(1)} custom-call(s32[1,1408]{1,0:T(1,128)S(1)} %get-tuple-element.29.meta_s.meta_ref, s32[1,1]{1,0:T(1,128)S(6)} %copy.15.count_s, f32[2048,1024]{1,0:T(8,128)S(1)} %shard_map.105.refs_0_), custom_call_target="tpu_custom_call", output_to_operand_aliasing={{}: (2, {})} | custom-call | flops 25165824 | bytes 25165824 | tf_op jit(solution)/shard_map/pallas_call | solution.py:239
  20.5 1.8 %collective-permute-done.4.refs_5_ = bf16[512,128]{1,0:T(8,128)(2,1)S(1)} collective-permute-done((bf16[512,128]{1,0:T(8,128)(2,1)S(1)}, bf16[512,128]{1,0:T(8,128)(2,1)S(1)}, u32[]{:S(2)}, u32[]{:S(2)}) %collective-permute-start.4) | collective-permute-done | bytes 131104 | tf_op jit(solution)/shard_map/ppermute | solution.py:51
  22.3 0.5 %collective-permute-start.7 = (bf16[512,128]{1,0:T(8,128)(2,1)S(1)}, bf16[512,128]{1,0:T(8,128)(2,1)S(1)}, u32[]{:S(2)}, u32[]{:S(2)}) collective-permute-start(bf16[512,128]{1,0:T(8,128)(2,1)S(1)} %collective-permute-done.4.refs_5_), channel_id=1, source_target_pairs={{0,1},{1,0},{2,3},{3,2},{4,5},{5,4},{6,7},{7,6},{8,9},{9,8},{10,11... | collective-permute-start | bytes 393224 | tf_op jit(solution)/shard_map/ppermute | solution.py:25
  22.8 0.8 %shard_map.109.refs_0_ = f32[2048,1024]{1,0:T(8,128)S(1)} custom-call(s32[1,1408]{1,0:T(1,128)S(1)} %get-tuple-element.29.meta_s.meta_ref, s32[1,1]{1,0:T(1,128)S(6)} %copy.15.count_s, f32[2048,1024]{1,0:T(8,128)S(1)} %shard_map.108.refs_0_), custom_call_target="tpu_custom_call", output_to_operand_aliasing={{}: (2, {})} | custom-call | flops 25165824 | bytes 25165824 | tf_op jit(solution)/shard_map/pallas_call | solution.py:239
  24.1 3.0 %shard_map.110 = (f32[2048,128]{1,0:T(8,128)S(1)}, bf16[1024,128]{1,0:T(8,128)(2,1)S(1)}, bf16[1024,128]{1,0:T(8,128)(2,1)S(1)}, bf16[2048,1024]{1,0:T(8,128)(2,...) custom-call(f32[2048,1024]{1,0:T(8,128)S(1)} %shard_map.109.refs_0_, ...), custom_call_target="tpu_custom_call" | custom-call | flops 1073741824 | bytes 8388608 | tf_op jit(solution)/shard_map/pallas_call | solution.py:359
  27.1 1.2 %shard_map.111 = (f32[1024,128]{1,0:T(8,128)S(1)}, bf16[1168,128]{1,0:T(8,128)(2,1)S(1)}, f32[128,128]{1,0:T(8,128)S(1)}) custom-call(bf16[2048,1024]{1,0:T(8,128)(2,1)S(1)} %get-tuple-element.41.grad_ref, bf16[2048,128]{1,0:T(8,128)(2,1)S(1)} %get-tuple-element.42.row_agg, bf16[1024,128]{1,0:T(8,128)(2,1)S(1)} %get-tuple-element.43.col_agg, ...), custom_call_target="tpu_custom_call" | custom-call | tf_op jit(solution)/shard_map/pallas_call | solution.py:557
  28.9 1.5 %collective-permute-done.9.early_ref = bf16[1024,128]{1,0:T(8,128)(2,1)S(1)} collective-permute-done((bf16[1024,128]{1,0:T(8,128)(2,1)S(1)}, bf16[1024,128]{1,0:T(8,128)(2,1)S(1)}, u32[]{:S(2)}, u32[]{:S(2)}) %collective-permute-start.9) | collective-permute-done | bytes 262176 | tf_op jit(solution)/shard_map/ppermute | solution.py:25
  30.5 1.5 %collective-permute-start.12 = (bf16[592,128]{1,0:T(8,128)(2,1)S(1)}, bf16[592,128]{1,0:T(8,128)(2,1)S(1)}, u32[]{:S(2)}, u32[]{:S(2)}) collective-permute-start(bf16[592,128]{1,0:T(8,128)(2,1)S(1)} %get-tuple-element.52), channel_id=1, source_target_pairs={{0,4},{1,17},{2,6},{3,19},{4,0},{5,21},{6,2},{7,23},{8,12},{9,25},... | collective-permute-start | bytes 454664 | tf_op jit(solution)/shard_map/ppermute | solution.py:51
  32.0 2.9 %collective-permute-start.13 = (bf16[592,128]{1,0:T(8,128)(2,1)S(1)}, bf16[592,128]{1,0:T(8,128)(2,1)S(1)}, u32[]{:S(2)}, u32[]{:S(2)}) collective-permute-start(bf16[592,128]{1,0:T(8,128)(2,1)S(1)} %get-tuple-element.53), channel_id=1, source_target_pairs={{0,6},{1,25},{2,4},{3,27},{4,2},{5,29},{6,0},{7,31},{8,14},{9,17},... | collective-permute-start | bytes 454664 | tf_op jit(solution)/shard_map/ppermute | solution.py:51
  34.9 2.2 %collective-permute-done.11.refs_1_ = bf16[592,128]{1,0:T(8,128)(2,1)S(1)} collective-permute-done((bf16[592,128]{1,0:T(8,128)(2,1)S(1)}, bf16[592,128]{1,0:T(8,128)(2,1)S(1)}, u32[]{:S(2)}, u32[]{:S(2)}) %collective-permute-start.11) | collective-permute-done | bytes 151584 | tf_op jit(solution)/shard_map/ppermute | solution.py:51
  37.1 2.8 %collective-permute-done.12.refs_2_ = bf16[592,128]{1,0:T(8,128)(2,1)S(1)} collective-permute-done((bf16[592,128]{1,0:T(8,128)(2,1)S(1)}, bf16[592,128]{1,0:T(8,128)(2,1)S(1)}, u32[]{:S(2)}, u32[]{:S(2)}) %collective-permute-start.12) | collective-permute-done | bytes 151584 | tf_op jit(solution)/shard_map/ppermute | solution.py:51
  40.1 3.5 %collective-permute-start.17 = (bf16[96,128]{1,0:T(8,128)(2,1)S(1)}, bf16[96,128]{1,0:T(8,128)(2,1)S(1)}, u32[]{:S(2)}, u32[]{:S(2)}) collective-permute-start(bf16[96,128]{1,0:T(8,128)(2,1)S(1)} %get-tuple-element.55.refs_0_), channel_id=1, source_target_pairs={{0,24},{1,7},{2,26},{3,5},{4,28},{5,3},{6,30},{7,1},{8,16},{9,15},... | collective-permute-start | bytes 73736 | tf_op jit(solution)/shard_map/ppermute | solution.py:51
  43.6 0.6 %collective-permute-start.15 = (bf16[96,128]{1,0:T(8,128)(2,1)S(1)}, bf16[96,128]{1,0:T(8,128)(2,1)S(1)}, u32[]{:S(2)}, u32[]{:S(2)}) collective-permute-start(bf16[96,128]{1,0:T(8,128)(2,1)S(1)} %get-tuple-element.55.refs_0_), channel_id=1, source_target_pairs={{0,8},{1,3},{2,10},{3,1},{4,12},{5,7},{6,14},{7,5},{8,0},{9,11},{1... | collective-permute-start | bytes 73736 | tf_op jit(solution)/shard_map/ppermute | solution.py:51
  44.3 1.2 %collective-permute-done.17.refs_3_ = bf16[96,128]{1,0:T(8,128)(2,1)S(1)} collective-permute-done((bf16[96,128]{1,0:T(8,128)(2,1)S(1)}, bf16[96,128]{1,0:T(8,128)(2,1)S(1)}, u32[]{:S(2)}, u32[]{:S(2)}) %collective-permute-start.17) | collective-permute-done | bytes 24608 | tf_op jit(solution)/shard_map/ppermute | solution.py:51
  45.4 2.0 %collective-permute-done.16.refs_2_ = bf16[96,128]{1,0:T(8,128)(2,1)S(1)} collective-permute-done((bf16[96,128]{1,0:T(8,128)(2,1)S(1)}, bf16[96,128]{1,0:T(8,128)(2,1)S(1)}, u32[]{:S(2)}, u32[]{:S(2)}) %collective-permute-start.16) | collective-permute-done | bytes 24608 | tf_op jit(solution)/shard_map/ppermute | solution.py:51
  47.8 0.9 %collective-permute-done.18.got_ref = f32[80,128]{1,0:T(8,128)S(1)} collective-permute-done((f32[80,128]{1,0:T(8,128)S(1)}, f32[80,128]{1,0:T(8,128)S(1)}, u32[]{:S(2)}, u32[]{:S(2)}) %collective-permute-start.18) | collective-permute-done | bytes 40992 | tf_op jit(solution)/shard_map/ppermute | solution.py:25
  48.8 0.8 %shard_map.116 = (bf16[256,128]{1,0:T(8,128)(2,1)}, f32[128,128]{1,0:T(8,128)}) custom-call(f32[256,128]{1,0:T(8,128)S(1)} %shard_map.114.inner_ref, f32[592,128]{1,0:T(8,128)S(1)} %get-tuple-element.54.mine_ref, f32[592,128]{1,0:T(8,128)S(1)} %collective-permute-done.14.theirs_ref, f32[80,128]{1,0:T(8,128)S(1)} %shard_map.115.last_ref, ...), custom_call_target="tpu_custom_call" | custom-call | tf_op jit(solution)/shard_map/pallas_call | solution.py:557
  (29 shorter events, 2.4 us)
Async XLA Ops:
  1.6 9.7 %collective-permute-start = (bf16[16,128]{1,0:T(8,128)(2,1)S(1)}, bf16[16,128]{1,0:T(8,128)(2,1)S(1)}, u32[]{:S(2)}, u32[]{:S(2)}) collective-permute-start(bf16[16,128]{1,0:T(8,128)(2,1)S(1)} %get-tuple-element.30), channel_id=1, source_target_pairs={{1,2},{2,1},{3,4},{4,3},{5,6},{6,5},{7,8},{8,7},{9,10},{10,9},{11,... | collective-permute-start | bytes 12296 | tf_op jit(solution)/shard_map/ppermute | solution.py:33
  11.3 1.4 %collective-permute-start.1 = (bf16[512,128]{1,0:T(8,128)(2,1)S(1)}, bf16[512,128]{1,0:T(8,128)(2,1)S(1)}, u32[]{:S(2)}, u32[]{:S(2)}) collective-permute-start(bf16[512,128]{1,0:T(8,128)(2,1)S(1)} %get-tuple-element.32.body_ref), channel_id=1, source_target_pairs={{0,1},{1,0},{2,3},{3,2},{4,5},{5,4},{6,7},{7,6},{8,9},{9,8},{10,11... | collective-permute-start | bytes 393224 | tf_op jit(solution)/shard_map/ppermute | solution.py:25
  11.4 1.3 %collective-permute-start.2 = (bf16[16,128]{1,0:T(8,128)(2,1)S(1)}, bf16[16,128]{1,0:T(8,128)(2,1)S(1)}, u32[]{:S(2)}, u32[]{:S(2)}) collective-permute-start(bf16[16,128]{1,0:T(8,128)(2,1)S(1)} %collective-permute-done.far_ref), channel_id=1, source_target_pairs={{0,1},{1,0},{2,3},{3,2},{4,5},{5,4},{6,7},{7,6},{8,9},{9,8},{10,11... | collective-permute-start | bytes 12296 | tf_op jit(solution)/shard_map/ppermute | solution.py:25
  12.9 7.7 %collective-permute-start.5 = (bf16[512,128]{1,0:T(8,128)(2,1)S(1)}, bf16[512,128]{1,0:T(8,128)(2,1)S(1)}, u32[]{:S(2)}, u32[]{:S(2)}) collective-permute-start(bf16[512,128]{1,0:T(8,128)(2,1)S(1)} %shard_map.107.refs_3_), channel_id=1, source_target_pairs={{0,6},{1,25},{2,4},{3,27},{4,2},{5,29},{6,0},{7,31},{8,14},{9,17},... | collective-permute-start | bytes 393224 | tf_op jit(solution)/shard_map/ppermute | solution.py:51
  13.6 8.7 %collective-permute-start.4 = (bf16[512,128]{1,0:T(8,128)(2,1)S(1)}, bf16[512,128]{1,0:T(8,128)(2,1)S(1)}, u32[]{:S(2)}, u32[]{:S(2)}) collective-permute-start(bf16[512,128]{1,0:T(8,128)(2,1)S(1)} %shard_map.107.refs_3_), channel_id=1, source_target_pairs={{0,4},{1,17},{2,6},{3,19},{4,0},{5,21},{6,2},{7,23},{8,12},{9,25},... | collective-permute-start | bytes 393224 | tf_op jit(solution)/shard_map/ppermute | solution.py:51
  13.6 8.7 %collective-permute-start.3 = (bf16[512,128]{1,0:T(8,128)(2,1)S(1)}, bf16[512,128]{1,0:T(8,128)(2,1)S(1)}, u32[]{:S(2)}, u32[]{:S(2)}) collective-permute-start(bf16[512,128]{1,0:T(8,128)(2,1)S(1)} %shard_map.107.refs_3_), channel_id=1, source_target_pairs={{0,2},{1,9},{2,0},{3,11},{4,6},{5,13},{6,4},{7,15},{8,10},{9,1},{1... | collective-permute-start | bytes 393224 | tf_op jit(solution)/shard_map/ppermute | solution.py:51
  20.5 3.6 %copy-start = (bf16[128,128]{1,0:T(8,128)(2,1)S(1)}, bf16[128,128]{1,0:T(8,128)(2,1)}, u32[]{:S(2)}) copy-start(bf16[128,128]{1,0:T(8,128)(2,1)} %weight_ref.3) | copy-start | bytes 98308
  22.3 1.3 %collective-permute-start.6 = (bf16[512,128]{1,0:T(8,128)(2,1)S(1)}, bf16[512,128]{1,0:T(8,128)(2,1)S(1)}, u32[]{:S(2)}, u32[]{:S(2)}) collective-permute-start(bf16[512,128]{1,0:T(8,128)(2,1)S(1)} %collective-permute-done.3.refs_4_), channel_id=1, source_target_pairs={{0,1},{1,0},{2,3},{3,2},{4,5},{5,4},{6,7},{7,6},{8,9},{9,8},{10,11... | collective-permute-start | bytes 393224 | tf_op jit(solution)/shard_map/ppermute | solution.py:25
  22.3 1.5 %collective-permute-start.7 = (bf16[512,128]{1,0:T(8,128)(2,1)S(1)}, bf16[512,128]{1,0:T(8,128)(2,1)S(1)}, u32[]{:S(2)}, u32[]{:S(2)}) collective-permute-start(bf16[512,128]{1,0:T(8,128)(2,1)S(1)} %collective-permute-done.4.refs_5_), channel_id=1, source_target_pairs={{0,1},{1,0},{2,3},{3,2},{4,5},{5,4},{6,7},{7,6},{8,9},{9,8},{10,11... | collective-permute-start | bytes 393224 | tf_op jit(solution)/shard_map/ppermute | solution.py:25
  22.8 1.3 %collective-permute-start.8 = (bf16[512,128]{1,0:T(8,128)(2,1)S(1)}, bf16[512,128]{1,0:T(8,128)(2,1)S(1)}, u32[]{:S(2)}, u32[]{:S(2)}) collective-permute-start(bf16[512,128]{1,0:T(8,128)(2,1)S(1)} %collective-permute-done.5.refs_6_), channel_id=1, source_target_pairs={{0,1},{1,0},{2,3},{3,2},{4,5},{5,4},{6,7},{7,6},{8,9},{9,8},{10,11... | collective-permute-start | bytes 393224 | tf_op jit(solution)/shard_map/ppermute | solution.py:25
  28.3 2.0 %collective-permute-start.10 = (bf16[1168,128]{1,0:T(8,128)(2,1)S(1)}, bf16[1168,128]{1,0:T(8,128)(2,1)S(1)}, u32[]{:S(2)}, u32[]{:S(2)}) collective-permute-start(bf16[1168,128]{1,0:T(8,128)(2,1)S(1)} %get-tuple-element.49), channel_id=1, source_target_pairs={{0,1},{1,0},{2,3},{3,2},{4,5},{5,4},{6,7},{7,6},{8,9},{9,8},{10,11... | collective-permute-start | bytes 897032 | tf_op jit(solution)/shard_map/ppermute | solution.py:25
  28.6 1.8 %collective-permute-start.9 = (bf16[1024,128]{1,0:T(8,128)(2,1)S(1)}, bf16[1024,128]{1,0:T(8,128)(2,1)S(1)}, u32[]{:S(2)}, u32[]{:S(2)}) collective-permute-start(bf16[1024,128]{1,0:T(8,128)(2,1)S(1)} %get-tuple-element.48), channel_id=1, source_target_pairs={{0,1},{1,0},{2,3},{3,2},{4,5},{5,4},{6,7},{7,6},{8,9},{9,8},{10,11... | collective-permute-start | bytes 786440 | tf_op jit(solution)/shard_map/ppermute | solution.py:25
  30.5 6.7 %collective-permute-start.11 = (bf16[592,128]{1,0:T(8,128)(2,1)S(1)}, bf16[592,128]{1,0:T(8,128)(2,1)S(1)}, u32[]{:S(2)}, u32[]{:S(2)}) collective-permute-start(bf16[592,128]{1,0:T(8,128)(2,1)S(1)} %get-tuple-element.51), channel_id=1, source_target_pairs={{0,2},{1,9},{2,0},{3,11},{4,6},{5,13},{6,4},{7,15},{8,10},{9,1},{1... | collective-permute-start | bytes 454664 | tf_op jit(solution)/shard_map/ppermute | solution.py:51
  30.5 9.4 %collective-permute-start.12 = (bf16[592,128]{1,0:T(8,128)(2,1)S(1)}, bf16[592,128]{1,0:T(8,128)(2,1)S(1)}, u32[]{:S(2)}, u32[]{:S(2)}) collective-permute-start(bf16[592,128]{1,0:T(8,128)(2,1)S(1)} %get-tuple-element.52), channel_id=1, source_target_pairs={{0,4},{1,17},{2,6},{3,19},{4,0},{5,21},{6,2},{7,23},{8,12},{9,25},... | collective-permute-start | bytes 454664 | tf_op jit(solution)/shard_map/ppermute | solution.py:51
  32.0 8.0 %collective-permute-start.13 = (bf16[592,128]{1,0:T(8,128)(2,1)S(1)}, bf16[592,128]{1,0:T(8,128)(2,1)S(1)}, u32[]{:S(2)}, u32[]{:S(2)}) collective-permute-start(bf16[592,128]{1,0:T(8,128)(2,1)S(1)} %get-tuple-element.53), channel_id=1, source_target_pairs={{0,6},{1,25},{2,4},{3,27},{4,2},{5,29},{6,0},{7,31},{8,14},{9,17},... | collective-permute-start | bytes 454664 | tf_op jit(solution)/shard_map/ppermute | solution.py:51
  40.1 7.5 %collective-permute-start.14 = (f32[592,128]{1,0:T(8,128)S(1)}, f32[592,128]{1,0:T(8,128)S(1)}, u32[]{:S(2)}, u32[]{:S(2)}) collective-permute-start(f32[592,128]{1,0:T(8,128)S(1)} %get-tuple-element.54.mine_ref), channel_id=1, source_target_pairs={{0,1},{1,0},{2,3},{3,2},{4,5},{5,4},{6,7},{7,6},{8,9},{9,8},{10,11... | collective-permute-start | bytes 909320 | tf_op jit(solution)/shard_map/ppermute | solution.py:25
  40.1 5.3 %collective-permute-start.17 = (bf16[96,128]{1,0:T(8,128)(2,1)S(1)}, bf16[96,128]{1,0:T(8,128)(2,1)S(1)}, u32[]{:S(2)}, u32[]{:S(2)}) collective-permute-start(bf16[96,128]{1,0:T(8,128)(2,1)S(1)} %get-tuple-element.55.refs_0_), channel_id=1, source_target_pairs={{0,24},{1,7},{2,26},{3,5},{4,28},{5,3},{6,30},{7,1},{8,16},{9,15},... | collective-permute-start | bytes 73736 | tf_op jit(solution)/shard_map/ppermute | solution.py:51
  43.6 3.8 %collective-permute-start.16 = (bf16[96,128]{1,0:T(8,128)(2,1)S(1)}, bf16[96,128]{1,0:T(8,128)(2,1)S(1)}, u32[]{:S(2)}, u32[]{:S(2)}) collective-permute-start(bf16[96,128]{1,0:T(8,128)(2,1)S(1)} %get-tuple-element.55.refs_0_), channel_id=1, source_target_pairs={{0,16},{1,5},{2,18},{3,7},{4,20},{5,1},{6,22},{7,3},{8,24},{9,13},... | collective-permute-start | bytes 73736 | tf_op jit(solution)/shard_map/ppermute | solution.py:51
  43.6 3.8 %collective-permute-start.15 = (bf16[96,128]{1,0:T(8,128)(2,1)S(1)}, bf16[96,128]{1,0:T(8,128)(2,1)S(1)}, u32[]{:S(2)}, u32[]{:S(2)}) collective-permute-start(bf16[96,128]{1,0:T(8,128)(2,1)S(1)} %get-tuple-element.55.refs_0_), channel_id=1, source_target_pairs={{0,8},{1,3},{2,10},{3,1},{4,12},{5,7},{6,14},{7,5},{8,0},{9,11},{1... | collective-permute-start | bytes 73736 | tf_op jit(solution)/shard_map/ppermute | solution.py:51
  47.5 1.3 %collective-permute-start.18 = (f32[80,128]{1,0:T(8,128)S(1)}, f32[80,128]{1,0:T(8,128)S(1)}, u32[]{:S(2)}, u32[]{:S(2)}) collective-permute-start(f32[80,128]{1,0:T(8,128)S(1)} %shard_map.115.last_ref), channel_id=1, source_target_pairs={{0,1},{1,0},{2,3},{3,2},{4,5},{5,4},{6,7},{7,6},{8,9},{9,8},{10,11... | collective-permute-start | bytes 122888 | tf_op jit(solution)/shard_map/ppermute | solution.py:25

commit v5 on v4

--- a/solution.py
+++ b/solution.py
@@ -238,7 +238,7 @@
     old = [] if before is None else [before]
     return pl.pallas_call(
         functools.partial(target_kernel, at, base, blocks, cols, per, part, bounds, filtered),
-        out_shape=jax.ShapeDtypeStruct(shape, jnp.float32),
+        out_shape=pltpu.VMEM(shape, jnp.float32),
         in_specs=[SMEM, SMEM] + [VMEM] * len(old),
         out_specs=VMEM,
         input_output_aliases={2: 0} if old else {},

time: 50.4 us -> 49.4 us (0.980); the launches traced: 49.6 us -> 49.4 us
  Pallas kernels: 13.1 us -> 11.9 us
  waiting for transfers between devices: 13.8 us -> 14.7 us
    pallas_call x3, Pallas kernels: 6.26 us -> 5.07 us  [targets(): pl.pallas_call(functools.partial(target_kernel, at, base, blocks, cols, p...]
    ppermute x9, waiting for transfers between devices: 10 us -> 11 us  [swap_mixed(): return lax.ppermute(x, AXES, pairs)]
  transfers between devices with their start and end apart: 19 -> 19, of which waited for: 10 -> 12; matrix products, arithmetic and copies ran while one was open for 0% -> 0% of each run, Pallas kernels for 14% -> 12%
where the time goes in v5:
time: 49.4 us
  starting transfers between devices  21.3 us (43%)
  waiting for transfers between devices  14.7 us (30%)
  Pallas kernels  11.9 us (24%)
  between operations  1.43 us (3%)
    ppermute x9, starting transfers between devices, swap_mixed(): return lax.ppermute(x, AXES, pairs)  13.1 us
    ppermute x9, waiting for transfers between devices, swap_mixed(): return lax.ppermute(x, AXES, pairs)  11 us
    ppermute x1, starting transfers between devices, swap_next(): return lax.ppermute(x, AXES, pairs)  6.44 us
    pallas_call x3, Pallas kernels, targets(): pl.pallas_call(functools.partial(target_kernel, at, base, blocks, cols, p...  5.07 us
    ppermute x9, waiting for transfers between devices, swap(): return lax.ppermute(x, axis, [(i, i ^ step) for i in range(count)])  3.76 us
    pallas_call x1, Pallas kernels, decode(): pl.pallas_call(lambda *refs: decode_kernel(nz, nrow, first, count, refs),...  2.98 us
    pallas_call x7, Pallas kernels, call(): pl.pallas_call(kernel, out_shape=outs, in_specs=specs or [VMEM] * len(ope...  2.56 us
    ppermute x9, starting transfers between devices, swap(): return lax.ppermute(x, axis, [(i, i ^ step) for i in range(count)])  1.8 us
  transfers between devices with their start and end apart: 19, of which 12 were waited for; matrix products, arithmetic and copies ran while one was open for 0% of the time, Pallas kernels for 12%

profile of v5, /device:TPU:0, one launch (start us, length us, event | category | flops | bytes accessed | tf_op | source)
XLA Modules:
  0.0 49.4 jit_solution(10368725263230237367)
XLA Ops:
  0.6 0.9 %shard_map.104 = (bf16[512,128]{1,0:T(8,128)(2,1)S(1)}, s32[1,1408]{1,0:T(1,128)S(1)}, bf16[16,128]{1,0:T(8,128)(2,1)S(1)}) custom-call(bf16[256,128]{1,0:T(8,128)(2,1)} %features_hbm.1, s32[1,1,384]{2,1,0:T(1,128)} %rows.1, s32[1,1,384]{2,1,0:T(1,128)} %cols.1, s32[1,1,384]{2,1,0:T(1,128)} %keys.1, s32[1,1,128]{2,1,0:T(1,128)} %nrows.1, ...), custom_call_target="tpu_custom_call" | custom-call | tf_op jit(solution)/shard_map/pallas_call | solution.py:106
  1.6 6.4 %collective-permute-start = (bf16[16,128]{1,0:T(8,128)(2,1)S(1)}, bf16[16,128]{1,0:T(8,128)(2,1)S(1)}, u32[]{:S(2)}, u32[]{:S(2)}) collective-permute-start(bf16[16,128]{1,0:T(8,128)(2,1)S(1)} %get-tuple-element.30), channel_id=1, source_target_pairs={{1,2},{2,1},{3,4},{4,3},{5,6},{6,5},{7,8},{8,7},{9,10},{10,9},{11,... | collective-permute-start | bytes 12296 | tf_op jit(solution)/shard_map/ppermute | solution.py:33
  9.0 1.9 %shard_map.105.refs_0_ = f32[2048,1024]{1,0:T(8,128)S(1)} custom-call(s32[1,1408]{1,0:T(1,128)S(1)} %get-tuple-element.29.meta_s.meta_ref, s32[1,1]{1,0:T(1,128)S(6)} %copy.15.count_s), custom_call_target="tpu_custom_call" | custom-call | flops 25165824 | bytes 25165824 | tf_op jit(solution)/shard_map/pallas_call | solution.py:239
  11.5 0.8 %collective-permute-done.2.sib_far_ref = bf16[16,128]{1,0:T(8,128)(2,1)S(1)} collective-permute-done((bf16[16,128]{1,0:T(8,128)(2,1)S(1)}, bf16[16,128]{1,0:T(8,128)(2,1)S(1)}, u32[]{:S(2)}, u32[]{:S(2)}) %collective-permute-start.2) | collective-permute-done | bytes 4128 | tf_op jit(solution)/shard_map/ppermute | solution.py:25
  12.5 1.1 %collective-permute-start.5 = (bf16[512,128]{1,0:T(8,128)(2,1)S(1)}, bf16[512,128]{1,0:T(8,128)(2,1)S(1)}, u32[]{:S(2)}, u32[]{:S(2)}) collective-permute-start(bf16[512,128]{1,0:T(8,128)(2,1)S(1)} %shard_map.107.refs_3_), channel_id=1, source_target_pairs={{0,6},{1,25},{2,4},{3,27},{4,2},{5,29},{6,0},{7,31},{8,14},{9,17},... | collective-permute-start | bytes 393224 | tf_op jit(solution)/shard_map/ppermute | solution.py:51
  13.7 3.2 %collective-permute-start.3 = (bf16[512,128]{1,0:T(8,128)(2,1)S(1)}, bf16[512,128]{1,0:T(8,128)(2,1)S(1)}, u32[]{:S(2)}, u32[]{:S(2)}) collective-permute-start(bf16[512,128]{1,0:T(8,128)(2,1)S(1)} %shard_map.107.refs_3_), channel_id=1, source_target_pairs={{0,2},{1,9},{2,0},{3,11},{4,6},{5,13},{6,4},{7,15},{8,10},{9,1},{1... | collective-permute-start | bytes 393224 | tf_op jit(solution)/shard_map/ppermute | solution.py:51
  17.0 2.3 %shard_map.108.refs_0_ = f32[2048,1024]{1,0:T(8,128)S(1)} custom-call(s32[1,1408]{1,0:T(1,128)S(1)} %get-tuple-element.29.meta_s.meta_ref, s32[1,1]{1,0:T(1,128)S(6)} %copy.15.count_s, f32[2048,1024]{1,0:T(8,128)S(1)} %shard_map.105.refs_0_), custom_call_target="tpu_custom_call", output_to_operand_aliasing={{}: (2, {})} | custom-call | flops 25165824 | bytes 25165824 | tf_op jit(solution)/shard_map/pallas_call | solution.py:239
  19.5 2.6 %collective-permute-done.4.refs_5_ = bf16[512,128]{1,0:T(8,128)(2,1)S(1)} collective-permute-done((bf16[512,128]{1,0:T(8,128)(2,1)S(1)}, bf16[512,128]{1,0:T(8,128)(2,1)S(1)}, u32[]{:S(2)}, u32[]{:S(2)}) %collective-permute-start.4) | collective-permute-done | bytes 131104 | tf_op jit(solution)/shard_map/ppermute | solution.py:51
  22.7 0.8 %shard_map.109.refs_0_ = f32[2048,1024]{1,0:T(8,128)S(1)} custom-call(s32[1,1408]{1,0:T(1,128)S(1)} %get-tuple-element.29.meta_s.meta_ref, s32[1,1]{1,0:T(1,128)S(6)} %copy.15.count_s, f32[2048,1024]{1,0:T(8,128)S(1)} %shard_map.108.refs_0_), custom_call_target="tpu_custom_call", output_to_operand_aliasing={{}: (2, {})} | custom-call | flops 25165824 | bytes 25165824 | tf_op jit(solution)/shard_map/pallas_call | solution.py:239
  24.0 3.0 %shard_map.110 = (f32[2048,128]{1,0:T(8,128)S(1)}, bf16[1024,128]{1,0:T(8,128)(2,1)S(1)}, bf16[1024,128]{1,0:T(8,128)(2,1)S(1)}, bf16[2048,1024]{1,0:T(8,128)(2,...) custom-call(f32[2048,1024]{1,0:T(8,128)S(1)} %shard_map.109.refs_0_, ...), custom_call_target="tpu_custom_call" | custom-call | flops 1073741824 | bytes 8388608 | tf_op jit(solution)/shard_map/pallas_call | solution.py:359
  27.0 1.2 %shard_map.111 = (f32[1024,128]{1,0:T(8,128)S(1)}, bf16[1168,128]{1,0:T(8,128)(2,1)S(1)}, f32[128,128]{1,0:T(8,128)S(1)}) custom-call(bf16[2048,1024]{1,0:T(8,128)(2,1)S(1)} %get-tuple-element.41.grad_ref, bf16[2048,128]{1,0:T(8,128)(2,1)S(1)} %get-tuple-element.42.row_agg, bf16[1024,128]{1,0:T(8,128)(2,1)S(1)} %get-tuple-element.43.col_agg, ...), custom_call_target="tpu_custom_call" | custom-call | tf_op jit(solution)/shard_map/pallas_call | solution.py:557
  28.8 1.5 %collective-permute-done.9.early_ref = bf16[1024,128]{1,0:T(8,128)(2,1)S(1)} collective-permute-done((bf16[1024,128]{1,0:T(8,128)(2,1)S(1)}, bf16[1024,128]{1,0:T(8,128)(2,1)S(1)}, u32[]{:S(2)}, u32[]{:S(2)}) %collective-permute-start.9) | collective-permute-done | bytes 262176 | tf_op jit(solution)/shard_map/ppermute | solution.py:25
  30.4 1.8 %collective-permute-start.12 = (bf16[592,128]{1,0:T(8,128)(2,1)S(1)}, bf16[592,128]{1,0:T(8,128)(2,1)S(1)}, u32[]{:S(2)}, u32[]{:S(2)}) collective-permute-start(bf16[592,128]{1,0:T(8,128)(2,1)S(1)} %get-tuple-element.52), channel_id=1, source_target_pairs={{0,4},{1,17},{2,6},{3,19},{4,0},{5,21},{6,2},{7,23},{8,12},{9,25},... | collective-permute-start | bytes 454664 | tf_op jit(solution)/shard_map/ppermute | solution.py:51
  32.2 2.6 %collective-permute-start.13 = (bf16[592,128]{1,0:T(8,128)(2,1)S(1)}, bf16[592,128]{1,0:T(8,128)(2,1)S(1)}, u32[]{:S(2)}, u32[]{:S(2)}) collective-permute-start(bf16[592,128]{1,0:T(8,128)(2,1)S(1)} %get-tuple-element.53), channel_id=1, source_target_pairs={{0,6},{1,25},{2,4},{3,27},{4,2},{5,29},{6,0},{7,31},{8,14},{9,17},... | collective-permute-start | bytes 454664 | tf_op jit(solution)/shard_map/ppermute | solution.py:51
  34.8 2.2 %collective-permute-done.11.refs_1_ = bf16[592,128]{1,0:T(8,128)(2,1)S(1)} collective-permute-done((bf16[592,128]{1,0:T(8,128)(2,1)S(1)}, bf16[592,128]{1,0:T(8,128)(2,1)S(1)}, u32[]{:S(2)}, u32[]{:S(2)}) %collective-permute-start.11) | collective-permute-done | bytes 151584 | tf_op jit(solution)/shard_map/ppermute | solution.py:51
  37.0 2.8 %collective-permute-done.12.refs_2_ = bf16[592,128]{1,0:T(8,128)(2,1)S(1)} collective-permute-done((bf16[592,128]{1,0:T(8,128)(2,1)S(1)}, bf16[592,128]{1,0:T(8,128)(2,1)S(1)}, u32[]{:S(2)}, u32[]{:S(2)}) %collective-permute-start.12) | collective-permute-done | bytes 151584 | tf_op jit(solution)/shard_map/ppermute | solution.py:51
  40.0 2.6 %collective-permute-start.17 = (bf16[96,128]{1,0:T(8,128)(2,1)S(1)}, bf16[96,128]{1,0:T(8,128)(2,1)S(1)}, u32[]{:S(2)}, u32[]{:S(2)}) collective-permute-start(bf16[96,128]{1,0:T(8,128)(2,1)S(1)} %get-tuple-element.55.refs_0_), channel_id=1, source_target_pairs={{0,24},{1,7},{2,26},{3,5},{4,28},{5,3},{6,30},{7,1},{8,16},{9,15},... | collective-permute-start | bytes 73736 | tf_op jit(solution)/shard_map/ppermute | solution.py:51
  42.6 0.9 %collective-permute-start.16 = (bf16[96,128]{1,0:T(8,128)(2,1)S(1)}, bf16[96,128]{1,0:T(8,128)(2,1)S(1)}, u32[]{:S(2)}, u32[]{:S(2)}) collective-permute-start(bf16[96,128]{1,0:T(8,128)(2,1)S(1)} %get-tuple-element.55.refs_0_), channel_id=1, source_target_pairs={{0,16},{1,5},{2,18},{3,7},{4,20},{5,1},{6,22},{7,3},{8,24},{9,13},... | collective-permute-start | bytes 73736 | tf_op jit(solution)/shard_map/ppermute | solution.py:51
  43.5 0.8 %collective-permute-start.15 = (bf16[96,128]{1,0:T(8,128)(2,1)S(1)}, bf16[96,128]{1,0:T(8,128)(2,1)S(1)}, u32[]{:S(2)}, u32[]{:S(2)}) collective-permute-start(bf16[96,128]{1,0:T(8,128)(2,1)S(1)} %get-tuple-element.55.refs_0_), channel_id=1, source_target_pairs={{0,8},{1,3},{2,10},{3,1},{4,12},{5,7},{6,14},{7,5},{8,0},{9,11},{1... | collective-permute-start | bytes 73736 | tf_op jit(solution)/shard_map/ppermute | solution.py:51
  44.2 0.6 %collective-permute-done.17.refs_3_ = bf16[96,128]{1,0:T(8,128)(2,1)S(1)} collective-permute-done((bf16[96,128]{1,0:T(8,128)(2,1)S(1)}, bf16[96,128]{1,0:T(8,128)(2,1)S(1)}, u32[]{:S(2)}, u32[]{:S(2)}) %collective-permute-start.17) | collective-permute-done | bytes 24608 | tf_op jit(solution)/shard_map/ppermute | solution.py:51
  44.8 1.6 %collective-permute-done.16.refs_2_ = bf16[96,128]{1,0:T(8,128)(2,1)S(1)} collective-permute-done((bf16[96,128]{1,0:T(8,128)(2,1)S(1)}, bf16[96,128]{1,0:T(8,128)(2,1)S(1)}, u32[]{:S(2)}, u32[]{:S(2)}) %collective-permute-start.16) | collective-permute-done | bytes 24608 | tf_op jit(solution)/shard_map/ppermute | solution.py:51
  46.4 0.9 %collective-permute-done.15.refs_1_ = bf16[96,128]{1,0:T(8,128)(2,1)S(1)} collective-permute-done((bf16[96,128]{1,0:T(8,128)(2,1)S(1)}, bf16[96,128]{1,0:T(8,128)(2,1)S(1)}, u32[]{:S(2)}, u32[]{:S(2)}) %collective-permute-start.15) | collective-permute-done | bytes 24608 | tf_op jit(solution)/shard_map/ppermute | solution.py:51
  47.7 0.9 %collective-permute-done.18.got_ref = f32[80,128]{1,0:T(8,128)S(1)} collective-permute-done((f32[80,128]{1,0:T(8,128)S(1)}, f32[80,128]{1,0:T(8,128)S(1)}, u32[]{:S(2)}, u32[]{:S(2)}) %collective-permute-start.18) | collective-permute-done | bytes 40992 | tf_op jit(solution)/shard_map/ppermute | solution.py:25
  48.6 0.8 %shard_map.116 = (bf16[256,128]{1,0:T(8,128)(2,1)}, f32[128,128]{1,0:T(8,128)}) custom-call(f32[256,128]{1,0:T(8,128)S(1)} %shard_map.114.inner_ref, f32[592,128]{1,0:T(8,128)S(1)} %get-tuple-element.54.mine_ref, f32[592,128]{1,0:T(8,128)S(1)} %collective-permute-done.14.theirs_ref, f32[80,128]{1,0:T(8,128)S(1)} %shard_map.115.last_ref, ...), custom_call_target="tpu_custom_call" | custom-call | tf_op jit(solution)/shard_map/pallas_call | solution.py:557
  (29 shorter events, 3.7 us)
Async XLA Ops:
  1.6 9.4 %collective-permute-start = (bf16[16,128]{1,0:T(8,128)(2,1)S(1)}, bf16[16,128]{1,0:T(8,128)(2,1)S(1)}, u32[]{:S(2)}, u32[]{:S(2)}) collective-permute-start(bf16[16,128]{1,0:T(8,128)(2,1)S(1)} %get-tuple-element.30), channel_id=1, source_target_pairs={{1,2},{2,1},{3,4},{4,3},{5,6},{6,5},{7,8},{8,7},{9,10},{10,9},{11,... | collective-permute-start | bytes 12296 | tf_op jit(solution)/shard_map/ppermute | solution.py:33
  11.0 1.4 %collective-permute-start.1 = (bf16[512,128]{1,0:T(8,128)(2,1)S(1)}, bf16[512,128]{1,0:T(8,128)(2,1)S(1)}, u32[]{:S(2)}, u32[]{:S(2)}) collective-permute-start(bf16[512,128]{1,0:T(8,128)(2,1)S(1)} %get-tuple-element.32.body_ref), channel_id=1, source_target_pairs={{0,1},{1,0},{2,3},{3,2},{4,5},{5,4},{6,7},{7,6},{8,9},{9,8},{10,11... | collective-permute-start | bytes 393224 | tf_op jit(solution)/shard_map/ppermute | solution.py:25
  11.0 1.3 %collective-permute-start.2 = (bf16[16,128]{1,0:T(8,128)(2,1)S(1)}, bf16[16,128]{1,0:T(8,128)(2,1)S(1)}, u32[]{:S(2)}, u32[]{:S(2)}) collective-permute-start(bf16[16,128]{1,0:T(8,128)(2,1)S(1)} %collective-permute-done.far_ref), channel_id=1, source_target_pairs={{0,1},{1,0},{2,3},{3,2},{4,5},{5,4},{6,7},{7,6},{8,9},{9,8},{10,11... | collective-permute-start | bytes 12296 | tf_op jit(solution)/shard_map/ppermute | solution.py:25
  12.5 7.0 %collective-permute-start.5 = (bf16[512,128]{1,0:T(8,128)(2,1)S(1)}, bf16[512,128]{1,0:T(8,128)(2,1)S(1)}, u32[]{:S(2)}, u32[]{:S(2)}) collective-permute-start(bf16[512,128]{1,0:T(8,128)(2,1)S(1)} %shard_map.107.refs_3_), channel_id=1, source_target_pairs={{0,6},{1,25},{2,4},{3,27},{4,2},{5,29},{6,0},{7,31},{8,14},{9,17},... | collective-permute-start | bytes 393224 | tf_op jit(solution)/shard_map/ppermute | solution.py:51
  13.6 8.6 %collective-permute-start.4 = (bf16[512,128]{1,0:T(8,128)(2,1)S(1)}, bf16[512,128]{1,0:T(8,128)(2,1)S(1)}, u32[]{:S(2)}, u32[]{:S(2)}) collective-permute-start(bf16[512,128]{1,0:T(8,128)(2,1)S(1)} %shard_map.107.refs_3_), channel_id=1, source_target_pairs={{0,4},{1,17},{2,6},{3,19},{4,0},{5,21},{6,2},{7,23},{8,12},{9,25},... | collective-permute-start | bytes 393224 | tf_op jit(solution)/shard_map/ppermute | solution.py:51
  13.7 8.4 %collective-permute-start.3 = (bf16[512,128]{1,0:T(8,128)(2,1)S(1)}, bf16[512,128]{1,0:T(8,128)(2,1)S(1)}, u32[]{:S(2)}, u32[]{:S(2)}) collective-permute-start(bf16[512,128]{1,0:T(8,128)(2,1)S(1)} %shard_map.107.refs_3_), channel_id=1, source_target_pairs={{0,2},{1,9},{2,0},{3,11},{4,6},{5,13},{6,4},{7,15},{8,10},{9,1},{1... | collective-permute-start | bytes 393224 | tf_op jit(solution)/shard_map/ppermute | solution.py:51
  19.3 4.7 %copy-start = (bf16[128,128]{1,0:T(8,128)(2,1)S(1)}, bf16[128,128]{1,0:T(8,128)(2,1)}, u32[]{:S(2)}) copy-start(bf16[128,128]{1,0:T(8,128)(2,1)} %weight_ref.3) | copy-start | bytes 98308
  22.2 1.3 %collective-permute-start.6 = (bf16[512,128]{1,0:T(8,128)(2,1)S(1)}, bf16[512,128]{1,0:T(8,128)(2,1)S(1)}, u32[]{:S(2)}, u32[]{:S(2)}) collective-permute-start(bf16[512,128]{1,0:T(8,128)(2,1)S(1)} %collective-permute-done.3.refs_4_), channel_id=1, source_target_pairs={{0,1},{1,0},{2,3},{3,2},{4,5},{5,4},{6,7},{7,6},{8,9},{9,8},{10,11... | collective-permute-start | bytes 393224 | tf_op jit(solution)/shard_map/ppermute | solution.py:25
  22.2 1.5 %collective-permute-start.7 = (bf16[512,128]{1,0:T(8,128)(2,1)S(1)}, bf16[512,128]{1,0:T(8,128)(2,1)S(1)}, u32[]{:S(2)}, u32[]{:S(2)}) collective-permute-start(bf16[512,128]{1,0:T(8,128)(2,1)S(1)} %collective-permute-done.4.refs_5_), channel_id=1, source_target_pairs={{0,1},{1,0},{2,3},{3,2},{4,5},{5,4},{6,7},{7,6},{8,9},{9,8},{10,11... | collective-permute-start | bytes 393224 | tf_op jit(solution)/shard_map/ppermute | solution.py:25
  22.7 1.3 %collective-permute-start.8 = (bf16[512,128]{1,0:T(8,128)(2,1)S(1)}, bf16[512,128]{1,0:T(8,128)(2,1)S(1)}, u32[]{:S(2)}, u32[]{:S(2)}) collective-permute-start(bf16[512,128]{1,0:T(8,128)(2,1)S(1)} %collective-permute-done.5.refs_6_), channel_id=1, source_target_pairs={{0,1},{1,0},{2,3},{3,2},{4,5},{5,4},{6,7},{7,6},{8,9},{9,8},{10,11... | collective-permute-start | bytes 393224 | tf_op jit(solution)/shard_map/ppermute | solution.py:25
  28.2 2.0 %collective-permute-start.10 = (bf16[1168,128]{1,0:T(8,128)(2,1)S(1)}, bf16[1168,128]{1,0:T(8,128)(2,1)S(1)}, u32[]{:S(2)}, u32[]{:S(2)}) collective-permute-start(bf16[1168,128]{1,0:T(8,128)(2,1)S(1)} %get-tuple-element.49), channel_id=1, source_target_pairs={{0,1},{1,0},{2,3},{3,2},{4,5},{5,4},{6,7},{7,6},{8,9},{9,8},{10,11... | collective-permute-start | bytes 897032 | tf_op jit(solution)/shard_map/ppermute | solution.py:25
  28.4 1.8 %collective-permute-start.9 = (bf16[1024,128]{1,0:T(8,128)(2,1)S(1)}, bf16[1024,128]{1,0:T(8,128)(2,1)S(1)}, u32[]{:S(2)}, u32[]{:S(2)}) collective-permute-start(bf16[1024,128]{1,0:T(8,128)(2,1)S(1)} %get-tuple-element.48), channel_id=1, source_target_pairs={{0,1},{1,0},{2,3},{3,2},{4,5},{5,4},{6,7},{7,6},{8,9},{9,8},{10,11... | collective-permute-start | bytes 786440 | tf_op jit(solution)/shard_map/ppermute | solution.py:25
  30.3 6.7 %collective-permute-start.11 = (bf16[592,128]{1,0:T(8,128)(2,1)S(1)}, bf16[592,128]{1,0:T(8,128)(2,1)S(1)}, u32[]{:S(2)}, u32[]{:S(2)}) collective-permute-start(bf16[592,128]{1,0:T(8,128)(2,1)S(1)} %get-tuple-element.51), channel_id=1, source_target_pairs={{0,2},{1,9},{2,0},{3,11},{4,6},{5,13},{6,4},{7,15},{8,10},{9,1},{1... | collective-permute-start | bytes 454664 | tf_op jit(solution)/shard_map/ppermute | solution.py:51
  30.4 9.4 %collective-permute-start.12 = (bf16[592,128]{1,0:T(8,128)(2,1)S(1)}, bf16[592,128]{1,0:T(8,128)(2,1)S(1)}, u32[]{:S(2)}, u32[]{:S(2)}) collective-permute-start(bf16[592,128]{1,0:T(8,128)(2,1)S(1)} %get-tuple-element.52), channel_id=1, source_target_pairs={{0,4},{1,17},{2,6},{3,19},{4,0},{5,21},{6,2},{7,23},{8,12},{9,25},... | collective-permute-start | bytes 454664 | tf_op jit(solution)/shard_map/ppermute | solution.py:51
  32.2 7.7 %collective-permute-start.13 = (bf16[592,128]{1,0:T(8,128)(2,1)S(1)}, bf16[592,128]{1,0:T(8,128)(2,1)S(1)}, u32[]{:S(2)}, u32[]{:S(2)}) collective-permute-start(bf16[592,128]{1,0:T(8,128)(2,1)S(1)} %get-tuple-element.53), channel_id=1, source_target_pairs={{0,6},{1,25},{2,4},{3,27},{4,2},{5,29},{6,0},{7,31},{8,14},{9,17},... | collective-permute-start | bytes 454664 | tf_op jit(solution)/shard_map/ppermute | solution.py:51
  39.9 7.5 %collective-permute-start.14 = (f32[592,128]{1,0:T(8,128)S(1)}, f32[592,128]{1,0:T(8,128)S(1)}, u32[]{:S(2)}, u32[]{:S(2)}) collective-permute-start(f32[592,128]{1,0:T(8,128)S(1)} %get-tuple-element.54.mine_ref), channel_id=1, source_target_pairs={{0,1},{1,0},{2,3},{3,2},{4,5},{5,4},{6,7},{7,6},{8,9},{9,8},{10,11... | collective-permute-start | bytes 909320 | tf_op jit(solution)/shard_map/ppermute | solution.py:25
  40.0 4.8 %collective-permute-start.17 = (bf16[96,128]{1,0:T(8,128)(2,1)S(1)}, bf16[96,128]{1,0:T(8,128)(2,1)S(1)}, u32[]{:S(2)}, u32[]{:S(2)}) collective-permute-start(bf16[96,128]{1,0:T(8,128)(2,1)S(1)} %get-tuple-element.55.refs_0_), channel_id=1, source_target_pairs={{0,24},{1,7},{2,26},{3,5},{4,28},{5,3},{6,30},{7,1},{8,16},{9,15},... | collective-permute-start | bytes 73736 | tf_op jit(solution)/shard_map/ppermute | solution.py:51
  42.6 3.8 %collective-permute-start.16 = (bf16[96,128]{1,0:T(8,128)(2,1)S(1)}, bf16[96,128]{1,0:T(8,128)(2,1)S(1)}, u32[]{:S(2)}, u32[]{:S(2)}) collective-permute-start(bf16[96,128]{1,0:T(8,128)(2,1)S(1)} %get-tuple-element.55.refs_0_), channel_id=1, source_target_pairs={{0,16},{1,5},{2,18},{3,7},{4,20},{5,1},{6,22},{7,3},{8,24},{9,13},... | collective-permute-start | bytes 73736 | tf_op jit(solution)/shard_map/ppermute | solution.py:51
  43.5 3.8 %collective-permute-start.15 = (bf16[96,128]{1,0:T(8,128)(2,1)S(1)}, bf16[96,128]{1,0:T(8,128)(2,1)S(1)}, u32[]{:S(2)}, u32[]{:S(2)}) collective-permute-start(bf16[96,128]{1,0:T(8,128)(2,1)S(1)} %get-tuple-element.55.refs_0_), channel_id=1, source_target_pairs={{0,8},{1,3},{2,10},{3,1},{4,12},{5,7},{6,14},{7,5},{8,0},{9,11},{1... | collective-permute-start | bytes 73736 | tf_op jit(solution)/shard_map/ppermute | solution.py:51
  47.3 1.3 %collective-permute-start.18 = (f32[80,128]{1,0:T(8,128)S(1)}, f32[80,128]{1,0:T(8,128)S(1)}, u32[]{:S(2)}, u32[]{:S(2)}) collective-permute-start(f32[80,128]{1,0:T(8,128)S(1)} %shard_map.115.last_ref), channel_id=1, source_target_pairs={{0,1},{1,0},{2,3},{3,2},{4,5},{5,4},{6,7},{7,6},{8,9},{9,8},{10,11... | collective-permute-start | bytes 122888 | tf_op jit(solution)/shard_map/ppermute | solution.py:25

commit v6 on v5

--- a/solution.py
+++ b/solution.py
@@ -258,9 +258,8 @@
     recv = refs[4 : 4 + steps]
     other = refs[4 + steps : 4 + 2 * steps]
     refs = refs[4 + 2 * steps :]
-    drow_ref, early_ref, late_ref, grad_ref, row_agg, col_agg, row_z = refs[:7]
-    (col_z,) = refs[7:]
-    split = early_ref.shape[0]
+    drow_ref, grad_ref, row_agg, col_agg, row_z = refs[:5]
+    (col_z,) = refs[5:]
     pair = pair_ref.shape[0]
     shard = pair // 2
     columns = nrow * shard
@@ -296,15 +295,10 @@
                 grad_ref[row : row + BLOCK, cut] = part.astype(bf16)
         drow = dots(grad_ref[at, :], col_z[...], nn) * (1.0 / 32.0)
         drow_ref[at, :] = drow
-        low = k * pair
-        if low < split:
-            early_ref[at, :] = drow.astype(bf16)
-        else:
-            late_ref[low - split : low - split + pair, :] = drow.astype(bf16)
 
 
 def column_kernel(
-    nz, grad_ref, row_agg, col_agg, row_z, drow_ref, late_ref, dcol_ref, give_ref, share_ref
+    nz, grad_ref, row_agg, col_agg, row_z, drow_ref, dcol_ref, give_ref, share_ref
 ):
     dots = functools.partial(lax.dot_general, preferred_element_type=jnp.float32)
     nn = (((1,), (0,)), ((), ()))
@@ -335,7 +329,7 @@
         give_ref[body + width :, :] = jnp.concatenate(edge, axis=0).astype(bf16)
 
     def second():
-        give_ref[0 : late_ref.shape[0], :] = late_ref[...]
+        give_ref[0:rows, :] = drow_ref[...].astype(bf16)
         give_ref[body + width :, :] = jnp.zeros((16, share.shape[1]), bf16)
 
     parity(first, second)
@@ -346,11 +340,8 @@
     width = weight.shape[1]
     bf16, real = jnp.bfloat16, jnp.float32
     shape = jax.ShapeDtypeStruct
-    early = max(count // 2, 1)
     outs = [
         shape((rows, width), real),
-        shape((early * rows // count, width), bf16),
-        shape((max(count - early, 1) * rows // count, width), bf16),
         shape((rows, columns), bf16),
         shape((rows, width), bf16),
         shape((columns, width), bf16),
@@ -372,7 +363,7 @@
 
 
 def column_parts(nz, parts, width):
-    drow, early, late, grad, row_agg, col_agg, row_z = parts
+    drow, grad, row_agg, col_agg, row_z = parts
     rows, columns = grad.shape
     bf16, real = jnp.bfloat16, jnp.float32
     shape = jax.ShapeDtypeStruct
@@ -380,14 +371,14 @@
         functools.partial(column_kernel, nz),
         (
             shape((columns, width), real),
-            shape((max(columns, rows // 2) + width + 16, width), bf16),
+            shape((max(columns, rows) + width + 16, width), bf16),
             shape((width, width), real),
         ),
-        (grad, row_agg, col_agg, row_z, drow, late), 10,
-    )
-
-
-def merge_kernel(nz, nrow, drow_ref, dcol_ref, share_ref, early_ref, late_ref, *messages):
+        (grad, row_agg, col_agg, row_z, drow), 10,
+    )
+
+
+def merge_kernel(nz, nrow, drow_ref, dcol_ref, share_ref, late_ref, *messages):
     width = share_ref.shape[0]
     half = width // 2
     pair = messages[0].shape[0] - half - 16
@@ -397,12 +388,10 @@
     z = lax.axis_index("col") // 2
     spot = lax.broadcasted_iota(jnp.int32, (16, width), 0)
 
-    split = early_ref.shape[0]
     tail = late_ref.shape[0] - width - 16
 
     def rows_of_other(start, size):
-        ref, start = (early_ref, start) if start < split else (late_ref, start - split)
-        return ref[start : start + size, :].astype(real)
+        return late_ref[start : start + size, :].astype(real)
 
     def chip_row(k, low):
         row = 0 if low else pair - 1
@@ -606,22 +595,19 @@
     ]
     if pieces == 1:
         drow = outs[0][0]
-        early = swap(outs[0][1], "col", 1)
         dcol, late, share = column_parts(nz, outs[0], width)
     else:
         found = [column_parts(count, x, width) for x in outs]
         drow = jnp.concatenate([x[0] for x in outs], axis=0)
         dcol, share = (tree_sum([x[k] for x in found]) for k in (0, 2))
-        split = drow.shape[0] // 2
-        early = swap(drow[0:split].astype(bf16), "col", 1)
         z = lax.axis_index("col") // 2
         pair_rows = drow.shape[0] // nz
         top = lax.dynamic_slice_in_dim(drow, z * pair_rows, 8)
         bottom = jnp.bitwise_xor(z, nz - 1) * pair_rows + pair_rows - 8
         edge = jnp.concatenate([top, lax.dynamic_slice_in_dim(drow, bottom, 8)], axis=0)
-        long = max(dcol.shape[0], split)
+        long = max(dcol.shape[0], drow.shape[0])
         even = jnp.concatenate([dcol, jnp.zeros((long - dcol.shape[0], width), real)], axis=0)
-        odd = jnp.concatenate([drow[split:], jnp.zeros((long - split, width), real)], axis=0)
+        odd = jnp.concatenate([drow, jnp.zeros((long - drow.shape[0], width), real)], axis=0)
         late = jnp.where(lax.rem(lax.axis_index("col"), 2) == 0, even, odd)
         late = jnp.concatenate([late, share, edge], axis=0).astype(bf16)
     late = swap(late, "col", 1)
@@ -629,7 +615,7 @@
     messages = call(
         functools.partial(merge_kernel, nz, nrow),
         [shape((2 * shard + half + 16, width), bf16)] * steps,
-        (drow, dcol, share, early, late), 8,
+        (drow, dcol, share, late), 8,
     )
     arrived = [swap_mixed(messages[k], k) for k in range(steps - 1, 0, -1)]
     mine, on = call(

time: 49.4 us -> 49.9 us (1.010); the launches traced: 49.4 us -> 49.3 us
  Pallas kernels: 11.9 us -> 14.3 us
  waiting for transfers between devices: 14.7 us -> 12.4 us
    ppermute x9, waiting for transfers between devices: 11 us -> 8.37 us  [swap_mixed(): return lax.ppermute(x, AXES, pairs)]
    pallas_call x3, Pallas kernels: 5.07 us -> 7.43 us  [targets(): pl.pallas_call(functools.partial(target_kernel, at, base, blocks, cols, p...]
    ppermute x9 -> x8, waiting for transfers between devices: 3.76 us -> 4.03 us  [swap(): return lax.ppermute(x, axis, [(i, i ^ step) for i in range(count)])]
    ppermute x9 -> x8, starting transfers between devices: 1.8 us -> 1.52 us  [swap(): return lax.ppermute(x, axis, [(i, i ^ step) for i in range(count)])]
  transfers between devices with their start and end apart: 19 -> 18, of which waited for: 12 -> 11; matrix products, arithmetic and copies ran while one was open for 0% -> 0% of each run, Pallas kernels for 12% -> 16%
where the time goes in v6:
time: 49.9 us; the launch traced here: 49.3 us
  starting transfers between devices  21.2 us (42%)
  Pallas kernels  14.3 us (29%)
  waiting for transfers between devices  12.4 us (25%)
  between operations  1.43 us (3%)
    ppermute x9, starting transfers between devices, swap_mixed(): return lax.ppermute(x, AXES, pairs)  13.2 us
    ppermute x9, waiting for transfers between devices, swap_mixed(): return lax.ppermute(x, AXES, pairs)  8.37 us
    pallas_call x3, Pallas kernels, targets(): pl.pallas_call(functools.partial(target_kernel, at, base, blocks, cols, p...  7.43 us
    ppermute x1, starting transfers between devices, swap_next(): return lax.ppermute(x, AXES, pairs)  6.44 us
    ppermute x8, waiting for transfers between devices, swap(): return lax.ppermute(x, axis, [(i, i ^ step) for i in range(count)])  4.03 us
    pallas_call x1, Pallas kernels, decode(): pl.pallas_call(lambda *refs: decode_kernel(nz, nrow, first, count, refs),...  2.97 us
    pallas_call x7, Pallas kernels, call(): pl.pallas_call(kernel, out_shape=outs, in_specs=specs or [VMEM] * len(ope...  2.56 us
    ppermute x8, starting transfers between devices, swap(): return lax.ppermute(x, axis, [(i, i ^ step) for i in range(count)])  1.52 us
  transfers between devices with their start and end apart: 18, of which 11 were waited for; matrix products, arithmetic and copies ran while one was open for 0% of the time, Pallas kernels for 16%

profile of v6, /device:TPU:0, one launch (start us, length us, event | category | flops | bytes accessed | tf_op | source)
XLA Modules:
  0.0 49.3 jit_solution(6141080568543169757)
XLA Ops:
  0.6 0.9 %shard_map.104 = (bf16[512,128]{1,0:T(8,128)(2,1)S(1)}, s32[1,1408]{1,0:T(1,128)S(1)}, bf16[16,128]{1,0:T(8,128)(2,1)S(1)}) custom-call(bf16[256,128]{1,0:T(8,128)(2,1)} %features_hbm.1, s32[1,1,384]{2,1,0:T(1,128)} %rows.1, s32[1,1,384]{2,1,0:T(1,128)} %cols.1, s32[1,1,384]{2,1,0:T(1,128)} %keys.1, s32[1,1,128]{2,1,0:T(1,128)} %nrows.1, ...), custom_call_target="tpu_custom_call" | custom-call | tf_op jit(solution)/shard_map/pallas_call | solution.py:106
  1.6 6.4 %collective-permute-start = (bf16[16,128]{1,0:T(8,128)(2,1)S(1)}, bf16[16,128]{1,0:T(8,128)(2,1)S(1)}, u32[]{:S(2)}, u32[]{:S(2)}) collective-permute-start(bf16[16,128]{1,0:T(8,128)(2,1)S(1)} %get-tuple-element.28), channel_id=1, source_target_pairs={{1,2},{2,1},{3,4},{4,3},{5,6},{6,5},{7,8},{8,7},{9,10},{10,9},{11,... | collective-permute-start | bytes 12296 | tf_op jit(solution)/shard_map/ppermute | solution.py:33
  9.0 2.6 %shard_map.105.refs_0_ = f32[2048,1024]{1,0:T(8,128)S(1)} custom-call(s32[1,1408]{1,0:T(1,128)S(1)} %get-tuple-element.27.meta_s.meta_ref, s32[1,1]{1,0:T(1,128)S(6)} %copy.15.count_s), custom_call_target="tpu_custom_call" | custom-call | flops 25165824 | bytes 25165824 | tf_op jit(solution)/shard_map/pallas_call | solution.py:239
  11.7 0.5 %collective-permute-start.2 = (bf16[16,128]{1,0:T(8,128)(2,1)S(1)}, bf16[16,128]{1,0:T(8,128)(2,1)S(1)}, u32[]{:S(2)}, u32[]{:S(2)}) collective-permute-start(bf16[16,128]{1,0:T(8,128)(2,1)S(1)} %collective-permute-done.far_ref), channel_id=1, source_target_pairs={{0,1},{1,0},{2,3},{3,2},{4,5},{5,4},{6,7},{7,6},{8,9},{9,8},{10,11... | collective-permute-start | bytes 12296 | tf_op jit(solution)/shard_map/ppermute | solution.py:25
  12.2 0.8 %collective-permute-done.2.sib_far_ref = bf16[16,128]{1,0:T(8,128)(2,1)S(1)} collective-permute-done((bf16[16,128]{1,0:T(8,128)(2,1)S(1)}, bf16[16,128]{1,0:T(8,128)(2,1)S(1)}, u32[]{:S(2)}, u32[]{:S(2)}) %collective-permute-start.2) | collective-permute-done | bytes 4128 | tf_op jit(solution)/shard_map/ppermute | solution.py:25
  13.2 0.5 collective-permute-start.5
  13.7 4.0 %collective-permute-start.3 = (bf16[512,128]{1,0:T(8,128)(2,1)S(1)}, bf16[512,128]{1,0:T(8,128)(2,1)S(1)}, u32[]{:S(2)}, u32[]{:S(2)}) collective-permute-start(bf16[512,128]{1,0:T(8,128)(2,1)S(1)} %shard_map.107.refs_3_), channel_id=1, source_target_pairs={{0,2},{1,9},{2,0},{3,11},{4,6},{5,13},{6,4},{7,15},{8,10},{9,1},{1... | collective-permute-start | bytes 393224 | tf_op jit(solution)/shard_map/ppermute | solution.py:51
  17.6 4.0 %shard_map.108.refs_0_ = f32[2048,1024]{1,0:T(8,128)S(1)} custom-call(s32[1,1408]{1,0:T(1,128)S(1)} %get-tuple-element.27.meta_s.meta_ref, s32[1,1]{1,0:T(1,128)S(6)} %copy.15.count_s, f32[2048,1024]{1,0:T(8,128)S(1)} %shard_map.105.refs_0_), custom_call_target="tpu_custom_call", output_to_operand_aliasing={{}: (2, {})} | custom-call | flops 25165824 | bytes 25165824 | tf_op jit(solution)/shard_map/pallas_call | solution.py:239
  21.7 0.7 %collective-permute-done.4.refs_5_ = bf16[512,128]{1,0:T(8,128)(2,1)S(1)} collective-permute-done((bf16[512,128]{1,0:T(8,128)(2,1)S(1)}, bf16[512,128]{1,0:T(8,128)(2,1)S(1)}, u32[]{:S(2)}, u32[]{:S(2)}) %collective-permute-start.4) | collective-permute-done | bytes 131104 | tf_op jit(solution)/shard_map/ppermute | solution.py:51
  22.4 0.5 %collective-permute-start.7 = (bf16[512,128]{1,0:T(8,128)(2,1)S(1)}, bf16[512,128]{1,0:T(8,128)(2,1)S(1)}, u32[]{:S(2)}, u32[]{:S(2)}) collective-permute-start(bf16[512,128]{1,0:T(8,128)(2,1)S(1)} %collective-permute-done.4.refs_5_), channel_id=1, source_target_pairs={{0,1},{1,0},{2,3},{3,2},{4,5},{5,4},{6,7},{7,6},{8,9},{9,8},{10,11... | collective-permute-start | bytes 393224 | tf_op jit(solution)/shard_map/ppermute | solution.py:25
  22.9 0.8 %shard_map.109.refs_0_ = f32[2048,1024]{1,0:T(8,128)S(1)} custom-call(s32[1,1408]{1,0:T(1,128)S(1)} %get-tuple-element.27.meta_s.meta_ref, s32[1,1]{1,0:T(1,128)S(6)} %copy.15.count_s, f32[2048,1024]{1,0:T(8,128)S(1)} %shard_map.108.refs_0_), custom_call_target="tpu_custom_call", output_to_operand_aliasing={{}: (2, {})} | custom-call | flops 25165824 | bytes 25165824 | tf_op jit(solution)/shard_map/pallas_call | solution.py:239
  24.2 3.0 %shard_map.110 = (f32[2048,128]{1,0:T(8,128)S(1)}, bf16[2048,1024]{1,0:T(8,128)(2,1)S(1)}, bf16[2048,128]{1,0:T(8,128)(2,1)S(1)}, bf16[1024,128]{1,0:T(8,128)(2,1)S(1)}, bf16[2048,128]{1,0:T(8,128)(2,1)S(1)}) custom-call(f32[2048,1024]{1,0:T(8,128)S(1)} %shard_map.109.refs_0_, f32[16,1024]{1,0:T(8,128)S(1)} %shard_map.106.refs_1_, ...), custom_call_target="tpu_custom_call" | custom-call | flops 1073741824 | bytes 8388608 | tf_op jit(solution)/shard_map/pallas_call | solution.py:350
  27.2 1.2 %shard_map.111 = (f32[1024,128]{1,0:T(8,128)S(1)}, bf16[2192,128]{1,0:T(8,128)(2,1)S(1)}, f32[128,128]{1,0:T(8,128)S(1)}) custom-call(bf16[2048,1024]{1,0:T(8,128)(2,1)S(1)} %get-tuple-element.39.grad_ref, bf16[2048,128]{1,0:T(8,128)(2,1)S(1)} %get-tuple-element.40.row_agg, bf16[1024,128]{1,0:T(8,128)(2,1)S(1)} %get-tuple-element.41.col_agg, ...), custom_call_target="tpu_custom_call" | custom-call | tf_op jit(solution)/shard_map/pallas_call | solution.py:546
  28.7 1.7 %collective-permute-done.9.late_ref = bf16[2192,128]{1,0:T(8,128)(2,1)S(1)} collective-permute-done((bf16[2192,128]{1,0:T(8,128)(2,1)S(1)}, bf16[2192,128]{1,0:T(8,128)(2,1)S(1)}, u32[]{:S(2)}, u32[]{:S(2)}) %collective-permute-start.9) | collective-permute-done | bytes 561184 | tf_op jit(solution)/shard_map/ppermute | solution.py:25
  30.9 1.4 %collective-permute-start.11 = (bf16[592,128]{1,0:T(8,128)(2,1)S(1)}, bf16[592,128]{1,0:T(8,128)(2,1)S(1)}, u32[]{:S(2)}, u32[]{:S(2)}) collective-permute-start(bf16[592,128]{1,0:T(8,128)(2,1)S(1)} %get-tuple-element.48), channel_id=1, source_target_pairs={{0,4},{1,17},{2,6},{3,19},{4,0},{5,21},{6,2},{7,23},{8,12},{9,25},... | collective-permute-start | bytes 454664 | tf_op jit(solution)/shard_map/ppermute | solution.py:51
  32.3 2.7 %collective-permute-start.12 = (bf16[592,128]{1,0:T(8,128)(2,1)S(1)}, bf16[592,128]{1,0:T(8,128)(2,1)S(1)}, u32[]{:S(2)}, u32[]{:S(2)}) collective-permute-start(bf16[592,128]{1,0:T(8,128)(2,1)S(1)} %get-tuple-element.49), channel_id=1, source_target_pairs={{0,6},{1,25},{2,4},{3,27},{4,2},{5,29},{6,0},{7,31},{8,14},{9,17},... | collective-permute-start | bytes 454664 | tf_op jit(solution)/shard_map/ppermute | solution.py:51
  35.0 2.0 %collective-permute-done.10.refs_1_ = bf16[592,128]{1,0:T(8,128)(2,1)S(1)} collective-permute-done((bf16[592,128]{1,0:T(8,128)(2,1)S(1)}, bf16[592,128]{1,0:T(8,128)(2,1)S(1)}, u32[]{:S(2)}, u32[]{:S(2)}) %collective-permute-start.10) | collective-permute-done | bytes 151584 | tf_op jit(solution)/shard_map/ppermute | solution.py:51
  37.0 3.2 %collective-permute-done.11.refs_2_ = bf16[592,128]{1,0:T(8,128)(2,1)S(1)} collective-permute-done((bf16[592,128]{1,0:T(8,128)(2,1)S(1)}, bf16[592,128]{1,0:T(8,128)(2,1)S(1)}, u32[]{:S(2)}, u32[]{:S(2)}) %collective-permute-start.11) | collective-permute-done | bytes 151584 | tf_op jit(solution)/shard_map/ppermute | solution.py:51
  40.4 2.9 %collective-permute-start.16 = (bf16[96,128]{1,0:T(8,128)(2,1)S(1)}, bf16[96,128]{1,0:T(8,128)(2,1)S(1)}, u32[]{:S(2)}, u32[]{:S(2)}) collective-permute-start(bf16[96,128]{1,0:T(8,128)(2,1)S(1)} %get-tuple-element.51.refs_0_), channel_id=1, source_target_pairs={{0,24},{1,7},{2,26},{3,5},{4,28},{5,3},{6,30},{7,1},{8,16},{9,15},... | collective-permute-start | bytes 73736 | tf_op jit(solution)/shard_map/ppermute | solution.py:51
  43.3 1.4 %collective-permute-start.14 = (bf16[96,128]{1,0:T(8,128)(2,1)S(1)}, bf16[96,128]{1,0:T(8,128)(2,1)S(1)}, u32[]{:S(2)}, u32[]{:S(2)}) collective-permute-start(bf16[96,128]{1,0:T(8,128)(2,1)S(1)} %get-tuple-element.51.refs_0_), channel_id=1, source_target_pairs={{0,8},{1,3},{2,10},{3,1},{4,12},{5,7},{6,14},{7,5},{8,0},{9,11},{1... | collective-permute-start | bytes 73736 | tf_op jit(solution)/shard_map/ppermute | solution.py:51
  44.7 0.5 collective-permute-done.16.refs_3_
  45.2 1.9 %collective-permute-done.15.refs_2_ = bf16[96,128]{1,0:T(8,128)(2,1)S(1)} collective-permute-done((bf16[96,128]{1,0:T(8,128)(2,1)S(1)}, bf16[96,128]{1,0:T(8,128)(2,1)S(1)}, u32[]{:S(2)}, u32[]{:S(2)}) %collective-permute-start.15) | collective-permute-done | bytes 24608 | tf_op jit(solution)/shard_map/ppermute | solution.py:51
  47.5 0.9 %collective-permute-done.17.got_ref = f32[80,128]{1,0:T(8,128)S(1)} collective-permute-done((f32[80,128]{1,0:T(8,128)S(1)}, f32[80,128]{1,0:T(8,128)S(1)}, u32[]{:S(2)}, u32[]{:S(2)}) %collective-permute-start.17) | collective-permute-done | bytes 40992 | tf_op jit(solution)/shard_map/ppermute | solution.py:25
  48.5 0.8 %shard_map.116 = (bf16[256,128]{1,0:T(8,128)(2,1)}, f32[128,128]{1,0:T(8,128)}) custom-call(f32[256,128]{1,0:T(8,128)S(1)} %shard_map.114.inner_ref, f32[592,128]{1,0:T(8,128)S(1)} %get-tuple-element.50.mine_ref, f32[592,128]{1,0:T(8,128)S(1)} %collective-permute-done.13.theirs_ref, f32[80,128]{1,0:T(8,128)S(1)} %shard_map.115.last_ref, ...), custom_call_target="tpu_custom_call" | custom-call | tf_op jit(solution)/shard_map/pallas_call | solution.py:546
  (27 shorter events, 2.5 us)
Async XLA Ops:
  1.6 10.1 %collective-permute-start = (bf16[16,128]{1,0:T(8,128)(2,1)S(1)}, bf16[16,128]{1,0:T(8,128)(2,1)S(1)}, u32[]{:S(2)}, u32[]{:S(2)}) collective-permute-start(bf16[16,128]{1,0:T(8,128)(2,1)S(1)} %get-tuple-element.28), channel_id=1, source_target_pairs={{1,2},{2,1},{3,4},{4,3},{5,6},{6,5},{7,8},{8,7},{9,10},{10,9},{11,... | collective-permute-start | bytes 12296 | tf_op jit(solution)/shard_map/ppermute | solution.py:33
  11.6 1.4 %collective-permute-start.1 = (bf16[512,128]{1,0:T(8,128)(2,1)S(1)}, bf16[512,128]{1,0:T(8,128)(2,1)S(1)}, u32[]{:S(2)}, u32[]{:S(2)}) collective-permute-start(bf16[512,128]{1,0:T(8,128)(2,1)S(1)} %get-tuple-element.30.body_ref), channel_id=1, source_target_pairs={{0,1},{1,0},{2,3},{3,2},{4,5},{5,4},{6,7},{7,6},{8,9},{9,8},{10,11... | collective-permute-start | bytes 393224 | tf_op jit(solution)/shard_map/ppermute | solution.py:25
  11.7 1.3 %collective-permute-start.2 = (bf16[16,128]{1,0:T(8,128)(2,1)S(1)}, bf16[16,128]{1,0:T(8,128)(2,1)S(1)}, u32[]{:S(2)}, u32[]{:S(2)}) collective-permute-start(bf16[16,128]{1,0:T(8,128)(2,1)S(1)} %collective-permute-done.far_ref), channel_id=1, source_target_pairs={{0,1},{1,0},{2,3},{3,2},{4,5},{5,4},{6,7},{7,6},{8,9},{9,8},{10,11... | collective-permute-start | bytes 12296 | tf_op jit(solution)/shard_map/ppermute | solution.py:25
  13.2 8.5 %collective-permute-start.5 = (bf16[512,128]{1,0:T(8,128)(2,1)S(1)}, bf16[512,128]{1,0:T(8,128)(2,1)S(1)}, u32[]{:S(2)}, u32[]{:S(2)}) collective-permute-start(bf16[512,128]{1,0:T(8,128)(2,1)S(1)} %shard_map.107.refs_3_), channel_id=1, source_target_pairs={{0,6},{1,25},{2,4},{3,27},{4,2},{5,29},{6,0},{7,31},{8,14},{9,17},... | collective-permute-start | bytes 393224 | tf_op jit(solution)/shard_map/ppermute | solution.py:51
  13.7 8.7 %collective-permute-start.4 = (bf16[512,128]{1,0:T(8,128)(2,1)S(1)}, bf16[512,128]{1,0:T(8,128)(2,1)S(1)}, u32[]{:S(2)}, u32[]{:S(2)}) collective-permute-start(bf16[512,128]{1,0:T(8,128)(2,1)S(1)} %shard_map.107.refs_3_), channel_id=1, source_target_pairs={{0,4},{1,17},{2,6},{3,19},{4,0},{5,21},{6,2},{7,23},{8,12},{9,25},... | collective-permute-start | bytes 393224 | tf_op jit(solution)/shard_map/ppermute | solution.py:51
  13.7 8.7 %collective-permute-start.3 = (bf16[512,128]{1,0:T(8,128)(2,1)S(1)}, bf16[512,128]{1,0:T(8,128)(2,1)S(1)}, u32[]{:S(2)}, u32[]{:S(2)}) collective-permute-start(bf16[512,128]{1,0:T(8,128)(2,1)S(1)} %shard_map.107.refs_3_), channel_id=1, source_target_pairs={{0,2},{1,9},{2,0},{3,11},{4,6},{5,13},{6,4},{7,15},{8,10},{9,1},{1... | collective-permute-start | bytes 393224 | tf_op jit(solution)/shard_map/ppermute | solution.py:51
  21.7 2.6 %copy-start = (bf16[128,128]{1,0:T(8,128)(2,1)S(1)}, bf16[128,128]{1,0:T(8,128)(2,1)}, u32[]{:S(2)}) copy-start(bf16[128,128]{1,0:T(8,128)(2,1)} %weight_ref.3) | copy-start | bytes 98308
  22.4 1.3 %collective-permute-start.6 = (bf16[512,128]{1,0:T(8,128)(2,1)S(1)}, bf16[512,128]{1,0:T(8,128)(2,1)S(1)}, u32[]{:S(2)}, u32[]{:S(2)}) collective-permute-start(bf16[512,128]{1,0:T(8,128)(2,1)S(1)} %collective-permute-done.3.refs_4_), channel_id=1, source_target_pairs={{0,1},{1,0},{2,3},{3,2},{4,5},{5,4},{6,7},{7,6},{8,9},{9,8},{10,11... | collective-permute-start | bytes 393224 | tf_op jit(solution)/shard_map/ppermute | solution.py:25
  22.4 1.5 %collective-permute-start.7 = (bf16[512,128]{1,0:T(8,128)(2,1)S(1)}, bf16[512,128]{1,0:T(8,128)(2,1)S(1)}, u32[]{:S(2)}, u32[]{:S(2)}) collective-permute-start(bf16[512,128]{1,0:T(8,128)(2,1)S(1)} %collective-permute-done.4.refs_5_), channel_id=1, source_target_pairs={{0,1},{1,0},{2,3},{3,2},{4,5},{5,4},{6,7},{7,6},{8,9},{9,8},{10,11... | collective-permute-start | bytes 393224 | tf_op jit(solution)/shard_map/ppermute | solution.py:25
  22.9 1.3 %collective-permute-start.8 = (bf16[512,128]{1,0:T(8,128)(2,1)S(1)}, bf16[512,128]{1,0:T(8,128)(2,1)S(1)}, u32[]{:S(2)}, u32[]{:S(2)}) collective-permute-start(bf16[512,128]{1,0:T(8,128)(2,1)S(1)} %collective-permute-done.5.refs_6_), channel_id=1, source_target_pairs={{0,1},{1,0},{2,3},{3,2},{4,5},{5,4},{6,7},{7,6},{8,9},{9,8},{10,11... | collective-permute-start | bytes 393224 | tf_op jit(solution)/shard_map/ppermute | solution.py:25
  28.4 2.0 %collective-permute-start.9 = (bf16[2192,128]{1,0:T(8,128)(2,1)S(1)}, bf16[2192,128]{1,0:T(8,128)(2,1)S(1)}, u32[]{:S(2)}, u32[]{:S(2)}) collective-permute-start(bf16[2192,128]{1,0:T(8,128)(2,1)S(1)} %get-tuple-element.45), channel_id=1, source_target_pairs={{0,1},{1,0},{2,3},{3,2},{4,5},{5,4},{6,7},{7,6},{8,9},{9,8},{10,11... | collective-permute-start | bytes 1683464 | tf_op jit(solution)/shard_map/ppermute | solution.py:25
  30.5 6.5 %collective-permute-start.10 = (bf16[592,128]{1,0:T(8,128)(2,1)S(1)}, bf16[592,128]{1,0:T(8,128)(2,1)S(1)}, u32[]{:S(2)}, u32[]{:S(2)}) collective-permute-start(bf16[592,128]{1,0:T(8,128)(2,1)S(1)} %get-tuple-element.47), channel_id=1, source_target_pairs={{0,2},{1,9},{2,0},{3,11},{4,6},{5,13},{6,4},{7,15},{8,10},{9,1},{1... | collective-permute-start | bytes 454664 | tf_op jit(solution)/shard_map/ppermute | solution.py:51
  30.9 9.4 %collective-permute-start.11 = (bf16[592,128]{1,0:T(8,128)(2,1)S(1)}, bf16[592,128]{1,0:T(8,128)(2,1)S(1)}, u32[]{:S(2)}, u32[]{:S(2)}) collective-permute-start(bf16[592,128]{1,0:T(8,128)(2,1)S(1)} %get-tuple-element.48), channel_id=1, source_target_pairs={{0,4},{1,17},{2,6},{3,19},{4,0},{5,21},{6,2},{7,23},{8,12},{9,25},... | collective-permute-start | bytes 454664 | tf_op jit(solution)/shard_map/ppermute | solution.py:51
  32.3 8.0 %collective-permute-start.12 = (bf16[592,128]{1,0:T(8,128)(2,1)S(1)}, bf16[592,128]{1,0:T(8,128)(2,1)S(1)}, u32[]{:S(2)}, u32[]{:S(2)}) collective-permute-start(bf16[592,128]{1,0:T(8,128)(2,1)S(1)} %get-tuple-element.49), channel_id=1, source_target_pairs={{0,6},{1,25},{2,4},{3,27},{4,2},{5,29},{6,0},{7,31},{8,14},{9,17},... | collective-permute-start | bytes 454664 | tf_op jit(solution)/shard_map/ppermute | solution.py:51
  40.3 7.0 %collective-permute-start.13 = (f32[592,128]{1,0:T(8,128)S(1)}, f32[592,128]{1,0:T(8,128)S(1)}, u32[]{:S(2)}, u32[]{:S(2)}) collective-permute-start(f32[592,128]{1,0:T(8,128)S(1)} %get-tuple-element.50.mine_ref), channel_id=1, source_target_pairs={{0,1},{1,0},{2,3},{3,2},{4,5},{5,4},{6,7},{7,6},{8,9},{9,8},{10,11... | collective-permute-start | bytes 909320 | tf_op jit(solution)/shard_map/ppermute | solution.py:25
  40.4 4.8 %collective-permute-start.16 = (bf16[96,128]{1,0:T(8,128)(2,1)S(1)}, bf16[96,128]{1,0:T(8,128)(2,1)S(1)}, u32[]{:S(2)}, u32[]{:S(2)}) collective-permute-start(bf16[96,128]{1,0:T(8,128)(2,1)S(1)} %get-tuple-element.51.refs_0_), channel_id=1, source_target_pairs={{0,24},{1,7},{2,26},{3,5},{4,28},{5,3},{6,30},{7,1},{8,16},{9,15},... | collective-permute-start | bytes 73736 | tf_op jit(solution)/shard_map/ppermute | solution.py:51
  43.3 3.8 %collective-permute-start.15 = (bf16[96,128]{1,0:T(8,128)(2,1)S(1)}, bf16[96,128]{1,0:T(8,128)(2,1)S(1)}, u32[]{:S(2)}, u32[]{:S(2)}) collective-permute-start(bf16[96,128]{1,0:T(8,128)(2,1)S(1)} %get-tuple-element.51.refs_0_), channel_id=1, source_target_pairs={{0,16},{1,5},{2,18},{3,7},{4,20},{5,1},{6,22},{7,3},{8,24},{9,13},... | collective-permute-start | bytes 73736 | tf_op jit(solution)/shard_map/ppermute | solution.py:51
  43.3 3.8 %collective-permute-start.14 = (bf16[96,128]{1,0:T(8,128)(2,1)S(1)}, bf16[96,128]{1,0:T(8,128)(2,1)S(1)}, u32[]{:S(2)}, u32[]{:S(2)}) collective-permute-start(bf16[96,128]{1,0:T(8,128)(2,1)S(1)} %get-tuple-element.51.refs_0_), channel_id=1, source_target_pairs={{0,8},{1,3},{2,10},{3,1},{4,12},{5,7},{6,14},{7,5},{8,0},{9,11},{1... | collective-permute-start | bytes 73736 | tf_op jit(solution)/shard_map/ppermute | solution.py:51
  47.2 1.3 %collective-permute-start.17 = (f32[80,128]{1,0:T(8,128)S(1)}, f32[80,128]{1,0:T(8,128)S(1)}, u32[]{:S(2)}, u32[]{:S(2)}) collective-permute-start(f32[80,128]{1,0:T(8,128)S(1)} %shard_map.115.last_ref), channel_id=1, source_target_pairs={{0,1},{1,0},{2,3},{3,2},{4,5},{5,4},{6,7},{7,6},{8,9},{9,8},{10,11... | collective-permute-start | bytes 122888 | tf_op jit(solution)/shard_map/ppermute | solution.py:25

commit v7 on v5

--- a/solution.py
+++ b/solution.py
@@ -295,7 +295,7 @@
                 part = n * curve[i * BLOCK : (i + 1) * BLOCK] + (n - tile)
                 grad_ref[row : row + BLOCK, cut] = part.astype(bf16)
         drow = dots(grad_ref[at, :], col_z[...], nn) * (1.0 / 32.0)
-        drow_ref[at, :] = drow
+        drow_ref[at, :] = drow.astype(bf16)
         low = k * pair
         if low < split:
             early_ref[at, :] = drow.astype(bf16)
@@ -317,7 +317,7 @@
         cut = slice(c, c + step)
         dcol = dots(row_t, grad_ref[:, cut], nn).T * (1.0 / 32.0)
         dcol_ref[cut, :] = dcol
-    share = dots(row_agg[...], drow_ref[...].astype(bf16), tn)
+    share = dots(row_agg[...], drow_ref[...], tn)
     share += dots(col_agg[...], dcol_ref[...].astype(bf16), tn)
     share_ref[...] = share
     width = share.shape[0]
@@ -329,9 +329,10 @@
 
     def first():
         give_ref[0:columns, :] = dcol_ref[...].astype(bf16)
-        top = pl.multiple_of(z * pair, 8)
-        bottom = pl.multiple_of(jnp.bitwise_xor(z, nz - 1) * pair + pair - 8, 8)
-        edge = [drow_ref[pl.ds(top, 8), :], drow_ref[pl.ds(bottom, 8), :]]
+        top = pl.multiple_of(z * pair, 16)
+        bottom = pl.multiple_of(jnp.bitwise_xor(z, nz - 1) * pair + pair - 16, 16)
+        edge = [drow_ref[pl.ds(top, 16), :], drow_ref[pl.ds(bottom, 16), :]]
+        edge = [edge[0].astype(jnp.float32)[0:8], edge[1].astype(jnp.float32)[8:16]]
         give_ref[body + width :, :] = jnp.concatenate(edge, axis=0).astype(bf16)
 
     def second():
@@ -348,7 +349,7 @@
     shape = jax.ShapeDtypeStruct
     early = max(count // 2, 1)
     outs = [
-        shape((rows, width), real),
+        shape((rows, width), bf16),
         shape((early * rows // count, width), bf16),
         shape((max(count - early, 1) * rows // count, width), bf16),
         shape((rows, columns), bf16),
@@ -410,7 +411,7 @@
         for t in range(nz):
             near = t * pair + (0 if low else pair - 16)
             at = row % 16 if not low else 0
-            value = drow_ref[near : near + 16, :] + rows_of_other(near, 16)
+            value = drow_ref[near : near + 16, :].astype(real) + rows_of_other(near, 16)
             found = jnp.where(k == t, value[at : at + 1], found)
         return found
 
@@ -425,7 +426,7 @@
         for k in range(len(messages)):
             if k < nz:
                 at = slice(k * pair, (k + 1) * pair)
-                total = drow_ref[at, :] + rows_of_other(k * pair, pair)
+                total = drow_ref[at, :].astype(real) + rows_of_other(k * pair, pair)
                 messages[k][0:pair, :] = total.astype(bf16)
             to = jnp.bitwise_xor(z, k)
             prev = jnp.bitwise_xor(jnp.maximum(to - 1, 0), z)
@@ -439,10 +440,10 @@
     def columns():
         share = share_ref[half:, :] + late_ref[tail + half : tail + width, :].astype(real)
         edge = late_ref[tail + width :, :].astype(real)
-        top = pl.multiple_of(z * pair, 8)
-        bottom = pl.multiple_of(jnp.bitwise_xor(z, nz - 1) * pair + pair - 8, 8)
-        first = drow_ref[pl.ds(top, 8), :][0:1] + edge[0:1]
-        last = drow_ref[pl.ds(bottom, 8), :][7:8] + edge[15:16]
+        top = pl.multiple_of(z * pair, 16)
+        bottom = pl.multiple_of(jnp.bitwise_xor(z, nz - 1) * pair + pair - 16, 16)
+        first = drow_ref[pl.ds(top, 16), :].astype(real)[0:1] + edge[0:1]
+        last = drow_ref[pl.ds(bottom, 16), :].astype(real)[15:16] + edge[15:16]
         for q in range(len(messages)):
             if q < nrow:
                 at = slice(q * shard, (q + 1) * shard)

time: 49.4 us -> 49.6 us (level)
  starting transfers between devices: 21.3 us -> 20.7 us
    ppermute x9, starting transfers between devices: 13.1 us -> 12.5 us  [swap_mixed(): return lax.ppermute(x, AXES, pairs)]
  transfers between devices with their start and end apart: 19 -> 19, of which waited for: 12 -> 11; matrix products, arithmetic and copies ran while one was open for 0% -> 0% of each run, Pallas kernels for 12% -> 12%
where the time goes in v7:
time: 49.6 us; the launch traced here: 49.3 us
  starting transfers between devices  20.7 us (42%)
  waiting for transfers between devices  15.1 us (30%)
  Pallas kernels  12.1 us (24%)
  between operations  1.43 us (3%)
    ppermute x9, starting transfers between devices, swap_mixed(): return lax.ppermute(x, AXES, pairs)  12.5 us
    ppermute x9, waiting for transfers between devices, swap_mixed(): return lax.ppermute(x, AXES, pairs)  11.3 us
    ppermute x1, starting transfers between devices, swap_next(): return lax.ppermute(x, AXES, pairs)  6.44 us
    pallas_call x3, Pallas kernels, targets(): pl.pallas_call(functools.partial(target_kernel, at, base, blocks, cols, p...  5.25 us
    ppermute x9, waiting for transfers between devices, swap(): return lax.ppermute(x, axis, [(i, i ^ step) for i in range(count)])  3.76 us
    pallas_call x1, Pallas kernels, decode(): pl.pallas_call(lambda *refs: decode_kernel(nz, nrow, first, count, refs),...  2.98 us
    pallas_call x7, Pallas kernels, call(): pl.pallas_call(kernel, out_shape=outs, in_specs=specs or [VMEM] * len(ope...  2.6 us
    ppermute x9, starting transfers between devices, swap(): return lax.ppermute(x, axis, [(i, i ^ step) for i in range(count)])  1.8 us
  transfers between devices with their start and end apart: 19, of which 11 were waited for; matrix products, arithmetic and copies ran while one was open for 0% of the time, Pallas kernels for 12%

profile of v7, /device:TPU:0, one launch (start us, length us, event | category | flops | bytes accessed | tf_op | source)
XLA Modules:
  0.0 49.3 jit_solution(10488698249315795068)
XLA Ops:
  0.6 0.9 %shard_map.104 = (bf16[512,128]{1,0:T(8,128)(2,1)S(1)}, s32[1,1408]{1,0:T(1,128)S(1)}, bf16[16,128]{1,0:T(8,128)(2,1)S(1)}) custom-call(bf16[256,128]{1,0:T(8,128)(2,1)} %features_hbm.1, s32[1,1,384]{2,1,0:T(1,128)} %rows.1, s32[1,1,384]{2,1,0:T(1,128)} %cols.1, s32[1,1,384]{2,1,0:T(1,128)} %keys.1, s32[1,1,128]{2,1,0:T(1,128)} %nrows.1, ...), custom_call_target="tpu_custom_call" | custom-call | tf_op jit(solution)/shard_map/pallas_call | solution.py:106
  1.6 6.4 %collective-permute-start = (bf16[16,128]{1,0:T(8,128)(2,1)S(1)}, bf16[16,128]{1,0:T(8,128)(2,1)S(1)}, u32[]{:S(2)}, u32[]{:S(2)}) collective-permute-start(bf16[16,128]{1,0:T(8,128)(2,1)S(1)} %get-tuple-element.30), channel_id=1, source_target_pairs={{1,2},{2,1},{3,4},{4,3},{5,6},{6,5},{7,8},{8,7},{9,10},{10,9},{11,... | collective-permute-start | bytes 12296 | tf_op jit(solution)/shard_map/ppermute | solution.py:33
  9.0 1.9 %shard_map.105.refs_0_ = f32[2048,1024]{1,0:T(8,128)S(1)} custom-call(s32[1,1408]{1,0:T(1,128)S(1)} %get-tuple-element.29.meta_s.meta_ref, s32[1,1]{1,0:T(1,128)S(6)} %copy.15.count_s), custom_call_target="tpu_custom_call" | custom-call | flops 25165824 | bytes 25165824 | tf_op jit(solution)/shard_map/pallas_call | solution.py:239
  11.5 0.8 %collective-permute-done.2.sib_far_ref = bf16[16,128]{1,0:T(8,128)(2,1)S(1)} collective-permute-done((bf16[16,128]{1,0:T(8,128)(2,1)S(1)}, bf16[16,128]{1,0:T(8,128)(2,1)S(1)}, u32[]{:S(2)}, u32[]{:S(2)}) %collective-permute-start.2) | collective-permute-done | bytes 4128 | tf_op jit(solution)/shard_map/ppermute | solution.py:25
  12.5 1.1 %collective-permute-start.5 = (bf16[512,128]{1,0:T(8,128)(2,1)S(1)}, bf16[512,128]{1,0:T(8,128)(2,1)S(1)}, u32[]{:S(2)}, u32[]{:S(2)}) collective-permute-start(bf16[512,128]{1,0:T(8,128)(2,1)S(1)} %shard_map.107.refs_3_), channel_id=1, source_target_pairs={{0,6},{1,25},{2,4},{3,27},{4,2},{5,29},{6,0},{7,31},{8,14},{9,17},... | collective-permute-start | bytes 393224 | tf_op jit(solution)/shard_map/ppermute | solution.py:51
  13.6 3.4 %collective-permute-start.3 = (bf16[512,128]{1,0:T(8,128)(2,1)S(1)}, bf16[512,128]{1,0:T(8,128)(2,1)S(1)}, u32[]{:S(2)}, u32[]{:S(2)}) collective-permute-start(bf16[512,128]{1,0:T(8,128)(2,1)S(1)} %shard_map.107.refs_3_), channel_id=1, source_target_pairs={{0,2},{1,9},{2,0},{3,11},{4,6},{5,13},{6,4},{7,15},{8,10},{9,1},{1... | collective-permute-start | bytes 393224 | tf_op jit(solution)/shard_map/ppermute | solution.py:51
  17.0 2.5 %shard_map.108.refs_0_ = f32[2048,1024]{1,0:T(8,128)S(1)} custom-call(s32[1,1408]{1,0:T(1,128)S(1)} %get-tuple-element.29.meta_s.meta_ref, s32[1,1]{1,0:T(1,128)S(6)} %copy.15.count_s, f32[2048,1024]{1,0:T(8,128)S(1)} %shard_map.105.refs_0_), custom_call_target="tpu_custom_call", output_to_operand_aliasing={{}: (2, {})} | custom-call | flops 25165824 | bytes 25165824 | tf_op jit(solution)/shard_map/pallas_call | solution.py:239
  19.5 2.6 %collective-permute-done.4.refs_5_ = bf16[512,128]{1,0:T(8,128)(2,1)S(1)} collective-permute-done((bf16[512,128]{1,0:T(8,128)(2,1)S(1)}, bf16[512,128]{1,0:T(8,128)(2,1)S(1)}, u32[]{:S(2)}, u32[]{:S(2)}) %collective-permute-start.4) | collective-permute-done | bytes 131104 | tf_op jit(solution)/shard_map/ppermute | solution.py:51
  22.2 0.5 %collective-permute-start.7 = (bf16[512,128]{1,0:T(8,128)(2,1)S(1)}, bf16[512,128]{1,0:T(8,128)(2,1)S(1)}, u32[]{:S(2)}, u32[]{:S(2)}) collective-permute-start(bf16[512,128]{1,0:T(8,128)(2,1)S(1)} %collective-permute-done.4.refs_5_), channel_id=1, source_target_pairs={{0,1},{1,0},{2,3},{3,2},{4,5},{5,4},{6,7},{7,6},{8,9},{9,8},{10,11... | collective-permute-start | bytes 393224 | tf_op jit(solution)/shard_map/ppermute | solution.py:25
  22.7 0.8 %shard_map.109.refs_0_ = f32[2048,1024]{1,0:T(8,128)S(1)} custom-call(s32[1,1408]{1,0:T(1,128)S(1)} %get-tuple-element.29.meta_s.meta_ref, s32[1,1]{1,0:T(1,128)S(6)} %copy.15.count_s, f32[2048,1024]{1,0:T(8,128)S(1)} %shard_map.108.refs_0_), custom_call_target="tpu_custom_call", output_to_operand_aliasing={{}: (2, {})} | custom-call | flops 25165824 | bytes 25165824 | tf_op jit(solution)/shard_map/pallas_call | solution.py:239
  24.0 3.0 %shard_map.110 = (bf16[2048,128]{1,0:T(8,128)(2,1)S(1)}, bf16[1024,128]{1,0:T(8,128)(2,1)S(1)}, bf16[1024,128]{1,0:T(8,128)(2,1)S(1)}, bf16[2048,1024]{1,0:T(8,1...) custom-call(f32[2048,1024]{1,0:T(8,128)S(1)} %shard_map.109.refs_0_, ...), custom_call_target="tpu_custom_call" | custom-call | flops 1073741824 | bytes 8388608 | tf_op jit(solution)/shard_map/pallas_call | solution.py:360
  27.0 1.2 %shard_map.111 = (f32[1024,128]{1,0:T(8,128)S(1)}, bf16[1168,128]{1,0:T(8,128)(2,1)S(1)}, f32[128,128]{1,0:T(8,128)S(1)}) custom-call(bf16[2048,1024]{1,0:T(8,128)(2,1)S(1)} %get-tuple-element.41.grad_ref, bf16[2048,128]{1,0:T(8,128)(2,1)S(1)} %get-tuple-element.42.row_agg, bf16[1024,128]{1,0:T(8,128)(2,1)S(1)} %get-tuple-element.43.col_agg, ...), custom_call_target="tpu_custom_call" | custom-call | tf_op jit(solution)/shard_map/pallas_call | solution.py:558
  28.8 1.5 %collective-permute-done.9.early_ref = bf16[1024,128]{1,0:T(8,128)(2,1)S(1)} collective-permute-done((bf16[1024,128]{1,0:T(8,128)(2,1)S(1)}, bf16[1024,128]{1,0:T(8,128)(2,1)S(1)}, u32[]{:S(2)}, u32[]{:S(2)}) %collective-permute-start.9) | collective-permute-done | bytes 262176 | tf_op jit(solution)/shard_map/ppermute | solution.py:25
  30.5 1.6 %collective-permute-start.12 = (bf16[592,128]{1,0:T(8,128)(2,1)S(1)}, bf16[592,128]{1,0:T(8,128)(2,1)S(1)}, u32[]{:S(2)}, u32[]{:S(2)}) collective-permute-start(bf16[592,128]{1,0:T(8,128)(2,1)S(1)} %get-tuple-element.52), channel_id=1, source_target_pairs={{0,4},{1,17},{2,6},{3,19},{4,0},{5,21},{6,2},{7,23},{8,12},{9,25},... | collective-permute-start | bytes 454664 | tf_op jit(solution)/shard_map/ppermute | solution.py:51
  32.0 2.8 %collective-permute-start.13 = (bf16[592,128]{1,0:T(8,128)(2,1)S(1)}, bf16[592,128]{1,0:T(8,128)(2,1)S(1)}, u32[]{:S(2)}, u32[]{:S(2)}) collective-permute-start(bf16[592,128]{1,0:T(8,128)(2,1)S(1)} %get-tuple-element.53), channel_id=1, source_target_pairs={{0,6},{1,25},{2,4},{3,27},{4,2},{5,29},{6,0},{7,31},{8,14},{9,17},... | collective-permute-start | bytes 454664 | tf_op jit(solution)/shard_map/ppermute | solution.py:51
  34.8 2.2 %collective-permute-done.11.refs_1_ = bf16[592,128]{1,0:T(8,128)(2,1)S(1)} collective-permute-done((bf16[592,128]{1,0:T(8,128)(2,1)S(1)}, bf16[592,128]{1,0:T(8,128)(2,1)S(1)}, u32[]{:S(2)}, u32[]{:S(2)}) %collective-permute-start.11) | collective-permute-done | bytes 151584 | tf_op jit(solution)/shard_map/ppermute | solution.py:51
  37.1 2.8 %collective-permute-done.12.refs_2_ = bf16[592,128]{1,0:T(8,128)(2,1)S(1)} collective-permute-done((bf16[592,128]{1,0:T(8,128)(2,1)S(1)}, bf16[592,128]{1,0:T(8,128)(2,1)S(1)}, u32[]{:S(2)}, u32[]{:S(2)}) %collective-permute-start.12) | collective-permute-done | bytes 151584 | tf_op jit(solution)/shard_map/ppermute | solution.py:51
  40.1 2.5 %collective-permute-start.17 = (bf16[96,128]{1,0:T(8,128)(2,1)S(1)}, bf16[96,128]{1,0:T(8,128)(2,1)S(1)}, u32[]{:S(2)}, u32[]{:S(2)}) collective-permute-start(bf16[96,128]{1,0:T(8,128)(2,1)S(1)} %get-tuple-element.55.refs_0_), channel_id=1, source_target_pairs={{0,24},{1,7},{2,26},{3,5},{4,28},{5,3},{6,30},{7,1},{8,16},{9,15},... | collective-permute-start | bytes 73736 | tf_op jit(solution)/shard_map/ppermute | solution.py:51
  42.6 0.7 %collective-permute-start.16 = (bf16[96,128]{1,0:T(8,128)(2,1)S(1)}, bf16[96,128]{1,0:T(8,128)(2,1)S(1)}, u32[]{:S(2)}, u32[]{:S(2)}) collective-permute-start(bf16[96,128]{1,0:T(8,128)(2,1)S(1)} %get-tuple-element.55.refs_0_), channel_id=1, source_target_pairs={{0,16},{1,5},{2,18},{3,7},{4,20},{5,1},{6,22},{7,3},{8,24},{9,13},... | collective-permute-start | bytes 73736 | tf_op jit(solution)/shard_map/ppermute | solution.py:51
  43.6 1.2 %collective-permute-done.17.refs_3_ = bf16[96,128]{1,0:T(8,128)(2,1)S(1)} collective-permute-done((bf16[96,128]{1,0:T(8,128)(2,1)S(1)}, bf16[96,128]{1,0:T(8,128)(2,1)S(1)}, u32[]{:S(2)}, u32[]{:S(2)}) %collective-permute-start.17) | collective-permute-done | bytes 24608 | tf_op jit(solution)/shard_map/ppermute | solution.py:51
  44.9 1.6 %collective-permute-done.16.refs_2_ = bf16[96,128]{1,0:T(8,128)(2,1)S(1)} collective-permute-done((bf16[96,128]{1,0:T(8,128)(2,1)S(1)}, bf16[96,128]{1,0:T(8,128)(2,1)S(1)}, u32[]{:S(2)}, u32[]{:S(2)}) %collective-permute-start.16) | collective-permute-done | bytes 24608 | tf_op jit(solution)/shard_map/ppermute | solution.py:51
  46.4 0.7 %collective-permute-done.15.refs_1_ = bf16[96,128]{1,0:T(8,128)(2,1)S(1)} collective-permute-done((bf16[96,128]{1,0:T(8,128)(2,1)S(1)}, bf16[96,128]{1,0:T(8,128)(2,1)S(1)}, u32[]{:S(2)}, u32[]{:S(2)}) %collective-permute-start.15) | collective-permute-done | bytes 24608 | tf_op jit(solution)/shard_map/ppermute | solution.py:51
  47.6 0.9 %collective-permute-done.18.got_ref = f32[80,128]{1,0:T(8,128)S(1)} collective-permute-done((f32[80,128]{1,0:T(8,128)S(1)}, f32[80,128]{1,0:T(8,128)S(1)}, u32[]{:S(2)}, u32[]{:S(2)}) %collective-permute-start.18) | collective-permute-done | bytes 40992 | tf_op jit(solution)/shard_map/ppermute | solution.py:25
  48.5 0.8 %shard_map.116 = (bf16[256,128]{1,0:T(8,128)(2,1)}, f32[128,128]{1,0:T(8,128)}) custom-call(f32[256,128]{1,0:T(8,128)S(1)} %shard_map.114.inner_ref, f32[592,128]{1,0:T(8,128)S(1)} %get-tuple-element.54.mine_ref, f32[592,128]{1,0:T(8,128)S(1)} %collective-permute-done.14.theirs_ref, f32[80,128]{1,0:T(8,128)S(1)} %shard_map.115.last_ref, ...), custom_call_target="tpu_custom_call" | custom-call | tf_op jit(solution)/shard_map/pallas_call | solution.py:558
  (29 shorter events, 3.2 us)
Async XLA Ops:
  1.6 9.4 %collective-permute-start = (bf16[16,128]{1,0:T(8,128)(2,1)S(1)}, bf16[16,128]{1,0:T(8,128)(2,1)S(1)}, u32[]{:S(2)}, u32[]{:S(2)}) collective-permute-start(bf16[16,128]{1,0:T(8,128)(2,1)S(1)} %get-tuple-element.30), channel_id=1, source_target_pairs={{1,2},{2,1},{3,4},{4,3},{5,6},{6,5},{7,8},{8,7},{9,10},{10,9},{11,... | collective-permute-start | bytes 12296 | tf_op jit(solution)/shard_map/ppermute | solution.py:33
  11.0 1.4 %collective-permute-start.1 = (bf16[512,128]{1,0:T(8,128)(2,1)S(1)}, bf16[512,128]{1,0:T(8,128)(2,1)S(1)}, u32[]{:S(2)}, u32[]{:S(2)}) collective-permute-start(bf16[512,128]{1,0:T(8,128)(2,1)S(1)} %get-tuple-element.32.body_ref), channel_id=1, source_target_pairs={{0,1},{1,0},{2,3},{3,2},{4,5},{5,4},{6,7},{7,6},{8,9},{9,8},{10,11... | collective-permute-start | bytes 393224 | tf_op jit(solution)/shard_map/ppermute | solution.py:25
  11.0 1.3 %collective-permute-start.2 = (bf16[16,128]{1,0:T(8,128)(2,1)S(1)}, bf16[16,128]{1,0:T(8,128)(2,1)S(1)}, u32[]{:S(2)}, u32[]{:S(2)}) collective-permute-start(bf16[16,128]{1,0:T(8,128)(2,1)S(1)} %collective-permute-done.far_ref), channel_id=1, source_target_pairs={{0,1},{1,0},{2,3},{3,2},{4,5},{5,4},{6,7},{7,6},{8,9},{9,8},{10,11... | collective-permute-start | bytes 12296 | tf_op jit(solution)/shard_map/ppermute | solution.py:25
  12.5 7.0 %collective-permute-start.5 = (bf16[512,128]{1,0:T(8,128)(2,1)S(1)}, bf16[512,128]{1,0:T(8,128)(2,1)S(1)}, u32[]{:S(2)}, u32[]{:S(2)}) collective-permute-start(bf16[512,128]{1,0:T(8,128)(2,1)S(1)} %shard_map.107.refs_3_), channel_id=1, source_target_pairs={{0,6},{1,25},{2,4},{3,27},{4,2},{5,29},{6,0},{7,31},{8,14},{9,17},... | collective-permute-start | bytes 393224 | tf_op jit(solution)/shard_map/ppermute | solution.py:51
  13.6 8.6 %collective-permute-start.4 = (bf16[512,128]{1,0:T(8,128)(2,1)S(1)}, bf16[512,128]{1,0:T(8,128)(2,1)S(1)}, u32[]{:S(2)}, u32[]{:S(2)}) collective-permute-start(bf16[512,128]{1,0:T(8,128)(2,1)S(1)} %shard_map.107.refs_3_), channel_id=1, source_target_pairs={{0,4},{1,17},{2,6},{3,19},{4,0},{5,21},{6,2},{7,23},{8,12},{9,25},... | collective-permute-start | bytes 393224 | tf_op jit(solution)/shard_map/ppermute | solution.py:51
  13.6 8.6 %collective-permute-start.3 = (bf16[512,128]{1,0:T(8,128)(2,1)S(1)}, bf16[512,128]{1,0:T(8,128)(2,1)S(1)}, u32[]{:S(2)}, u32[]{:S(2)}) collective-permute-start(bf16[512,128]{1,0:T(8,128)(2,1)S(1)} %shard_map.107.refs_3_), channel_id=1, source_target_pairs={{0,2},{1,9},{2,0},{3,11},{4,6},{5,13},{6,4},{7,15},{8,10},{9,1},{1... | collective-permute-start | bytes 393224 | tf_op jit(solution)/shard_map/ppermute | solution.py:51
  19.5 4.5 %copy-start = (bf16[128,128]{1,0:T(8,128)(2,1)S(1)}, bf16[128,128]{1,0:T(8,128)(2,1)}, u32[]{:S(2)}) copy-start(bf16[128,128]{1,0:T(8,128)(2,1)} %weight_ref.3) | copy-start | bytes 98308
  22.2 1.3 %collective-permute-start.6 = (bf16[512,128]{1,0:T(8,128)(2,1)S(1)}, bf16[512,128]{1,0:T(8,128)(2,1)S(1)}, u32[]{:S(2)}, u32[]{:S(2)}) collective-permute-start(bf16[512,128]{1,0:T(8,128)(2,1)S(1)} %collective-permute-done.3.refs_4_), channel_id=1, source_target_pairs={{0,1},{1,0},{2,3},{3,2},{4,5},{5,4},{6,7},{7,6},{8,9},{9,8},{10,11... | collective-permute-start | bytes 393224 | tf_op jit(solution)/shard_map/ppermute | solution.py:25
  22.2 1.5 %collective-permute-start.7 = (bf16[512,128]{1,0:T(8,128)(2,1)S(1)}, bf16[512,128]{1,0:T(8,128)(2,1)S(1)}, u32[]{:S(2)}, u32[]{:S(2)}) collective-permute-start(bf16[512,128]{1,0:T(8,128)(2,1)S(1)} %collective-permute-done.4.refs_5_), channel_id=1, source_target_pairs={{0,1},{1,0},{2,3},{3,2},{4,5},{5,4},{6,7},{7,6},{8,9},{9,8},{10,11... | collective-permute-start | bytes 393224 | tf_op jit(solution)/shard_map/ppermute | solution.py:25
  22.7 1.3 %collective-permute-start.8 = (bf16[512,128]{1,0:T(8,128)(2,1)S(1)}, bf16[512,128]{1,0:T(8,128)(2,1)S(1)}, u32[]{:S(2)}, u32[]{:S(2)}) collective-permute-start(bf16[512,128]{1,0:T(8,128)(2,1)S(1)} %collective-permute-done.5.refs_6_), channel_id=1, source_target_pairs={{0,1},{1,0},{2,3},{3,2},{4,5},{5,4},{6,7},{7,6},{8,9},{9,8},{10,11... | collective-permute-start | bytes 393224 | tf_op jit(solution)/shard_map/ppermute | solution.py:25
  28.2 2.0 %collective-permute-start.10 = (bf16[1168,128]{1,0:T(8,128)(2,1)S(1)}, bf16[1168,128]{1,0:T(8,128)(2,1)S(1)}, u32[]{:S(2)}, u32[]{:S(2)}) collective-permute-start(bf16[1168,128]{1,0:T(8,128)(2,1)S(1)} %get-tuple-element.49), channel_id=1, source_target_pairs={{0,1},{1,0},{2,3},{3,2},{4,5},{5,4},{6,7},{7,6},{8,9},{9,8},{10,11... | collective-permute-start | bytes 897032 | tf_op jit(solution)/shard_map/ppermute | solution.py:25
  28.5 1.7 %collective-permute-start.9 = (bf16[1024,128]{1,0:T(8,128)(2,1)S(1)}, bf16[1024,128]{1,0:T(8,128)(2,1)S(1)}, u32[]{:S(2)}, u32[]{:S(2)}) collective-permute-start(bf16[1024,128]{1,0:T(8,128)(2,1)S(1)} %get-tuple-element.48), channel_id=1, source_target_pairs={{0,1},{1,0},{2,3},{3,2},{4,5},{5,4},{6,7},{7,6},{8,9},{9,8},{10,11... | collective-permute-start | bytes 786440 | tf_op jit(solution)/shard_map/ppermute | solution.py:25
  30.4 6.7 %collective-permute-start.11 = (bf16[592,128]{1,0:T(8,128)(2,1)S(1)}, bf16[592,128]{1,0:T(8,128)(2,1)S(1)}, u32[]{:S(2)}, u32[]{:S(2)}) collective-permute-start(bf16[592,128]{1,0:T(8,128)(2,1)S(1)} %get-tuple-element.51), channel_id=1, source_target_pairs={{0,2},{1,9},{2,0},{3,11},{4,6},{5,13},{6,4},{7,15},{8,10},{9,1},{1... | collective-permute-start | bytes 454664 | tf_op jit(solution)/shard_map/ppermute | solution.py:51
  30.5 9.4 %collective-permute-start.12 = (bf16[592,128]{1,0:T(8,128)(2,1)S(1)}, bf16[592,128]{1,0:T(8,128)(2,1)S(1)}, u32[]{:S(2)}, u32[]{:S(2)}) collective-permute-start(bf16[592,128]{1,0:T(8,128)(2,1)S(1)} %get-tuple-element.52), channel_id=1, source_target_pairs={{0,4},{1,17},{2,6},{3,19},{4,0},{5,21},{6,2},{7,23},{8,12},{9,25},... | collective-permute-start | bytes 454664 | tf_op jit(solution)/shard_map/ppermute | solution.py:51
  32.0 7.9 %collective-permute-start.13 = (bf16[592,128]{1,0:T(8,128)(2,1)S(1)}, bf16[592,128]{1,0:T(8,128)(2,1)S(1)}, u32[]{:S(2)}, u32[]{:S(2)}) collective-permute-start(bf16[592,128]{1,0:T(8,128)(2,1)S(1)} %get-tuple-element.53), channel_id=1, source_target_pairs={{0,6},{1,25},{2,4},{3,27},{4,2},{5,29},{6,0},{7,31},{8,14},{9,17},... | collective-permute-start | bytes 454664 | tf_op jit(solution)/shard_map/ppermute | solution.py:51
  40.0 7.3 %collective-permute-start.14 = (f32[592,128]{1,0:T(8,128)S(1)}, f32[592,128]{1,0:T(8,128)S(1)}, u32[]{:S(2)}, u32[]{:S(2)}) collective-permute-start(f32[592,128]{1,0:T(8,128)S(1)} %get-tuple-element.54.mine_ref), channel_id=1, source_target_pairs={{0,1},{1,0},{2,3},{3,2},{4,5},{5,4},{6,7},{7,6},{8,9},{9,8},{10,11... | collective-permute-start | bytes 909320 | tf_op jit(solution)/shard_map/ppermute | solution.py:25
  40.1 4.8 %collective-permute-start.17 = (bf16[96,128]{1,0:T(8,128)(2,1)S(1)}, bf16[96,128]{1,0:T(8,128)(2,1)S(1)}, u32[]{:S(2)}, u32[]{:S(2)}) collective-permute-start(bf16[96,128]{1,0:T(8,128)(2,1)S(1)} %get-tuple-element.55.refs_0_), channel_id=1, source_target_pairs={{0,24},{1,7},{2,26},{3,5},{4,28},{5,3},{6,30},{7,1},{8,16},{9,15},... | collective-permute-start | bytes 73736 | tf_op jit(solution)/shard_map/ppermute | solution.py:51
  42.6 3.8 %collective-permute-start.16 = (bf16[96,128]{1,0:T(8,128)(2,1)S(1)}, bf16[96,128]{1,0:T(8,128)(2,1)S(1)}, u32[]{:S(2)}, u32[]{:S(2)}) collective-permute-start(bf16[96,128]{1,0:T(8,128)(2,1)S(1)} %get-tuple-element.55.refs_0_), channel_id=1, source_target_pairs={{0,16},{1,5},{2,18},{3,7},{4,20},{5,1},{6,22},{7,3},{8,24},{9,13},... | collective-permute-start | bytes 73736 | tf_op jit(solution)/shard_map/ppermute | solution.py:51
  43.4 3.8 %collective-permute-start.15 = (bf16[96,128]{1,0:T(8,128)(2,1)S(1)}, bf16[96,128]{1,0:T(8,128)(2,1)S(1)}, u32[]{:S(2)}, u32[]{:S(2)}) collective-permute-start(bf16[96,128]{1,0:T(8,128)(2,1)S(1)} %get-tuple-element.55.refs_0_), channel_id=1, source_target_pairs={{0,8},{1,3},{2,10},{3,1},{4,12},{5,7},{6,14},{7,5},{8,0},{9,11},{1... | collective-permute-start | bytes 73736 | tf_op jit(solution)/shard_map/ppermute | solution.py:51
  47.2 1.3 %collective-permute-start.18 = (f32[80,128]{1,0:T(8,128)S(1)}, f32[80,128]{1,0:T(8,128)S(1)}, u32[]{:S(2)}, u32[]{:S(2)}) collective-permute-start(f32[80,128]{1,0:T(8,128)S(1)} %shard_map.115.last_ref), channel_id=1, source_target_pairs={{0,1},{1,0},{2,3},{3,2},{4,5},{5,4},{6,7},{7,6},{8,9},{9,8},{10,11... | collective-permute-start | bytes 122888 | tf_op jit(solution)/shard_map/ppermute | solution.py:25
